TPU v7x, 32 devices: a whole 2x2x4 slice. The times are simulated.
32 devices in a mesh: dp: 8 (over z, x), seq: 4 (over y, core).
Axes of the slice: x: 2, y: 2, z: 4, core: 2. Of those that a mesh axis runs over, the one named last changes fastest.
Arguments:
- frames: float32 [8192, 1024], P(('dp', 'seq')), may hold values from -6 to 6
- time_embed: float32 [8, 1024], P('dp'), may hold values from -6 to 6
- clip_len: int32 [8, 6], P('dp'), may hold values from 1 to 512, 1024 in all within a row
- w_qkv: bfloat16 [1024, 3072], P('dp'), may hold values from -0.1875 to 0.1875
- b_qkv: bfloat16 [3072], P('dp'), may hold values from -1.75 to 1.75
- w_out: bfloat16 [1024, 1024], P('dp'), may hold values from -1.5 to 1.5
- b_out: bfloat16 [1024], P('dp'), may hold values from -1.75 to 1.75
- w_up: bfloat16 [1024, 2048], P('dp'), may hold values from -0.1875 to 0.1875
- b_up: bfloat16 [2048], P('dp'), may hold values from -1.75 to 1.75
- w_down: bfloat16 [2048, 1024], P('dp'), may hold values from -0.25 to 0.25
- b_down: bfloat16 [1024], P('dp'), may hold values from -1.75 to 1.75
- w_mod: bfloat16 [1024, 6144], P('dp'), may hold values from -0.1875 to 0.1875
- b_mod: bfloat16 [6144], P('dp'), may hold values from -2.5 to 2.5
- cotangent: float32 [8192, 1024], P(('dp', 'seq')), may hold values from -6 to 6
Outputs:
- block_out: float32 [8192, 1024], P(('dp', 'seq'))
- grad_input: float32 [8192, 1024], P(('dp', 'seq'))
- grad_time: float32 [8, 1024], P('dp')
- grad_w_qkv: float32 [1024, 3072], P('dp')
- grad_b_qkv: float32 [3072], P('dp')
- grad_w_out: float32 [1024, 1024], P('dp')
- grad_b_out: float32 [1024], P('dp')
- grad_w_up: float32 [1024, 2048], P('dp')
- grad_b_up: float32 [2048], P('dp')
- grad_w_down: float32 [2048, 1024], P('dp')
- grad_b_down: float32 [1024], P('dp')
- grad_w_mod: float32 [1024, 6144], P('dp')
- grad_b_mod: float32 [6144], P('dp')
Inputs may be any that keep to these rules, and one draw needn't show every extreme that they name: `clip_len`: each row sums to 1024; each row's longest clip has exactly 512 frames.
All inputs are finite; a program needn't handle non-finite values.
Results may differ from a plain program's by a relative error of at most 0.015.
The roundings to bfloat16 on the way count: a program that leaves them out, or rounds other values in their place, can miss the bound.
Values may be sent and summed in bfloat16 or wider, within the bound.
A program may use at most 192 MiB of HBM per device.

v0:
```python
import math

import jax
import jax.numpy as jnp
from jax import lax
from jax.sharding import PartitionSpec as P

HEADS = 16


norm_eps = 1e-06


def as_sent(value):

    def short(part):
        return part.astype(jnp.bfloat16) if part.dtype == jnp.float32 else part

    return jax.tree.map(short, value)


def layer_norm(values):
    mean_val = jnp.mean(values, axis=-1, keepdims=True)
    centred = values - mean_val
    variance = jnp.mean(centred * centred, axis=-1, keepdims=True)
    return centred * lax.rsqrt(variance + norm_eps)


def modulate(values, shift_term, scale_term):
    return layer_norm(values) * (1.0 + scale_term) + shift_term


def rotate(values, cosine_tab, sine_tab):
    half_dim = values.shape[-1] // 2
    lower_half = values[..., :half_dim]
    upper_half = values[..., half_dim:]
    return jnp.concatenate(
        [
            lower_half * cosine_tab - upper_half * sine_tab,
            upper_half * cosine_tab + lower_half * sine_tab,
        ],
        axis=-1,
    )


def angles(positions, head_dim):
    half_dim = head_dim // 2
    inv_rate = jnp.exp(
        jnp.arange(half_dim, dtype=jnp.float32) * (-2.0 * math.log(10000.0) / head_dim)
    )
    phases = positions.astype(jnp.float32)[:, None] * inv_rate[None, :]
    return (jnp.cos(phases)[:, None, :], jnp.sin(phases)[:, None, :])


def across_rows(left_side, right_side):
    return lax.dot_general(
        left_side, right_side, (((0,), (0,)), ((), ())), preferred_element_type=jnp.float32
    )


def against(left_side, right_side):
    return lax.dot_general(
        left_side, right_side, (((1,), (1,)), ((), ())), preferred_element_type=jnp.float32
    )


def forward_dot(left_side, right_side):
    return jnp.dot(left_side, right_side, preferred_element_type=jnp.float32)


def column_sums(values):
    return jnp.sum(values.astype(jnp.float32), axis=0)


def per_device(
    frames,
    time_embed,
    clip_len,
    w_qkv,
    b_qkv,
    w_out,
    b_out,
    w_up,
    b_up,
    w_down,
    b_down,
    w_mod,
    b_mod,
    cotangent,
):
    seq_count = lax.axis_size("seq")
    seq_rank = lax.axis_index("seq")
    frame_rows = frames.shape[0]
    model_width = frames.shape[1]
    length = frame_rows * seq_count
    heads_here = HEADS // seq_count
    head_dim = model_width // HEADS
    local_width = heads_here * head_dim
    factor = head_dim ** (-0.5)
    block_rows = min(512, length)
    block_count = length // block_rows
    shards = (w_qkv, b_qkv, w_out, b_out, w_up, b_up, w_down, b_down, w_mod, b_mod)
    gathered = (
        lax.all_gather(shards[0], "dp", axis=0, tiled=True),
        lax.all_gather(shards[1], "dp", axis=0, tiled=True),
        lax.all_gather(shards[2], "dp", axis=0, tiled=True),
        lax.all_gather(shards[3], "dp", axis=0, tiled=True),
        lax.all_gather(shards[4], "dp", axis=0, tiled=True),
        lax.all_gather(shards[5], "dp", axis=0, tiled=True),
        lax.all_gather(shards[6], "dp", axis=0, tiled=True),
        lax.all_gather(shards[7], "dp", axis=0, tiled=True),
        lax.all_gather(shards[8], "dp", axis=0, tiled=True),
        lax.all_gather(shards[9], "dp", axis=0, tiled=True),
    )
    wq_full, bq_full, wo_full, bo_full, wu_full, bu_full, wd_full, bd_full, wm_full, bm_full = (
        gathered
    )
    lengths = clip_len[0]
    clip_end = jnp.cumsum(lengths)
    clip_start = clip_end - lengths
    item_frames = jnp.arange(length, dtype=jnp.int32)
    inside = (item_frames[:, None] >= clip_start[None, :]) & (
        item_frames[:, None] < clip_end[None, :]
    )
    clip_ids = jnp.sum(
        jnp.where(inside, jnp.arange(lengths.shape[0], dtype=jnp.int32)[None, :], 0), axis=1
    )
    positions = item_frames - jnp.sum(jnp.where(inside, clip_start[None, :], 0), axis=1)
    own_positions = lax.dynamic_slice_in_dim(positions, seq_rank * frame_rows, frame_rows, 0)
    cosine_tab, sine_tab = angles(own_positions, head_dim)
    time_act = jax.nn.silu(time_embed).astype(jnp.bfloat16)
    modulation = forward_dot(time_act, wm_full) + bm_full.astype(jnp.float32)
    shift_a, scale_a, gate_a, shift_f, scale_f, gate_f = jnp.split(modulation, 6, axis=1)
    x_a = modulate(frames, shift_a, scale_a).astype(jnp.bfloat16)
    projected = forward_dot(x_a, wq_full) + bq_full.astype(jnp.float32)
    pieces = projected.reshape(frame_rows, 3, HEADS, head_dim)
    query = rotate(pieces[:, 0], cosine_tab, sine_tab).astype(jnp.bfloat16)
    keys_own = rotate(pieces[:, 1], cosine_tab, sine_tab).astype(jnp.bfloat16)
    values_own = pieces[:, 2].astype(jnp.bfloat16)
    packed = jnp.stack([query, keys_own, values_own], axis=1).reshape(frame_rows, 3, model_width)
    heads_in = lax.all_to_all(packed, "seq", split_axis=2, concat_axis=0, tiled=True)
    query_heads = heads_in[:, 0].reshape(length, heads_here, head_dim)
    keys_heads = heads_in[:, 1].reshape(length, heads_here, head_dim)
    values_heads = heads_in[:, 2].reshape(length, heads_here, head_dim)

    def block_scores(block_index):
        first_row = block_index * block_rows
        query_blk = lax.dynamic_slice_in_dim(query_heads, first_row, block_rows, 0)
        clip_blk = lax.dynamic_slice_in_dim(clip_ids, first_row, block_rows, 0)
        same_clip = (clip_blk[:, None] == clip_ids[None, :])[None]
        raw_scores = (
            jnp.einsum("qhe,khe->hqk", query_blk, keys_heads, preferred_element_type=jnp.float32)
            * factor
        )
        return (query_blk, same_clip, jnp.where(same_clip, raw_scores, -1e30))

    def attend(block_index):
        query_blk, same_clip, masked = block_scores(block_index)
        row_max = jnp.max(masked, axis=-1, keepdims=True)
        exp_scores = jnp.exp(masked - row_max)
        row_sum = jnp.sum(exp_scores, axis=-1, keepdims=True)
        attn_prob = (exp_scores / row_sum).astype(jnp.bfloat16)
        mixed_rows = jnp.einsum(
            "hqk,khe->qhe", attn_prob, values_heads, preferred_element_type=jnp.float32
        )
        return (mixed_rows.astype(jnp.bfloat16), row_max + jnp.log(row_sum))

    attn_blocks, log_totals = lax.map(attend, jnp.arange(block_count))
    attn_heads = attn_blocks.reshape(length, local_width)
    attn_out = lax.all_to_all(attn_heads, "seq", split_axis=0, concat_axis=1, tiled=True)
    attn_branch = forward_dot(attn_out, wo_full) + bo_full.astype(jnp.float32)
    x_mid = frames + gate_a * attn_branch
    x_f = modulate(x_mid, shift_f, scale_f).astype(jnp.bfloat16)
    hidden = forward_dot(x_f, wu_full) + bu_full.astype(jnp.float32)
    gelu_act = jax.nn.gelu(hidden, approximate=True).astype(jnp.bfloat16)
    ffn_branch = forward_dot(gelu_act, wd_full) + bd_full.astype(jnp.float32)
    block_out = x_mid + gate_f * ffn_branch
    wq_back, bq_back, wo_back, bo_back, wu_back, bu_back, wd_back, bd_back, wm_back, bm_back = (
        gathered
    )
    d_ffn = (gate_f * cotangent).astype(jnp.bfloat16)
    d_gate_f = jnp.sum(cotangent * ffn_branch, axis=0, keepdims=True)
    g_wd = across_rows(gelu_act, d_ffn)
    g_bd = column_sums(d_ffn)
    d_gelu = against(d_ffn, wd_back)
    gelu_pull = jax.vjp(lambda inner: jax.nn.gelu(inner, approximate=True), hidden)[1]
    d_hidden = gelu_pull(d_gelu)[0].astype(jnp.bfloat16)
    g_wu = across_rows(x_f, d_hidden)
    g_bu = column_sums(d_hidden)
    d_xf = against(d_hidden, wu_back)
    mid_pull = jax.vjp(modulate, x_mid, shift_f, scale_f)[1]
    d_mid_part, d_shift_f, d_scale_f = mid_pull(d_xf)
    d_mid = cotangent + d_mid_part
    d_attn = (gate_a * d_mid).astype(jnp.bfloat16)
    d_gate_a = jnp.sum(d_mid * attn_branch, axis=0, keepdims=True)
    g_wo = across_rows(attn_out, d_attn)
    g_bo = column_sums(d_attn)
    d_out = against(d_attn, wo_back).astype(jnp.bfloat16)
    grad_heads = lax.all_to_all(d_out, "seq", split_axis=1, concat_axis=0, tiled=True).reshape(
        length, heads_here, head_dim
    )

    def attend_back(running, inputs):
        grad_keys, grad_values = running
        block_index, log_blk = inputs
        query_blk, same_clip, masked = block_scores(block_index)
        attn_prob = jnp.exp(masked - log_blk)
        prob_low = attn_prob.astype(jnp.bfloat16)
        grad_blk = lax.dynamic_slice_in_dim(grad_heads, block_index * block_rows, block_rows, 0)
        d_prob = jnp.einsum(
            "qhe,khe->hqk", grad_blk, values_heads, preferred_element_type=jnp.float32
        )
        d_scores = attn_prob * (d_prob - jnp.sum(d_prob * attn_prob, axis=-1, keepdims=True))
        d_scores = jnp.where(same_clip, d_scores, 0.0).astype(jnp.bfloat16)
        d_query = (
            jnp.einsum("hqk,khe->qhe", d_scores, keys_heads, preferred_element_type=jnp.float32)
            * factor
        )
        grad_keys = (
            grad_keys
            + jnp.einsum("hqk,qhe->khe", d_scores, query_blk, preferred_element_type=jnp.float32)
            * factor
        )
        grad_values = grad_values + jnp.einsum(
            "hqk,qhe->khe", prob_low, grad_blk, preferred_element_type=jnp.float32
        )
        return ((grad_keys, grad_values), d_query.astype(jnp.bfloat16))

    zero_heads = jnp.zeros((length, heads_here, head_dim), jnp.float32)
    (grad_keys, grad_values), query_grads = lax.scan(
        attend_back, (zero_heads, zero_heads), (jnp.arange(block_count), log_totals)
    )
    grads_stacked = jnp.stack(
        [
            query_grads.reshape(length, heads_here, head_dim),
            grad_keys.astype(jnp.bfloat16),
            grad_values.astype(jnp.bfloat16),
        ],
        axis=1,
    )
    grads_frames = lax.all_to_all(
        grads_stacked.reshape(length, 3, local_width),
        "seq",
        split_axis=0,
        concat_axis=2,
        tiled=True,
    )
    grad_query = rotate(
        grads_frames[:, 0].reshape(frame_rows, HEADS, head_dim).astype(jnp.float32),
        cosine_tab,
        -sine_tab,
    )
    grad_key = rotate(
        grads_frames[:, 1].reshape(frame_rows, HEADS, head_dim).astype(jnp.float32),
        cosine_tab,
        -sine_tab,
    )
    grad_value = grads_frames[:, 2].astype(jnp.float32)
    d_projected = jnp.concatenate(
        [
            grad_query.reshape(frame_rows, model_width),
            grad_key.reshape(frame_rows, model_width),
            grad_value,
        ],
        axis=1,
    ).astype(jnp.bfloat16)
    g_wq = across_rows(x_a, d_projected)
    g_bq = column_sums(d_projected)
    d_xa = against(d_projected, wq_back)
    input_pull = jax.vjp(modulate, frames, shift_a, scale_a)[1]
    d_input_part, d_shift_a, d_scale_a = input_pull(d_xa)
    grad_input = d_mid + d_input_part
    mod_part = jnp.concatenate(
        [d_shift_a, d_scale_a, d_gate_a, d_shift_f, d_scale_f, d_gate_f], axis=1
    )
    d_mod = lax.psum(mod_part, "seq").astype(jnp.bfloat16)
    d_time_act = against(d_mod, wm_back)
    silu_pull = jax.vjp(jax.nn.silu, time_embed)[1]
    grad_time = silu_pull(d_time_act)[0]
    main_terms = (g_wq, g_bq, g_wo, g_bo, g_wu, g_bu, g_wd, g_bd)
    seq_share = 1.0 / seq_count
    g_wm = across_rows(time_act, d_mod) * seq_share
    g_bm = d_mod[0].astype(jnp.float32) * seq_share
    grad_terms = main_terms + (g_wm, g_bm)
    extra_terms = ()
    dp_sums = lax.psum_scatter(grad_terms, "dp", scatter_dimension=0, tiled=True)
    grad_sums = jax.tree.map(
        lambda part: part.astype(jnp.float32), lax.psum(as_sent(tuple(dp_sums)), "seq")
    )
    s_wq, s_bq, s_wo, s_bo, s_wu, s_bu, s_wd, s_bd, s_wm, s_bm = tuple(grad_sums) + extra_terms
    return (
        block_out,
        grad_input,
        grad_time,
        s_wq,
        s_bq,
        s_wo,
        s_bo,
        s_wu,
        s_bu,
        s_wd,
        s_bd,
        s_wm,
        s_bm,
    )


def solution(mesh):
    placed = (
        P(("dp", "seq"), None),
        P("dp", None),
        P("dp", None),
        P("dp", None),
        P("dp"),
        P("dp", None),
        P("dp"),
        P("dp", None),
        P("dp"),
        P("dp", None),
        P("dp"),
        P("dp", None),
        P("dp"),
        P(("dp", "seq"), None),
    )
    return jax.shard_map(
        per_device,
        mesh=mesh,
        in_specs=placed,
        out_specs=(
            P(("dp", "seq"), None),
            P(("dp", "seq"), None),
            P("dp", None),
            P("dp", None),
            P("dp"),
            P("dp", None),
            P("dp"),
            P("dp", None),
            P("dp"),
            P("dp", None),
            P("dp"),
            P("dp", None),
            P("dp"),
        ),
        check_vma=False,
    )
```

profile of v0, /device:TPU:0, one launch (start us, length us, event | category | flops | bytes accessed | tf_op | source)
XLA Modules:
  0.0 1608.1 jit_solution(8863701262765900073)
XLA Ops:
  10.1 32.3 %all-gather = bf16[8,1,768]{2,1,0:T(2,128)(2,1)S(1)} all-gather(bf16[1,1,768]{2,1,0:T(2,128)(2,1)S(1)} %reshape.349), channel_id=1, replica_groups=mesh['dp'=8,'seq'=4] {'dp'}, dimensions={0}, use_global_device_ids=true | all-gather | bytes 13824 | tf_op jit(solution)/shard_map/all_gather | solution.py:113
  42.5 26.3 %all-gather.1 = bf16[8,1,384]{2,1,0:T(2,128)(2,1)S(1)} all-gather(bf16[1,1,384]{2,1,0:T(2,128)(2,1)S(1)} %reshape.351), channel_id=1, replica_groups=mesh['dp'=8,'seq'=4] {'dp'}, dimensions={0}, use_global_device_ids=true | all-gather | bytes 6912 | tf_op jit(solution)/shard_map/all_gather | solution.py:105
  70.4 119.1 %all-gather.11.cloned.1.call-done = bf16[1024,6144]{1,0:T(8,128)(2,1)} async-done(((bf16[128,6144]{1,0:T(8,128)(2,1)}), bf16[1024,6144]{1,0:T(8,128)(2,1)}) %all-gather.11.cloned.1.call-update) | async-done | bytes 12582928 | tf_op jit(solution)/shard_map/all_gather | solution.py:112
  189.5 6.3 fusion.110
  195.9 93.1 %all-gather.13.cloned.1.call-done = bf16[1024,3072]{1,0:T(8,128)(2,1)} async-done(((bf16[128,3072]{1,0:T(8,128)(2,1)}), bf16[1024,3072]{1,0:T(8,128)(2,1)}) %all-gather.13.cloned.1.call-update) | async-done | bytes 6291472 | tf_op jit(solution)/shard_map/all_gather | solution.py:104
  288.9 6.3 convolution_add_fusion
  295.3 3.6 copy.86
  302.6 2.7 copy.87
  305.2 3.6 all-to-all-start
  309.5 25.1 %all-to-all-done = bf16[256,3,1024]{0,1,2:T(4,128)(2,1)S(1)} async-done(((bf16[256,3,1024]{0,1,2:T(4,128)(2,1)}), bf16[256,3,1024]{0,1,2:T(4,128)(2,1)S(1)}, u32[]{:S(2)}, u32[]{:S(2)}) %all-to-all-start) | async-done | bytes 1572896 | tf_op jit(solution)/shard_map/all_to_all | solution.py:141
  341.4 17.6 %while.27 = (s32[]{:T(128)}, bf16[2,512,4,64]{1,3,2,0:T(8,128)(2,1)S(1)}, f32[2,4,512,1]{2,1,3,0:T(4,128)S(1)}, s32[2]{0:T(128)S(1)}, s32[1024]{0:T(1024)S(1)}, ...) while((s32[]{:T(128)}, ...), condition=%wide.region_8.9_spmd, body=%wide.region_5.8_spmd.sunk | while | flops 562690048 | bytes 28911808 | solution.py:168
  344.8 2.3 fusion.177
  347.2 3.0 fusion.178
  353.6 2.3 fusion.177
  356.0 3.0 fusion.178
  360.4 2.1 all_to_all.56
  363.4 3.5 all-to-all-start.1
  366.9 17.8 %all-gather.2 = bf16[8,1,128]{2,1,0:T(2,128)(2,1)S(1)} all-gather(bf16[1,1,128]{2,1,0:T(2,128)(2,1)S(1)} %bitcast.220), channel_id=1, replica_groups=mesh['dp'=8,'seq'=4] {'dp'}, dimensions={0}, use_global_device_ids=true | all-gather | bytes 2304 | tf_op jit(solution)/shard_map/all_gather | solution.py:107
  384.8 17.1 %all-gather.3 = bf16[8,1,256]{2,1,0:T(2,128)(2,1)S(1)} all-gather(bf16[1,1,256]{2,1,0:T(2,128)(2,1)S(1)} %reshape.355), channel_id=1, replica_groups=mesh['dp'=8,'seq'=4] {'dp'}, dimensions={0}, use_global_device_ids=true | all-gather | bytes 4608 | tf_op jit(solution)/shard_map/all_gather | solution.py:109
  401.9 17.8 %all-gather.4 = bf16[8,1,128]{2,1,0:T(2,128)(2,1)S(1)} all-gather(bf16[1,1,128]{2,1,0:T(2,128)(2,1)S(1)} %bitcast.221), channel_id=1, replica_groups=mesh['dp'=8,'seq'=4] {'dp'}, dimensions={0}, use_global_device_ids=true | all-gather | bytes 2304 | tf_op jit(solution)/shard_map/all_gather | solution.py:111
  420.5 3.6 fusion.126
  424.4 4.9 convolution_add_fusion.1
  429.3 57.1 %all-gather.19.cloned.1.call-done = bf16[2048,1024]{1,0:T(8,128)(2,1)} async-done(((bf16[256,1024]{1,0:T(8,128)(2,1)}), bf16[2048,1024]{1,0:T(8,128)(2,1)}) %all-gather.19.cloned.1.call-update) | async-done | bytes 4194320 | tf_op jit(solution)/shard_map/all_gather | solution.py:110
  486.4 6.4 multiply_reduce_fusion.1
  492.8 3.0 convert_reduce_fusion.1
  495.8 2.1 multiply_reduce_fusion.2
  501.7 2.7 fusion.130
  504.5 5.9 fusion.121
  511.4 6.3 fusion.122
  518.8 2.3 convolution_convert_fusion
  521.9 3.9 all-to-all-start.2
  525.9 8.7 all-to-all-done.2
  535.7 2.2 reshape.339
  538.7 119.2 %while.28 = (s32[]{:T(128)}, f32[1024,4,64]{0,2,1:T(8,128)}, f32[1024,4,64]{0,2,1:T(8,128)}, bf16[2,512,4,64]{1,3,2,0:T(8,128)(2,1)}, s32[2]{0:T(128)S(1)}, /*in...) while((s32[]{:T(128)}, f32[1024,4,64]{0,2,1:T(8,128)}, ...), condition=%wide.region_15.16_spmd.clone, body=%wide.region_13.15_spmd.clone.sunk | while | flops 1398806528 | bytes 104663816 | solution.py:230
  540.0 4.5 fusion.190
  544.9 4.5 fusion.189
  549.5 23.5 %fusion.191 = f32[1024,4,64]{0,2,1:T(8,128)} fusion(f32[4,512,1024]{2,1,0:T(8,128)} %fusion.189, f32[4,512,1024]{2,1,0:T(8,128)} %fusion.190, f32[4,512]{1,0:T(4,128)S(1)} %dynamic-slice_bitcast_fusion.2, pred[512,1024]{1,0:T(8,128)(4,1)S(1)} %broadcast_compare_fusion.5, f32[1024,4,64]{0,2,1:T(8,128)} %get-tuple-element.474, pred[]{:T(512)S(6)} %compare.3, ...), kind=kOutput, calls=%fused_computation.39.clone.1 | convolution fusion | flops 292293632 | bytes 36978692 | tf_op jit(solution)/shard_map/while/body/eval_jaxpr/hqk,qhe->khe/dot_general | solution.py:221
  572.9 18.0 %fusion.193 = bf16[2,512,4,64]{1,3,2,0:T(8,128)(2,1)} fusion(bf16[2,512,4,64]{1,3,2,0:T(8,128)(2,1)} %get-tuple-element.476, s32[]{:T(128)} %get-tuple-element.473, bf16[1024,4,64]{0,2,1:T(8,128)(2,1)S(1)} %get-tuple-element.495, f32[4,512,1024]{2,1,0:T(8,128)} %fusion.189, f32[4,512,1024]{2,1,0:T(8,128)} %fusion.190, ...), kind=kOutput, calls=%fused_computation.44.clone.1 | convolution fusion | flops 291769344 | bytes 35406336 | tf_op jit(solution)/shard_map/while/body/eval_jaxpr/hqk,khe->qhe/dot_general | solution.py:216
  590.9 6.8 fusion.192
  599.0 4.8 fusion.190
  604.2 4.5 fusion.189
  608.8 23.6 %fusion.191 = f32[1024,4,64]{0,2,1:T(8,128)} fusion(f32[4,512,1024]{2,1,0:T(8,128)} %fusion.189, f32[4,512,1024]{2,1,0:T(8,128)} %fusion.190, f32[4,512]{1,0:T(4,128)S(1)} %dynamic-slice_bitcast_fusion.2, pred[512,1024]{1,0:T(8,128)(4,1)S(1)} %broadcast_compare_fusion.5, f32[1024,4,64]{0,2,1:T(8,128)} %get-tuple-element.474, pred[]{:T(512)S(6)} %compare.3, ...), kind=kOutput, calls=%fused_computation.39.clone.1 | convolution fusion | flops 292293632 | bytes 36978692 | tf_op jit(solution)/shard_map/while/body/eval_jaxpr/hqk,qhe->khe/dot_general | solution.py:221
  632.4 18.3 %fusion.193 = bf16[2,512,4,64]{1,3,2,0:T(8,128)(2,1)} fusion(bf16[2,512,4,64]{1,3,2,0:T(8,128)(2,1)} %get-tuple-element.476, s32[]{:T(128)} %get-tuple-element.473, bf16[1024,4,64]{0,2,1:T(8,128)(2,1)S(1)} %get-tuple-element.495, f32[4,512,1024]{2,1,0:T(8,128)} %fusion.189, f32[4,512,1024]{2,1,0:T(8,128)} %fusion.190, ...), kind=kOutput, calls=%fused_computation.44.clone.1 | convolution fusion | flops 291769344 | bytes 35406336 | tf_op jit(solution)/shard_map/while/body/eval_jaxpr/hqk,khe->qhe/dot_general | solution.py:216
  650.7 7.1 fusion.192
  662.7 2.9 copy.98
  665.7 28.9 %all_to_all.71 = bf16[1024,3,256]{2,1,0:T(4,128)(2,1)} all-to-all(bf16[1024,3,256]{2,1,0:T(4,128)(2,1)S(1)} %copy.98), channel_id=1, replica_groups=mesh['dp'=8,'seq'=4] {'seq'}, dimensions={0} | all-to-all | bytes 3145728 | tf_op jit(solution)/shard_map/all_to_all | solution.py:241
  694.6 2.9 copy.99
  698.8 6.6 fusion.119
  706.2 4.9 multiply_reduce_fusion.4
  713.8 13.6 psum.77
  727.6 11.9 multiply_multiply_fusion
  741.4 2.3 reduce-scatter.10.cloned.1.call-done
  743.7 2.1 convert_element_type.222
  745.8 149.6 %reduce-scatter.12.cloned.1.call-done = f32[256,1024]{1,0:T(8,128)} async-done(((f32[2048,1024]{1,0:T(8,128)}), f32[256,1024]{1,0:T(8,128)}) %reduce-scatter.12.cloned.1.call-update) | async-done | bytes 1048592 | tf_op jit(solution)/shard_map/reduce_scatter | solution.py:286
  895.3 2.1 convert_element_type.227
  897.4 208.3 %reduce-scatter.6.cloned.1.call-done = f32[128,3072]{1,0:T(8,128)} async-done(((f32[1024,3072]{1,0:T(8,128)}), f32[128,3072]{1,0:T(8,128)}) %reduce-scatter.6.cloned.1.call-update) | async-done | bytes 1572880 | tf_op jit(solution)/shard_map/reduce_scatter | solution.py:286
  1105.7 2.4 convert_element_type.212
  1108.1 404.5 %reduce-scatter.14.cloned.1.call-done = f32[128,6144]{1,0:T(8,128)} async-done(((f32[1024,6144]{1,0:T(8,128)}), f32[128,6144]{1,0:T(8,128)}) %reduce-scatter.14.cloned.1.call-update) | async-done | bytes 3145744 | tf_op jit(solution)/shard_map/reduce_scatter | solution.py:286
  1512.6 3.2 convert_element_type.232
  1519.5 35.7 %all-reduce.5 = (bf16[3072]{0:T(1024)(128)(2,1)S(1)}, bf16[1024]{0:T(1024)(128)(2,1)S(1)}, bf16[2048]{0:T(1024)(128)(2,1)S(1)}, bf16[1024]{0:T(1024)(128)(2,1)S(1)}, bf16[6144]{0:T(1024)(128)(2,1)S(1)}) all-reduce(f32[3072]{0:T(1024)S(1)} %convert_reduce_fusion, ...), channel_id=3, replica_groups=mesh['dp'=8,'seq'=4] {'dp'}, use_global_device_ids=true, to_apply=%region_28.29.clone | all-reduce | flops 13312 | bytes 79872
  1555.6 5.9 all-reduce.6
  1564.3 8.6 fusion.109
  1573.0 20.6 %all-reduce.10.cloned.1.call-done = (bf16[128,3072]{1,0:T(8,128)(2,1)}, bf16[128,1024]{1,0:T(8,128)(2,1)}, bf16[128,2048]{1,0:T(8,128)(2,1)}, bf16[256,1024]{1,0:T(8,128)(2,1)}, bf16[128,6144]{1,0:T(8,128)(2,1)}) async-done(((bf16[128,3072]{1,0:T(8,128)(2,1)}, bf16[128,1024]{1,0:T(8,128)(2,1)}, bf16[128,2048]{1,0:T(8,128)(2,1)}, bf16[256,1024]{1,0:T(8,128)(2,1)}, bf16[128,6144]{1,0:T(8,128)(2,1)}), ...) | async-done | bytes 3670032 | tf_op jit(solution)/shard_map/psum | solution.py:288
  1593.5 3.5 convert_element_type.233
  (239 shorter events, 54.9 us)
Async XLA Ops:
  7.2 2.9 copy-start.41
  7.2 35.2 %copy-start.42 = (bf16[384]{0:T(512)(128)(2,1)S(1)}, bf16[384]{0:T(512)(128)(2,1)}, u32[]{:S(2)}) copy-start(bf16[384]{0:T(512)(128)(2,1)} %param.22) | copy-start | bytes 2308
  7.2 61.6 %copy-start.47 = (s32[1,6]{1,0:T(1,128)S(1)}, s32[1,6]{1,0:T(1,128)}, u32[]{:S(2)}) copy-start(s32[1,6]{1,0:T(1,128)} %param.20) | copy-start | bytes 76
  7.2 61.7 %copy-start = (f32[256,1024]{1,0:T(8,128)S(1)}, f32[256,1024]{1,0:T(8,128)}, u32[]{:S(2)}) copy-start(f32[256,1024]{1,0:T(8,128)} %param.18) | copy-start | bytes 3145732
  7.2 182.3 %copy-start.27 = (f32[1,1024]{1,0:T(1,128)S(1)}, f32[1,1024]{1,0:T(1,128)}, u32[]{:S(2)}) copy-start(f32[1,1024]{1,0:T(1,128)} %param.19) | copy-start | bytes 12292
  7.2 182.3 %all-gather.11.cloned.1.call-start = ((), (), s32[]{:S(2)}) async-start(), calls=%async_computation.9 | async-start | bytes 14155776 | tf_op jit(solution)/shard_map/all_gather | solution.py:112
  8.0 281.0 %all-gather.13.cloned.1.call-start = ((), (), s32[]{:S(2)}) async-start(), calls=%async_computation.10 | async-start | bytes 7077888 | tf_op jit(solution)/shard_map/all_gather | solution.py:104
  8.7 411.0 %all-gather.15.cloned.1.call-start = ((), (), s32[]{:S(2)}) async-start(), calls=%async_computation.11 | async-start | bytes 2359296 | tf_op jit(solution)/shard_map/all_gather | solution.py:106
  9.4 414.9 %all-gather.17.cloned.1.call-start = ((), (), s32[]{:S(2)}) async-start(), calls=%async_computation.12 | async-start | bytes 4718592 | tf_op jit(solution)/shard_map/all_gather | solution.py:108
  69.3 219.6 %copy-start.29 = (f32[256]{0:T(256)}, f32[256]{0:T(256)S(1)}, u32[]{:S(2)}) copy-start(f32[256]{0:T(256)S(1)} %broadcast_multiply_fusion.2) | copy-start | bytes 3076
  69.6 126.3 %copy-start.34 = (f32[256]{0:T(256)}, f32[256]{0:T(256)S(1)}, u32[]{:S(2)}) copy-start(f32[256]{0:T(256)S(1)} %multiply_reduce_fusion.8) | copy-start | bytes 3076
  69.6 219.4 %copy-start.31 = (f32[256]{0:T(256)}, f32[256]{0:T(256)S(1)}, u32[]{:S(2)}) copy-start(f32[256]{0:T(256)S(1)} %fusion.115) | copy-start | bytes 3076
  70.4 231.5 %copy-start.19 = (f32[256,32]{0,1:T(8,128)}, f32[256,32]{0,1:T(8,128)S(1)}, u32[]{:S(2)}) copy-start(f32[256,32]{0,1:T(8,128)S(1)} %get-tuple-element.296) | copy-start | bytes 98308
  195.9 99.4 %copy-start.21 = (f32[1,1024]{1,0:T(1,128)}, f32[1,1024]{1,0:T(1,128)S(1)}, u32[]{:S(2)}) copy-start(f32[1,1024]{1,0:T(1,128)S(1)} %get-tuple-element.292) | copy-start | bytes 12292
  195.9 99.4 %copy-start.24 = (f32[1,1024]{1,0:T(1,128)}, f32[1,1024]{1,0:T(1,128)S(1)}, u32[]{:S(2)}) copy-start(f32[1,1024]{1,0:T(1,128)S(1)} %get-tuple-element.291) | copy-start | bytes 12292
  305.2 29.3 %all-to-all-start = ((bf16[256,3,1024]{0,1,2:T(4,128)(2,1)}), bf16[256,3,1024]{0,1,2:T(4,128)(2,1)S(1)}, u32[]{:S(2)}, u32[]{:S(2)}) async-start(bf16[256,3,1024]{0,1,2:T(4,128)(2,1)} %copy.87), calls=%async_computation | async-start | bytes 4194304 | tf_op jit(solution)/shard_map/all_to_all | solution.py:141
  308.8 177.5 %all-gather.19.cloned.1.call-start = ((), (), s32[]{:S(2)}) async-start(), calls=%async_computation.13 | async-start | bytes 4718592 | tf_op jit(solution)/shard_map/all_gather | solution.py:110
  359.0 60.7 %copy-start.1 = (bf16[1024,4,64]{0,2,1:T(8,128)(2,1)}, bf16[1024,4,64]{0,2,1:T(8,128)(2,1)S(1)}, u32[]{:S(2)}) copy-start(bf16[1024,4,64]{0,2,1:T(8,128)(2,1)S(1)} %get-tuple-element.536) | copy-start | bytes 1572868
  359.0 7.9 copy-start.43
  359.0 25.7 %copy-start.48 = (bf16[256]{0:T(256)(128)(2,1)S(1)}, bf16[256]{0:T(256)(128)(2,1)}, u32[]{:S(2)}) copy-start(bf16[256]{0:T(256)(128)(2,1)} %param.26) | copy-start | bytes 1540
  359.1 42.9 %copy-start.44 = (bf16[128]{0:T(256)(128)(2,1)S(1)}, bf16[128]{0:T(256)(128)(2,1)}, u32[]{:S(2)}) copy-start(bf16[128]{0:T(256)(128)(2,1)} %param.28) | copy-start | bytes 772
  363.4 56.3 %all-to-all-start.1 = ((bf16[4,256,256]{1,2,0:T(8,128)(2,1)}), bf16[4,256,256]{1,2,0:T(8,128)(2,1)S(1)}, u32[]{:S(2)}, u32[]{:S(2)}) async-start(bf16[4,256,256]{1,2,0:T(8,128)(2,1)} %copy.94), calls=%async_computation.1 | async-start | bytes 1048576 | tf_op jit(solution)/shard_map/all_to_all | solution.py:170
  366.9 372.7 %reduce-scatter.8.cloned.1.call-start = ((), (), s32[]{:S(2)}) async-start(), calls=%async_computation.15 | async-start | bytes 4718592 | tf_op jit(solution)/shard_map/reduce_scatter | solution.py:286
  419.7 0.8 copy-start.3
  486.4 6.4 copy-start.8
  486.4 6.4 copy-start.46
  492.8 3.0 copy-start.17
  492.8 3.0 copy-start.45
  495.8 2.1 copy-start.11
  497.9 1.2 copy-start.13
  497.9 3.8 copy-start.4
  500.9 0.8 copy-start.9
  504.4 239.3 %reduce-scatter.10.cloned.1.call-start = ((), (), s32[]{:S(2)}) async-start(), calls=%async_computation.16 | async-start | bytes 9437184 | tf_op jit(solution)/shard_map/reduce_scatter | solution.py:286
  510.3 1.0 copy-start.18
  510.4 385.0 %reduce-scatter.12.cloned.1.call-start = ((), (), s32[]{:S(2)}) async-start(), calls=%async_computation.17 | async-start | bytes 9437184 | tf_op jit(solution)/shard_map/reduce_scatter | solution.py:286
  517.7 1.0 copy-start.10
  521.1 17.6 %copy-start.2 = (bf16[1024,4,64]{0,2,1:T(8,128)(2,1)S(1)}, bf16[1024,4,64]{0,2,1:T(8,128)(2,1)}, u32[]{:S(2)}) copy-start(bf16[1024,4,64]{0,2,1:T(8,128)(2,1)} %copy-done.1) | copy-start | bytes 1572868
  521.9 12.7 all-to-all-start.2
  525.8 579.9 %reduce-scatter.6.cloned.1.call-start = ((), (), s32[]{:S(2)}) async-start(), calls=%async_computation.14 | async-start | bytes 14155776 | tf_op jit(solution)/shard_map/reduce_scatter | solution.py:286
  540.0 5.0 copy-start.5
  598.9 5.3 copy-start.5
  657.9 3.4 copy-start.12
  697.5 0.8 copy-start.20
  697.5 0.8 copy-start.26
  697.7 1.0 copy-start.22
  697.7 1.0 copy-start.25
  697.7 1.0 copy-start.30
  697.8 1.0 copy-start.32
  705.4 807.2 %reduce-scatter.14.cloned.1.call-start = ((), (), s32[]{:S(2)}) async-start(), calls=%async_computation.18 | async-start | bytes 28311552 | tf_op jit(solution)/shard_map/reduce_scatter | solution.py:286
  706.1 5.0 copy-start.35
  711.1 1.2 copy-start.6
  711.1 1.5 copy-start.7
  711.1 2.7 copy-start.39
  711.1 2.7 copy-start.38
  711.1 2.7 copy-start.37
  739.5 854.0 %all-reduce.10.cloned.1.call-start = ((), (), s32[]{:S(2)}) async-start(), calls=%async_computation.19 | async-start | bytes 7340032 | tf_op jit(solution)/shard_map/psum | solution.py:288
  1108.1 407.7 %copy-start.49 = (u32[32]{0:T(128)S(1)}, u32[32]{0:T(128)}, u32[]{:S(2)}) copy-start(u32[32]{0:T(128)} %constant.104) | copy-start | bytes 388
  1515.8 3.7 copy-start.33
  1515.8 3.7 copy-start.36
  1515.8 3.7 copy-start.40
  1593.5 3.5 copy-start.14
  1593.5 4.8 copy-start.16
  1597.0 2.4 copy-start.15
  1597.0 3.5 copy-start.23
  (1 other events, 0.7 us)
Sparse Core Ops, SparseCore 0:
  10.3 179.2 all-gather.10
  191.7 97.1 all-gather.12
  291.1 47.4 all-gather.14
  340.6 72.1 all-gather.16
  414.7 71.6 all-gather.18
  504.5 86.2 reduce-scatter.7
  594.9 148.7 reduce-scatter.9
  747.3 147.9 reduce-scatter.11
  899.3 206.3 reduce-scatter.5
  1110.0 402.5 reduce-scatter.13
  1516.7 76.8 all-reduce.9
where the time goes:
time: 1620 us; the launch traced here: 1610 us
  waiting for transfers between devices  1090 us (67%)
  blocking collectives  195 us (12%)
  matrix products  195 us (12%)
  other arithmetic  50.4 us (3%)
  local copies, waits for them, and re-layouts  43.7 us (3%)
  between operations  17.6 us (1%)
    reduce_scatter x5, waiting for transfers between devices, per_device(): lax.psum_scatter(grad_terms, 'dp', scatter_dimension=0, tiled=True)  765 us
    all_gather x1, waiting for transfers between devices, per_device(): lax.all_gather(shards[8], 'dp', axis=0, tiled=True)  119 us
    all_gather x1, waiting for transfers between devices, per_device(): lax.all_gather(shards[0], 'dp', axis=0, tiled=True)  93.1 us
    all_gather x1, waiting for transfers between devices, per_device(): lax.all_gather(shards[6], 'dp', axis=0, tiled=True)  57.1 us
    dot_general x2, matrix products, attend_back(): jnp.einsum('hqk,qhe->khe', d_scores, query_blk, preferred_element_type=jn...  47.1 us
    dot_general x2, matrix products, attend_back(): jnp.einsum('hqk,khe->qhe', d_scores, keys_heads, preferred_element_type=j...  36.3 us
    unnamed x1, blocking collectives  35.7 us
  transfers between devices with their start and end apart: 14, of which 10 were waited for; matrix products, arithmetic and copies ran while one was open for 16% of the time, Pallas kernels for 0%

commit v1 on v0

v1 whole, which is shorter than its diff:
```python
import math

import jax
import jax.numpy as jnp
from jax import lax
from jax.sharding import PartitionSpec as P

HEADS = 16


norm_eps = 1e-06


def layer_norm(values):
    mean_val = jnp.mean(values, axis=-1, keepdims=True)
    centred = values - mean_val
    variance = jnp.mean(centred * centred, axis=-1, keepdims=True)
    return centred * lax.rsqrt(variance + norm_eps)


def modulate(values, shift_term, scale_term):
    return layer_norm(values) * (1.0 + scale_term) + shift_term


def rotate(values, cosine_tab, sine_tab):
    half_dim = values.shape[-1] // 2
    lower_half = values[..., :half_dim]
    upper_half = values[..., half_dim:]
    return jnp.concatenate(
        [
            lower_half * cosine_tab - upper_half * sine_tab,
            upper_half * cosine_tab + lower_half * sine_tab,
        ],
        axis=-1,
    )


def angles(positions, head_dim):
    half_dim = head_dim // 2
    inv_rate = jnp.exp(
        jnp.arange(half_dim, dtype=jnp.float32) * (-2.0 * math.log(10000.0) / head_dim)
    )
    phases = positions.astype(jnp.float32)[:, None] * inv_rate[None, :]
    return (jnp.cos(phases)[:, None, :], jnp.sin(phases)[:, None, :])


def across_rows(left_side, right_side):
    return lax.dot_general(
        left_side, right_side, (((0,), (0,)), ((), ())), preferred_element_type=jnp.float32
    )


def against(left_side, right_side):
    return lax.dot_general(
        left_side, right_side, (((1,), (1,)), ((), ())), preferred_element_type=jnp.float32
    )


def forward_dot(left_side, right_side):
    return jnp.dot(left_side, right_side, preferred_element_type=jnp.float32)


def column_sums(values):
    return jnp.sum(values.astype(jnp.float32), axis=0)


def seq_gather(value):
    return lax.all_gather(value, "seq", axis=0, tiled=True)


def dp_gather(value):
    return lax.all_gather(value, "dp", axis=0, tiled=True)


def seq_reduce(value):
    return lax.psum_scatter(
        value.astype(jnp.bfloat16), "seq", scatter_dimension=0, tiled=True
    ).astype(jnp.float32)


def dp_reduce(value):
    return lax.psum_scatter(value.astype(jnp.bfloat16), "dp", scatter_dimension=0, tiled=True)


def clip_layout(lengths, length):
    clips = lengths.shape[0]
    earlier = jnp.arange(clips)[None, :] <= jnp.arange(clips)[:, None]
    clip_end = jnp.sum(jnp.where(earlier, lengths[None, :], 0), axis=1)
    clip_start = clip_end - lengths
    item_frames = jnp.arange(length, dtype=jnp.int32)
    inside = (item_frames[:, None] >= clip_start[None, :]) & (
        item_frames[:, None] < clip_end[None, :]
    )
    clip_ids = jnp.sum(
        jnp.where(inside, jnp.arange(clips, dtype=jnp.int32)[None, :], 0), axis=1
    )
    positions = item_frames - jnp.sum(jnp.where(inside, clip_start[None, :], 0), axis=1)
    return (clip_ids, positions)


def per_device(
    frames,
    time_embed,
    clip_len,
    w_qkv,
    b_qkv,
    w_out,
    b_out,
    w_up,
    b_up,
    w_down,
    b_down,
    w_mod,
    b_mod,
    cotangent,
):
    seq_count = lax.axis_size("seq")
    seq_rank = lax.axis_index("seq")
    dp_count = lax.axis_size("dp")
    dp_rank = lax.axis_index("dp")
    frame_rows = frames.shape[0]
    model_width = frames.shape[1]
    length = frame_rows * seq_count
    heads_here = HEADS // seq_count
    head_dim = model_width // HEADS
    local_width = heads_here * head_dim
    factor = head_dim ** (-0.5)
    block_rows = min(512, length)
    block_count = length // block_rows
    own_rows = w_qkv.shape[0]
    ff_width = w_up.shape[1]
    units_each = w_down.shape[0] // seq_count
    units_here = ff_width // seq_count

    def own_part(value, axis):
        return lax.dynamic_index_in_dim(value, seq_rank, axis, keepdims=False)

    wq_part = own_part(w_qkv.reshape(own_rows, 3, seq_count, local_width), 2).reshape(
        own_rows, 3 * local_width
    )
    wu_part = own_part(w_up.reshape(own_rows, dp_count, seq_count, units_each), 2).reshape(
        own_rows, units_here
    )
    wd_part = own_part(w_down.reshape(seq_count, units_each, model_width), 0)
    wq_here = dp_gather(wq_part)
    wo_full = dp_gather(w_out)
    wu_here = dp_gather(wu_part)
    wd_here = dp_gather(wd_part)
    sizes = [b_qkv.shape[0], b_out.shape[0], b_up.shape[0], b_down.shape[0]]
    biases = lax.all_gather(jnp.concatenate([b_qkv, b_out, b_up, b_down]), "dp", axis=0)
    cuts = [sizes[0], sizes[0] + sizes[1], sizes[0] + sizes[1] + sizes[2]]
    bq_all, bo_all, bu_all, bd_all = (
        b.astype(jnp.float32) for b in jnp.split(biases, cuts, axis=1)
    )
    bq_here = own_part(bq_all.reshape(3, seq_count, local_width), 1).reshape(3 * local_width)
    bo_full = bo_all.reshape(model_width)
    bu_here = own_part(bu_all.reshape(dp_count, seq_count, units_each), 1).reshape(units_here)
    bd_full = bd_all.reshape(model_width)

    clip_ids, positions = clip_layout(clip_len[0], length)
    cosine_tab, sine_tab = angles(positions, head_dim)

    time_act = jax.nn.silu(time_embed).astype(jnp.bfloat16)
    time_all = dp_gather(time_act)
    time_cols = lax.dynamic_slice_in_dim(time_all, dp_rank * own_rows, own_rows, 1)
    bias_cols = lax.dynamic_update_slice(
        jnp.zeros((6 * model_width,), jnp.float32),
        b_mod.astype(jnp.float32),
        (dp_rank * b_mod.shape[0],),
    )
    modulation = lax.psum_scatter(
        forward_dot(time_cols, w_mod) + bias_cols, "dp", scatter_dimension=0, tiled=True
    )
    shift_a, scale_a, gate_a, shift_f, scale_f, gate_f = jnp.split(modulation, 6, axis=1)

    d_ffn = (gate_f * cotangent).astype(jnp.bfloat16)
    d_ffn_item = seq_gather(d_ffn)
    x_a = seq_gather(modulate(frames, shift_a, scale_a).astype(jnp.bfloat16))
    projected = forward_dot(x_a, wq_here) + bq_here
    pieces = projected.reshape(length, 3, heads_here, head_dim)
    query_heads = rotate(pieces[:, 0], cosine_tab, sine_tab).astype(jnp.bfloat16)
    keys_heads = rotate(pieces[:, 1], cosine_tab, sine_tab).astype(jnp.bfloat16)
    values_heads = pieces[:, 2].astype(jnp.bfloat16)

    def block_scores(block_index):
        first_row = block_index * block_rows
        query_blk = lax.dynamic_slice_in_dim(query_heads, first_row, block_rows, 0)
        clip_blk = lax.dynamic_slice_in_dim(clip_ids, first_row, block_rows, 0)
        same_clip = (clip_blk[:, None] == clip_ids[None, :])[None]
        raw_scores = (
            jnp.einsum("qhe,khe->hqk", query_blk, keys_heads, preferred_element_type=jnp.float32)
            * factor
        )
        return (query_blk, same_clip, jnp.where(same_clip, raw_scores, -1e30))

    def attend(block_index):
        query_blk, same_clip, masked = block_scores(block_index)
        row_max = jnp.max(masked, axis=-1, keepdims=True)
        exp_scores = jnp.exp(masked - row_max)
        row_sum = jnp.sum(exp_scores, axis=-1, keepdims=True)
        attn_prob = (exp_scores / row_sum).astype(jnp.bfloat16)
        mixed_rows = jnp.einsum(
            "hqk,khe->qhe", attn_prob, values_heads, preferred_element_type=jnp.float32
        )
        return (mixed_rows.astype(jnp.bfloat16), row_max + jnp.log(row_sum))

    attn_blocks, log_totals = lax.map(attend, jnp.arange(block_count))
    attn_heads = attn_blocks.reshape(length, local_width)
    attn_out = lax.all_to_all(attn_heads, "seq", split_axis=0, concat_axis=1, tiled=True)
    attn_branch = forward_dot(attn_out, wo_full) + bo_full
    x_mid = frames + gate_a * attn_branch
    x_f = seq_gather(modulate(x_mid, shift_f, scale_f).astype(jnp.bfloat16))
    hidden = forward_dot(x_f, wu_here) + bu_here
    gelu_act, gelu_pull = jax.vjp(lambda inner: jax.nn.gelu(inner, approximate=True), hidden)
    gelu_act = gelu_act.astype(jnp.bfloat16)
    ffn_branch = seq_reduce(forward_dot(gelu_act, wd_here)) + bd_full
    block_out = x_mid + gate_f * ffn_branch
    d_gate_f = jnp.sum(cotangent * ffn_branch, axis=0, keepdims=True)
    d_gelu = against(d_ffn_item, wd_here)
    d_hidden = gelu_pull(d_gelu)[0].astype(jnp.bfloat16)
    d_xf = seq_reduce(against(d_hidden, wu_here))
    g_wd = across_rows(gelu_act, d_ffn_item)
    g_bd = column_sums(d_ffn_item)
    g_wu = across_rows(x_f, d_hidden)
    g_bu = column_sums(d_hidden)
    mid_pull = jax.vjp(modulate, x_mid, shift_f, scale_f)[1]
    d_mid_part, d_shift_f, d_scale_f = mid_pull(d_xf)
    d_mid = cotangent + d_mid_part
    d_attn = (gate_a * d_mid).astype(jnp.bfloat16)
    d_gate_a = jnp.sum(d_mid * attn_branch, axis=0, keepdims=True)
    g_wo_run = across_rows(attn_out, d_attn)
    g_wo = lax.psum_scatter(
        g_wo_run.astype(jnp.bfloat16), "seq", scatter_dimension=1, tiled=True
    )
    g_bo = column_sums(d_attn)
    d_out = against(d_attn, wo_full).astype(jnp.bfloat16)
    grad_heads = lax.all_to_all(d_out, "seq", split_axis=1, concat_axis=0, tiled=True).reshape(
        length, heads_here, head_dim
    )

    def attend_back(running, inputs):
        grad_keys, grad_values = running
        block_index, log_blk = inputs
        query_blk, same_clip, masked = block_scores(block_index)
        attn_prob = jnp.exp(masked - log_blk)
        prob_low = attn_prob.astype(jnp.bfloat16)
        grad_blk = lax.dynamic_slice_in_dim(grad_heads, block_index * block_rows, block_rows, 0)
        d_prob = jnp.einsum(
            "qhe,khe->hqk", grad_blk, values_heads, preferred_element_type=jnp.float32
        )
        d_scores = attn_prob * (d_prob - jnp.sum(d_prob * attn_prob, axis=-1, keepdims=True))
        d_scores = jnp.where(same_clip, d_scores, 0.0).astype(jnp.bfloat16)
        d_query = (
            jnp.einsum("hqk,khe->qhe", d_scores, keys_heads, preferred_element_type=jnp.float32)
            * factor
        )
        grad_keys = (
            grad_keys
            + jnp.einsum("hqk,qhe->khe", d_scores, query_blk, preferred_element_type=jnp.float32)
            * factor
        )
        grad_values = grad_values + jnp.einsum(
            "hqk,qhe->khe", prob_low, grad_blk, preferred_element_type=jnp.float32
        )
        return ((grad_keys, grad_values), d_query.astype(jnp.bfloat16))

    zero_heads = jnp.zeros((length, heads_here, head_dim), jnp.float32)
    (grad_keys, grad_values), query_grads = lax.scan(
        attend_back, (zero_heads, zero_heads), (jnp.arange(block_count), log_totals)
    )
    def turned_back(value):
        return rotate(value.astype(jnp.bfloat16).astype(jnp.float32), cosine_tab, -sine_tab)

    d_projected = jnp.concatenate(
        [
            turned_back(query_grads.reshape(length, heads_here, head_dim)).reshape(length, -1),
            turned_back(grad_keys).reshape(length, -1),
            grad_values.reshape(length, -1),
        ],
        axis=1,
    ).astype(jnp.bfloat16)
    d_xa = seq_reduce(against(d_projected, wq_here))
    g_wq = across_rows(x_a, d_projected)
    g_bq = column_sums(d_projected)
    input_pull = jax.vjp(modulate, frames, shift_a, scale_a)[1]
    d_input_part, d_shift_a, d_scale_a = input_pull(d_xa)
    grad_input = d_mid + d_input_part
    mod_part = jnp.concatenate(
        [d_shift_a, d_scale_a, d_gate_a, d_shift_f, d_scale_f, d_gate_f, g_bo[None]], axis=1
    )
    mod_sum = lax.psum(mod_part, "seq")
    d_mod = dp_gather(mod_sum[:, : 6 * model_width].astype(jnp.bfloat16))
    g_wm = across_rows(time_cols, d_mod)
    g_bm = column_sums(
        lax.dynamic_slice_in_dim(d_mod, dp_rank * b_mod.shape[0], b_mod.shape[0], 1)
    )
    d_time_act = lax.all_to_all(
        against(d_mod, w_mod), "dp", split_axis=0, concat_axis=1, tiled=True
    )
    grad_time = jax.vjp(jax.nn.silu, time_embed)[1](d_time_act)[0]

    def spread(value):
        return lax.all_gather(dp_reduce(value), "seq", axis=0).astype(jnp.float32)

    s_wq = (
        spread(g_wq)
        .reshape(seq_count, own_rows, 3, local_width)
        .transpose(1, 2, 0, 3)
        .reshape(own_rows, 3 * model_width)
    )
    s_wo = spread(g_wo).transpose(1, 0, 2).reshape(own_rows, model_width)
    s_wu = (
        spread(g_wu)
        .reshape(seq_count, own_rows, dp_count, units_each)
        .transpose(1, 2, 0, 3)
        .reshape(own_rows, ff_width)
    )
    s_wd = spread(g_wd).reshape(seq_count * units_each, model_width)
    bq_item = lax.all_gather(g_bq, "seq", axis=0).reshape(seq_count, 3, local_width)
    bu_item = lax.all_gather(g_bu, "seq", axis=0).reshape(seq_count, dp_count, units_each)
    bias_terms = jnp.concatenate(
        [
            bq_item.transpose(1, 0, 2).reshape(dp_count, sizes[0]),
            mod_sum[:, 6 * model_width :].reshape(dp_count, sizes[1]),
            bu_item.transpose(1, 0, 2).reshape(dp_count, sizes[2]),
            g_bd.reshape(dp_count, sizes[3]),
        ],
        axis=1,
    )
    bias_sums = lax.psum_scatter(bias_terms, "dp", scatter_dimension=0, tiled=True)[0]
    s_bq, s_bo, s_bu, s_bd = jnp.split(bias_sums, cuts)
    return (
        block_out,
        grad_input,
        grad_time,
        s_wq,
        s_bq,
        s_wo,
        s_bo,
        s_wu,
        s_bu,
        s_wd,
        s_bd,
        g_wm,
        g_bm,
    )


def solution(mesh):
    placed = (
        P(("dp", "seq"), None),
        P("dp", None),
        P("dp", None),
        P("dp", None),
        P("dp"),
        P("dp", None),
        P("dp"),
        P("dp", None),
        P("dp"),
        P("dp", None),
        P("dp"),
        P("dp", None),
        P("dp"),
        P(("dp", "seq"), None),
    )
    return jax.shard_map(
        per_device,
        mesh=mesh,
        in_specs=placed,
        out_specs=(
            P(("dp", "seq"), None),
            P(("dp", "seq"), None),
            P("dp", None),
            P("dp", None),
            P("dp"),
            P("dp", None),
            P("dp"),
            P("dp", None),
            P("dp"),
            P("dp", None),
            P("dp"),
            P("dp", None),
            P("dp"),
        ),
        check_vma=False,
    )
```

time: 1620 us -> 847 us (0.52)
  waiting for transfers between devices: 1090 us -> 362 us
  matrix products: 195 us -> 170 us
  other arithmetic: 50.4 us -> 34 us
    reduce_scatter x5 -> x8, waiting for transfers between devices: 765 us -> 129 us  [the longest x3 92.1 us: seq_reduce(): lax.psum_scatter(value.astype(jnp.bfloat16), 'seq', scatter_dimension=0,...]
    all_gather x5 -> x7, waiting for transfers between devices: 269 us -> 162 us  [the longest x4 92.9 us: dp_gather(): return lax.all_gather(value, 'dp', axis=0, tiled=True)]
    unnamed x11 -> x17, waiting for transfers between devices: 2.69 us -> 66.8 us
    all_to_all x1 -> x0, blocking collectives: 28.9 us -> none  [per_device(): lax.all_to_all(grads_stacked.reshape(length, 3, local_width), 'seq', spli...]
    all_to_all x1, waiting for transfers between devices: 25.1 us -> 0.01 us  [per_device(): lax.all_to_all(against(d_mod, w_mod), 'dp', split_axis=0, concat_axis=1,...]
    all_gather x5 -> x9, blocking collectives: 111 us -> 135 us  [the longest x2 63.2 us: dp_gather(): return lax.all_gather(value, 'dp', axis=0, tiled=True)]
    convert_element_type x25 -> x3, other arithmetic: 23.8 us -> 2.19 us  [the longest x1 1.05 us: per_device(): x_f = seq_gather(modulate(x_mid, shift_f, scale_f).astype(jnp.bfloat16))]
    psum x1 -> x0, waiting for transfers between devices: 20.6 us -> none  [per_device(): lax.psum(as_sent(tuple(dp_sums)), 'seq')]
  transfers between devices with their start and end apart: 14 -> 19, of which waited for: 10 -> 14; matrix products, arithmetic and copies ran while one was open for 16% -> 27% of each run, Pallas kernels for 0% -> 0%
where the time goes in v1:
time: 847 us; the launch traced here: 837 us
  waiting for transfers between devices  362 us (43%)
  blocking collectives  183 us (22%)
  matrix products  170 us (20%)
  local copies, waits for them, and re-layouts  55.6 us (7%)
  other arithmetic  34 us (4%)
  between operations  14.9 us (2%)
  starting transfers between devices  14.3 us (2%)
    all_gather x4, waiting for transfers between devices, dp_gather(): return lax.all_gather(value, 'dp', axis=0, tiled=True)  92.9 us
    reduce_scatter x3, waiting for transfers between devices, seq_reduce(): lax.psum_scatter(value.astype(jnp.bfloat16), 'seq', scatter_dimension=0,...  92.1 us
    all_gather x3, waiting for transfers between devices, seq_gather(): return lax.all_gather(value, 'seq', axis=0, tiled=True)  69.3 us
    unnamed x17, waiting for transfers between devices  66.8 us
    all_gather x2, blocking collectives, dp_gather(): return lax.all_gather(value, 'dp', axis=0, tiled=True)  63.2 us
    dot_general x2, matrix products, attend_back(): jnp.einsum('hqk,qhe->khe', d_scores, query_blk, preferred_element_type=jn...  47.9 us
    dot_general x2, matrix products, attend_back(): jnp.einsum('hqk,khe->qhe', d_scores, keys_heads, preferred_element_type=j...  45 us
    unnamed x1, blocking collectives  37.6 us
  transfers between devices with their start and end apart: 19, of which 14 were waited for; matrix products, arithmetic and copies ran while one was open for 27% of the time, Pallas kernels for 0%

profile of v1, /device:TPU:0, one launch (start us, length us, event | category | flops | bytes accessed | tf_op | source)
XLA Modules:
  0.0 837.3 jit_solution(6360103712881818143)
XLA Ops:
  8.7 32.2 %all-gather.8 = bf16[8,1,1024]{2,1,0:T(2,128)(2,1)S(1)} all-gather(bf16[1,1,1024]{2,1,0:T(2,128)(2,1)S(1)} %get-tuple-element.283), channel_id=1, replica_groups=mesh['dp'=8,'seq'=4] {'dp'}, dimensions={0}, use_global_device_ids=true | all-gather | bytes 18432 | tf_op jit(solution)/shard_map/all_gather | solution.py:72
  42.7 2.3 copy.92
  47.8 66.0 %all-reduce.4.cloned.1.call-done = f32[8,6144]{1,0:T(8,128)} async-done(((f32[8,6144]{1,0:T(8,128)}), f32[8,6144]{1,0:T(8,128)}) %all-reduce.4.cloned.1.call-update) | async-done | bytes 196624
  120.1 30.6 %all-gather.9 = bf16[8,1,896]{2,1,0:T(2,128)(2,1)S(1)} all-gather(bf16[1,1,896]{2,1,0:T(2,128)(2,1)S(1)} %reshape.463), channel_id=2, replica_groups=mesh['dp'=8,'seq'=4] {'dp'}, dimensions={0}, use_global_device_ids=true | all-gather | bytes 16128 | tf_op jit(solution)/shard_map/all_gather | solution.py:150
  151.9 9.3 %all-gather.23.cloned.1.call-done = bf16[1024,768]{0,1:T(8,128)(2,1)} async-done(((bf16[128,768]{0,1:T(8,128)(2,1)}), bf16[1024,768]{0,1:T(8,128)(2,1)}) %all-gather.23.cloned.1.call-update) | async-done | bytes 1572880 | tf_op jit(solution)/shard_map/all_gather | solution.py:72
  161.2 23.0 %all-gather.21.cloned.1.call-done = bf16[1024,1024]{1,0:T(8,128)(2,1)} async-done(((bf16[256,1024]{1,0:T(8,128)(2,1)}), bf16[1024,1024]{1,0:T(8,128)(2,1)}) %all-gather.21.cloned.1.call-update) | async-done | bytes 2097168 | tf_op jit(solution)/shard_map/all_gather | solution.py:68
  184.2 3.9 convolution_add_fusion.1
  191.4 21.1 %while.27 = (s32[]{:T(128)}, bf16[2,512,4,64]{1,3,2,0:T(8,128)(2,1)}, f32[2,4,512,1]{2,1,3,0:T(4,128)S(1)}, s32[2]{0:T(128)S(1)}, s32[1024]{0:T(1024)S(1)}, /*in...) while((s32[]{:T(128)}, ...), condition=%wide.region_9.10_spmd, body=%wide.region_6.9_spmd.sunk | while | flops 562690048 | bytes 35203356 | solution.py:207
  193.1 2.6 fusion.181
  195.7 2.3 fusion.182
  198.1 3.0 fusion.183
  203.6 2.6 fusion.181
  206.3 2.3 fusion.182
  208.6 3.0 fusion.183
  212.4 2.5 copy.93
  214.9 2.9 all_to_all.38
  219.7 4.2 all-to-all-start
  224.1 11.6 %all-gather.25.cloned.1.call-done = bf16[1024,1024]{1,0:T(8,128)(2,1)} async-done(((bf16[128,1024]{1,0:T(8,128)(2,1)}), bf16[1024,1024]{1,0:T(8,128)(2,1)}) %all-gather.25.cloned.1.call-update) | async-done | bytes 2097168 | tf_op jit(solution)/shard_map/all_gather | solution.py:72
  235.8 3.5 fusion.131
  243.2 33.3 %all-gather.29.cloned.1.call-done = bf16[1024,512]{0,1:T(8,128)(2,1)} async-done(((bf16[128,512]{0,1:T(8,128)(2,1)}), bf16[1024,512]{0,1:T(8,128)(2,1)}) %all-gather.29.cloned.1.call-update) | async-done | bytes 1048592 | tf_op jit(solution)/shard_map/all_gather | solution.py:72
  276.5 23.6 %all-gather.27.cloned.1.call-done = bf16[1024,1024]{1,0:T(8,128)(2,1)} async-done(((bf16[256,1024]{1,0:T(8,128)(2,1)}), bf16[1024,1024]{1,0:T(8,128)(2,1)}) %all-gather.27.cloned.1.call-update) | async-done | bytes 2097168 | tf_op jit(solution)/shard_map/all_gather | solution.py:68
  300.1 4.5 fusion.133
  304.5 38.6 %all-gather.33.cloned.1.call-done = bf16[1,512,1024]{2,1,0:T(8,128)(2,1)} async-done(((bf16[1,64,1024]{2,1,0:T(8,128)(2,1)}), bf16[1,512,1024]{2,1,0:T(8,128)(2,1)}) %all-gather.33.cloned.1.call-update) | async-done | bytes 1048592 | tf_op jit(solution)/shard_map/all_gather | solution.py:72
  343.2 4.7 convolution_convert_fusion.2
  347.9 30.3 %reduce-scatter.9.cloned.1.call-done = bf16[256,1024]{1,0:T(8,128)(2,1)} async-done(((bf16[1024,1024]{1,0:T(8,128)(2,1)}), bf16[256,1024]{1,0:T(8,128)(2,1)}) %reduce-scatter.9.cloned.1.call-update) | async-done | bytes 524304 | tf_op jit(solution)/shard_map/reduce_scatter | solution.py:76
  378.2 2.6 multiply_reduce_fusion.1
  381.0 22.7 %all-gather.31.cloned.1.call-done = bf16[1024,1024]{1,0:T(8,128)(2,1)} async-done(((bf16[256,1024]{1,0:T(8,128)(2,1)}), bf16[1024,1024]{1,0:T(8,128)(2,1)}) %all-gather.31.cloned.1.call-update) | async-done | bytes 2097168 | tf_op jit(solution)/shard_map/all_gather | solution.py:68
  403.6 5.1 convert_reduce_fusion.2
  409.7 2.6 convolution_convert_fusion.1
  412.3 4.2 convolution_convert_fusion.6
  416.6 27.3 %reduce-scatter.11.cloned.1.call-done = bf16[256,1024]{1,0:T(8,128)(2,1)} async-done(((bf16[1024,1024]{1,0:T(8,128)(2,1)}), bf16[256,1024]{1,0:T(8,128)(2,1)}) %reduce-scatter.11.cloned.1.call-update) | async-done | bytes 524304 | tf_op jit(solution)/shard_map/reduce_scatter | solution.py:76
  450.5 4.2 all-to-all-start.1
  454.7 4.7 convolution_convert_fusion.5
  459.5 4.1 all-to-all-done.1
  463.6 2.1 copy.97
  465.7 2.2 reshape.394
  468.7 117.4 %while.28 = (s32[]{:T(128)}, f32[1024,4,64]{0,2,1:T(8,128)}, f32[1024,4,64]{0,2,1:T(8,128)}, bf16[2,512,4,64]{1,3,2,0:T(8,128)(2,1)}, s32[2]{0:T(128)S(1)}, /*in...) while((s32[]{:T(128)}, f32[1024,4,64]{0,2,1:T(8,128)}, ...), condition=%wide.region_18.19_spmd.clone, body=%wide.region_16.18_spmd.clone.sunk | while | flops 1398806528 | bytes 148703632 | solution.py:268
  472.4 2.5 fusion.197
  476.6 4.5 fusion.194
  481.1 22.5 %fusion.198 = bf16[2,512,4,64]{1,3,2,0:T(8,128)(2,1)} fusion(bf16[2,512,4,64]{1,3,2,0:T(8,128)(2,1)} %get-tuple-element.498, s32[]{:T(128)S(6)} %copy.148, bf16[1024,4,64]{0,2,1:T(8,128)(2,1)S(1)} %get-tuple-element.517, f32[4,512,1024]{2,1,0:T(8,128)} %fusion.194, f32[4,512,1024]{2,1,0:T(8,128)} %copy-done.1, ...), kind=kOutput, calls=%fused_computation.44.clone.1 | convolution fusion | flops 291769344 | bytes 35405828 | tf_op jit(solution)/shard_map/while/body/eval_jaxpr/hqk,khe->qhe/dot_general | solution.py:254
  503.6 23.8 %fusion.196 = f32[1024,4,64]{0,2,1:T(8,128)} fusion(f32[4,512,1024]{2,1,0:T(8,128)} %fusion.194, f32[4,512,1024]{2,1,0:T(8,128)} %copy-done.1, f32[4,512]{1,0:T(4,128)S(1)} %dynamic-slice_bitcast_fusion.4, pred[512,1024]{1,0:T(8,128)(4,1)} %copy-done.9, f32[1024,4,64]{0,2,1:T(8,128)} %get-tuple-element.496, pred[]{:T(512)S(6)} %compare.3, ...), kind=kOutput, calls=%fused_computation.39.clone.1 | convolution fusion | flops 292293632 | bytes 36978692 | tf_op jit(solution)/shard_map/while/body/eval_jaxpr/hqk,qhe->khe/dot_general | solution.py:259
  530.7 2.5 fusion.197
  534.9 4.5 fusion.194
  539.4 22.5 %fusion.198 = bf16[2,512,4,64]{1,3,2,0:T(8,128)(2,1)} fusion(bf16[2,512,4,64]{1,3,2,0:T(8,128)(2,1)} %get-tuple-element.498, s32[]{:T(128)S(6)} %copy.148, bf16[1024,4,64]{0,2,1:T(8,128)(2,1)S(1)} %get-tuple-element.517, f32[4,512,1024]{2,1,0:T(8,128)} %fusion.194, f32[4,512,1024]{2,1,0:T(8,128)} %copy-done.1, ...), kind=kOutput, calls=%fused_computation.44.clone.1 | convolution fusion | flops 291769344 | bytes 35405828 | tf_op jit(solution)/shard_map/while/body/eval_jaxpr/hqk,khe->qhe/dot_general | solution.py:254
  561.9 24.1 %fusion.196 = f32[1024,4,64]{0,2,1:T(8,128)} fusion(f32[4,512,1024]{2,1,0:T(8,128)} %fusion.194, f32[4,512,1024]{2,1,0:T(8,128)} %copy-done.1, f32[4,512]{1,0:T(4,128)S(1)} %dynamic-slice_bitcast_fusion.4, pred[512,1024]{1,0:T(8,128)(4,1)} %copy-done.9, f32[1024,4,64]{0,2,1:T(8,128)} %get-tuple-element.496, pred[]{:T(512)S(6)} %compare.3, ...), kind=kOutput, calls=%fused_computation.39.clone.1 | convolution fusion | flops 292293632 | bytes 36978692 | tf_op jit(solution)/shard_map/while/body/eval_jaxpr/hqk,qhe->khe/dot_general | solution.py:259
  590.8 3.0 convolution_convert_fusion.4
  593.9 3.3 convolution_convert_fusion
  597.2 4.6 convolution_convert_fusion.3
  601.9 5.2 all-gather.12
  609.2 8.1 all-gather.6
  622.6 7.7 all-gather.7
  631.6 5.2 all-gather.11
  636.8 22.0 %reduce-scatter.15.cloned.1.call-done = bf16[128,768]{1,0:T(8,128)(2,1)} async-done(((bf16[1024,768]{1,0:T(8,128)(2,1)}), bf16[128,768]{1,0:T(8,128)(2,1)}) %reduce-scatter.15.cloned.1.call-update) | async-done | bytes 196624 | tf_op jit(solution)/shard_map/reduce_scatter | solution.py:82
  658.9 9.2 %all-gather.2 = bf16[512,768]{1,0:T(8,128)(2,1)} all-gather(bf16[128,768]{1,0:T(8,128)(2,1)} %reduce-scatter.15.cloned.1.call-done), channel_id=4, replica_groups=mesh['dp'=8,'seq'=4] {'seq'}, dimensions={0}, use_global_device_ids=true | all-gather | bytes 983040 | tf_op jit(solution)/shard_map/all_gather | solution.py:303
  671.2 2.7 copy.101
  673.9 3.1 copy.107
  677.0 14.6 %reduce-scatter.17.cloned.1.call-done = bf16[1024,256]{1,0:T(8,128)(2,1)} async-done(((bf16[1024,1024]{1,0:T(8,128)(2,1)}), bf16[1024,256]{1,0:T(8,128)(2,1)}) %reduce-scatter.17.cloned.1.call-update) | async-done | bytes 524304 | tf_op jit(solution)/shard_map/reduce_scatter | solution.py:232
  691.6 34.6 %reduce-scatter.13.cloned.1.call-done = bf16[256,1024]{1,0:T(8,128)(2,1)} async-done(((bf16[1024,1024]{1,0:T(8,128)(2,1)}), bf16[256,1024]{1,0:T(8,128)(2,1)}) %reduce-scatter.13.cloned.1.call-update) | async-done | bytes 524304 | tf_op jit(solution)/shard_map/reduce_scatter | solution.py:76
  730.9 10.7 %psum.7 = f32[1,7168]{1,0:T(1,128)S(1)} all-reduce(f32[1,7168]{1,0:T(1,128)S(1)} %constant_dynamic-update-slice_fusion), channel_id=1, replica_groups=mesh['dp'=8,'seq'=4] {'seq'}, use_global_device_ids=true, to_apply=%region_29.30 | all-reduce | flops 7168 | bytes 57344 | tf_op jit(solution)/shard_map/psum | solution.py:291
  741.6 31.0 %all-gather.10 = bf16[8,1,6144]{2,1,0:T(2,128)(2,1)S(1)} all-gather(bf16[1,1,6144]{2,1,0:T(2,128)(2,1)S(1)} %fusion.121), channel_id=1, replica_groups=mesh['dp'=8,'seq'=4] {'dp'}, dimensions={0}, use_global_device_ids=true | all-gather | bytes 110592 | tf_op jit(solution)/shard_map/all_gather | solution.py:72
  773.7 5.2 all-to-all-start.2
  778.9 37.6 %all-reduce.1 = f32[8,896]{1,0:T(8,128)S(1)} all-reduce(f32[8,896]{1,0:T(8,128)S(1)} %pad_maximum_fusion.5), channel_id=15, replica_groups=mesh['dp'=8,'seq'=4] {'dp'}, use_global_device_ids=true, to_apply=%region_34.35.clone | all-reduce | flops 7168 | bytes 57344
  816.5 2.3 fusion.113
  823.7 6.0 all-gather.5
  (284 shorter events, 71.6 us)
Async XLA Ops:
  7.2 34.5 %copy-start = (bf16[128,6144]{1,0:T(8,128)(2,1)S(1)}, bf16[128,6144]{1,0:T(8,128)(2,1)}, u32[]{:S(2)}) copy-start(bf16[128,6144]{1,0:T(8,128)(2,1)} %param.29) | copy-start | bytes 4718596
  7.2 106.6 %all-reduce.4.cloned.1.call-start = ((), (), s32[]{:S(2)}) async-start(), calls=%async_computation.26 | async-start | bytes 393216
  40.8 5.8 copy-start.40
  41.7 5.1 copy-start.2
  42.7 4.2 copy-start.53
  42.7 118.5 %all-gather.23.cloned.1.call-start = ((), (), s32[]{:S(2)}) async-start(), calls=%async_computation.12 | async-start | bytes 1769472 | tf_op jit(solution)/shard_map/all_gather | solution.py:72
  46.7 137.5 %all-gather.21.cloned.1.call-start = ((), (), s32[]{:S(2)}) async-start(), calls=%async_computation.11 | async-start | bytes 2621440 | tf_op jit(solution)/shard_map/all_gather | solution.py:68
  47.5 71.5 %copy-start.35 = (f32[256]{0:T(256)}, f32[256]{0:T(256)S(1)}, u32[]{:S(2)}) copy-start(f32[256]{0:T(256)S(1)} %broadcast_multiply_fusion.1) | copy-start | bytes 3076
  47.8 66.1 %copy-start.44 = (f32[256]{0:T(256)}, f32[256]{0:T(256)S(1)}, u32[]{:S(2)}) copy-start(f32[256]{0:T(256)S(1)} %multiply_reduce_fusion.4) | copy-start | bytes 3076
  47.8 72.0 %copy-start.52 = (s32[1,6]{1,0:T(1,128)S(1)}, s32[1,6]{1,0:T(1,128)}, u32[]{:S(2)}) copy-start(s32[1,6]{1,0:T(1,128)} %param.20) | copy-start | bytes 76
  47.8 72.1 %copy-start.46 = (bf16[384]{0:T(512)(128)(2,1)S(1)}, bf16[384]{0:T(512)(128)(2,1)}, u32[]{:S(2)}) copy-start(bf16[384]{0:T(512)(128)(2,1)} %param.22) | copy-start | bytes 2308
  47.8 72.1 %copy-start.47 = (bf16[128]{0:T(256)(128)(2,1)S(1)}, bf16[128]{0:T(256)(128)(2,1)}, u32[]{:S(2)}) copy-start(bf16[128]{0:T(256)(128)(2,1)} %param.28) | copy-start | bytes 772
  47.8 72.1 %copy-start.48 = (bf16[256]{0:T(256)(128)(2,1)S(1)}, bf16[256]{0:T(256)(128)(2,1)}, u32[]{:S(2)}) copy-start(bf16[256]{0:T(256)(128)(2,1)} %param.26) | copy-start | bytes 1540
  47.8 72.1 %copy-start.49 = (bf16[128]{0:T(256)(128)(2,1)S(1)}, bf16[128]{0:T(256)(128)(2,1)}, u32[]{:S(2)}) copy-start(bf16[128]{0:T(256)(128)(2,1)} %param.24) | copy-start | bytes 772
  47.8 71.9 %copy-start.42 = (f32[256]{0:T(256)}, f32[256]{0:T(256)S(1)}, u32[]{:S(2)}) copy-start(f32[256]{0:T(256)S(1)} %fusion.126) | copy-start | bytes 3076
  117.1 118.7 %all-gather.25.cloned.1.call-start = ((), (), s32[]{:S(2)}) async-start(), calls=%async_computation.13 | async-start | bytes 2359296 | tf_op jit(solution)/shard_map/all_gather | solution.py:72
  117.7 158.8 %all-gather.29.cloned.1.call-start = ((), (), s32[]{:S(2)}) async-start(), calls=%async_computation.15 | async-start | bytes 1179648 | tf_op jit(solution)/shard_map/all_gather | solution.py:72
  151.9 37.3 %copy-start.26 = (f32[1024,32]{0,1:T(8,128)}, f32[1024,32]{0,1:T(8,128)S(1)}, u32[]{:S(2)}) copy-start(f32[1024,32]{0,1:T(8,128)S(1)} %get-tuple-element.318) | copy-start | bytes 393220
  195.7 2.4 copy-start.6
  195.7 2.4 copy-start.22
  206.2 2.4 copy-start.6
  206.2 2.4 copy-start.22
  219.7 16.0 %all-to-all-start = ((bf16[4,256,256]{1,2,0:T(8,128)(2,1)}), bf16[4,256,256]{1,2,0:T(8,128)(2,1)}, u32[]{:S(2)}, u32[]{:S(2)}) async-start(bf16[4,256,256]{1,2,0:T(8,128)(2,1)} %copy.94), calls=%async_computation | async-start | bytes 1048576 | tf_op jit(solution)/shard_map/all_to_all | solution.py:209
  223.9 76.2 %all-gather.27.cloned.1.call-start = ((), (), s32[]{:S(2)}) async-start(), calls=%async_computation.14 | async-start | bytes 2621440 | tf_op jit(solution)/shard_map/all_gather | solution.py:68
  241.3 101.9 %all-gather.33.cloned.1.call-start = ((), (), s32[]{:S(2)}) async-start(), calls=%async_computation.25 | async-start | bytes 1179648 | tf_op jit(solution)/shard_map/all_gather | solution.py:72
  243.0 135.3 %reduce-scatter.9.cloned.1.call-start = ((), (), s32[]{:S(2)}) async-start(), calls=%async_computation.16 | async-start | bytes 2621440 | tf_op jit(solution)/shard_map/reduce_scatter | solution.py:76
  347.9 30.4 %copy-start.14 = (f32[256,1024]{1,0:T(8,128)S(1)}, f32[256,1024]{1,0:T(8,128)}, u32[]{:S(2)}) copy-start(f32[256,1024]{1,0:T(8,128)} %param.31) | copy-start | bytes 3145732
  347.9 55.8 %all-gather.31.cloned.1.call-start = ((), (), s32[]{:S(2)}) async-start(), calls=%async_computation.17 | async-start | bytes 2621440 | tf_op jit(solution)/shard_map/all_gather | solution.py:68
  380.9 28.8 %copy-start.51 = (bf16[1024,512]{0,1:T(8,128)(2,1)S(1)}, bf16[1024,512]{0,1:T(8,128)(2,1)}, u32[]{:S(2)}) copy-start(bf16[1024,512]{0,1:T(8,128)(2,1)} %all-gather.29.cloned.1.call-done) | copy-start | bytes 3145732
  380.9 63.0 %reduce-scatter.11.cloned.1.call-start = ((), (), s32[]{:S(2)}) async-start(), calls=%async_computation.18 | async-start | bytes 2621440 | tf_op jit(solution)/shard_map/reduce_scatter | solution.py:76
  412.3 31.6 %copy-start.5 = (f32[256,1024]{1,0:T(8,128)S(1)}, f32[256,1024]{1,0:T(8,128)}, u32[]{:S(2)}) copy-start(f32[256,1024]{1,0:T(8,128)} %copy-done.4) | copy-start | bytes 3145732
  412.3 196.9 %reduce-scatter.21.cloned.1.call-start = ((), (), s32[]{:S(2)}) async-start(), calls=%async_computation.23 | async-start | bytes 1179648 | tf_op jit(solution)/shard_map/reduce_scatter | solution.py:82
  443.9 3.1 copy-start.12
  443.9 3.1 copy-start.15
  443.9 3.1 copy-start.25
  447.0 1.9 copy-start.17
  448.9 1.6 copy-start.24
  450.5 13.1 %all-to-all-start.1 = ((bf16[256,4,256]{2,0,1:T(8,128)(2,1)}), bf16[256,4,256]{2,0,1:T(8,128)(2,1)}, u32[]{:S(2)}, u32[]{:S(2)}) async-start(bf16[256,4,256]{2,0,1:T(8,128)(2,1)} %bitcast.171), calls=%async_computation.3 | async-start | bytes 1048576 | tf_op jit(solution)/shard_map/all_to_all | solution.py:237
  454.7 167.9 %reduce-scatter.23.cloned.1.call-start = ((), (), s32[]{:S(2)}) async-start(), calls=%async_computation.24 | async-start | bytes 1179648 | tf_op jit(solution)/shard_map/reduce_scatter | solution.py:82
  459.4 9.3 %copy-start.7 = (bf16[1024,4,64]{0,2,1:T(8,128)(2,1)S(1)}, bf16[1024,4,64]{0,2,1:T(8,128)(2,1)}, u32[]{:S(2)}) copy-start(bf16[1024,4,64]{0,2,1:T(8,128)(2,1)} %get-tuple-element.542) | copy-start | bytes 1572868
  459.4 9.3 %copy-start.8 = (bf16[1024,4,64]{0,2,1:T(8,128)(2,1)S(1)}, bf16[1024,4,64]{0,2,1:T(8,128)(2,1)}, u32[]{:S(2)}) copy-start(bf16[1024,4,64]{0,2,1:T(8,128)(2,1)} %get-tuple-element.543) | copy-start | bytes 1572868
  459.5 199.4 %reduce-scatter.15.cloned.1.call-start = ((), (), s32[]{:S(2)}) async-start(), calls=%async_computation.20 | async-start | bytes 1769472 | tf_op jit(solution)/shard_map/reduce_scatter | solution.py:82
  472.4 3.2 copy-start.1
  530.7 3.2 copy-start.1
  588.8 2.0 copy-start.50
  589.2 8.0 copy-start.18
  589.3 8.0 copy-start.20
  593.8 97.8 %reduce-scatter.17.cloned.1.call-start = ((), (), s32[]{:S(2)}) async-start(), calls=%async_computation.21 | async-start | bytes 2621440 | tf_op jit(solution)/shard_map/reduce_scatter | solution.py:232
  597.2 129.0 %reduce-scatter.13.cloned.1.call-start = ((), (), s32[]{:S(2)}) async-start(), calls=%async_computation.19 | async-start | bytes 2621440 | tf_op jit(solution)/shard_map/reduce_scatter | solution.py:76
  601.8 221.8 %reduce-scatter.19.cloned.1.call-start = ((), (), s32[]{:S(2)}) async-start(), calls=%async_computation.22 | async-start | bytes 589824 | tf_op jit(solution)/shard_map/reduce_scatter | solution.py:82
  622.6 8.8 %copy-start.19 = (bf16[1024,4,64]{0,2,1:T(8,128)(2,1)S(1)}, bf16[1024,4,64]{0,2,1:T(8,128)(2,1)}, u32[]{:S(2)}) copy-start(bf16[1024,4,64]{0,2,1:T(8,128)(2,1)} %copy-done.18) | copy-start | bytes 1572868
  622.6 8.8 %copy-start.21 = (bf16[1024,4,64]{0,2,1:T(8,128)(2,1)S(1)}, bf16[1024,4,64]{0,2,1:T(8,128)(2,1)}, u32[]{:S(2)}) copy-start(bf16[1024,4,64]{0,2,1:T(8,128)(2,1)} %copy-done.20) | copy-start | bytes 1572868
  673.9 52.3 %copy-start.3 = (f32[256,1024]{1,0:T(8,128)S(1)}, f32[256,1024]{1,0:T(8,128)}, u32[]{:S(2)}) copy-start(f32[256,1024]{1,0:T(8,128)} %param.18) | copy-start | bytes 3145732
  673.9 52.3 %copy-start.34 = (f32[1,1024]{1,0:T(1,128)S(1)}, f32[1,1024]{1,0:T(1,128)}, u32[]{:S(2)}) copy-start(f32[1,1024]{1,0:T(1,128)} %copy-done.33) | copy-start | bytes 12292
  673.9 52.3 %copy-start.36 = (f32[256]{0:T(256)S(1)}, f32[256]{0:T(256)}, u32[]{:S(2)}) copy-start(f32[256]{0:T(256)} %copy-done.35) | copy-start | bytes 3076
  673.9 53.8 %copy-start.45 = (f32[256]{0:T(256)S(1)}, f32[256]{0:T(256)}, u32[]{:S(2)}) copy-start(f32[256]{0:T(256)} %copy-done.44) | copy-start | bytes 3076
  673.9 53.8 %copy-start.43 = (f32[256]{0:T(256)S(1)}, f32[256]{0:T(256)}, u32[]{:S(2)}) copy-start(f32[256]{0:T(256)} %copy-done.42) | copy-start | bytes 3076
  726.2 3.2 copy-start.11
  726.2 3.2 copy-start.13
  726.2 3.2 copy-start.16
  730.8 85.6 %copy-start.41 = (bf16[8,1,128]{2,1,0:T(2,128)(2,1)S(1)}, bf16[8,1,128]{2,1,0:T(2,128)(2,1)}, u32[]{:S(2)}) copy-start(bf16[8,1,128]{2,1,0:T(2,128)(2,1)} %copy-done.40) | copy-start | bytes 6148
  773.7 49.4 %copy-start.38 = (f32[1,1024]{1,0:T(1,128)S(1)}, f32[1,1024]{1,0:T(1,128)}, u32[]{:S(2)}) copy-start(f32[1,1024]{1,0:T(1,128)} %param.19) | copy-start | bytes 12292
  773.7 49.4 %copy-start.39 = (f32[1,1024]{1,0:T(1,128)S(1)}, f32[1,1024]{1,0:T(1,128)}, u32[]{:S(2)}) copy-start(f32[1,1024]{1,0:T(1,128)} %get-tuple-element.284) | copy-start | bytes 12292
  773.7 49.3 %all-to-all-start.2 = ((f32[8,1,128]{2,1,0:T(1,128)}), f32[8,1,128]{2,1,0:T(1,128)S(1)}, u32[]{:S(2)}, u32[]{:S(2)}) async-start(f32[8,1,128]{2,1,0:T(1,128)} %bitcast.42), calls=%async_computation.5 | async-start | bytes 8192 | tf_op jit(solution)/shard_map/all_to_all | solution.py:297
  (18 other events, 21.2 us)
Sparse Core Ops, SparseCore 0:
  42.8 70.9 all-reduce.3
  116.7 44.4 all-gather.22
  163.4 20.7 all-gather.20
  186.4 49.2 all-gather.24
  238.4 38.0 all-gather.28
  278.6 21.4 all-gather.26
  303.0 40.1 all-gather.32
  348.0 30.1 reduce-scatter.8
  381.0 22.5 all-gather.30
  412.4 31.4 reduce-scatter.10
  447.7 63.5 reduce-scatter.20
  514.5 62.5 reduce-scatter.22
  593.9 64.8 reduce-scatter.14
  661.2 30.3 reduce-scatter.16
  694.7 31.4 reduce-scatter.12
  729.4 62.0 reduce-scatter.18

commit v2 on v1

--- a/solution.py
+++ b/solution.py
@@ -1,14 +1,611 @@
+import functools
 import math
 
 import jax
 import jax.numpy as jnp
 from jax import lax
+from jax.experimental import pallas as pl
+from jax.experimental.pallas import tpu as pltpu
 from jax.sharding import PartitionSpec as P
 
 HEADS = 16
-
-
+MESH = pl.DeviceIdType.MESH
+f32 = jnp.float32
+bf16 = jnp.bfloat16
 norm_eps = 1e-06
+
+
+def nn(left_side, right_side):
+    return lax.dot_general(left_side, right_side, (((1,), (0,)), ((), ())), preferred_element_type=f32)
+
+
+def nt(left_side, right_side):
+    return lax.dot_general(left_side, right_side, (((1,), (1,)), ((), ())), preferred_element_type=f32)
+
+
+def merged(ref):
+    shape = ref.shape
+    return ref[...].reshape(shape[0] * shape[1], shape[2])
+
+
+def swap_halves(values, lane):
+    up = pltpu.roll(values, 96, 1)
+    down = pltpu.roll(values, 32, 1)
+    return jnp.where(lane % 64 < 32, up, down)
+
+
+def gelu_both(h):
+    c = math.sqrt(2.0 / math.pi)
+    h2 = h * h
+    t = jnp.tanh(c * h * (1.0 + 0.044715 * h2))
+    half = 0.5 * (1.0 + t)
+    return h * half, half + 0.5 * h * (1.0 - t * t) * (c * (1.0 + 3.0 * 0.044715 * h2))
+
+
+def normed(values):
+    mean_val = jnp.mean(values, axis=-1, keepdims=True)
+    centred = values - mean_val
+    rstd = lax.rsqrt(jnp.mean(centred * centred, axis=-1, keepdims=True) + norm_eps)
+    return centred * rstd, rstd
+
+
+def norm_back(e, n, rstd):
+    return (e - jnp.mean(e, axis=-1, keepdims=True) - n * jnp.mean(e * n, axis=-1, keepdims=True)) * rstd
+
+
+class Links:
+    def __init__(self, n, send, recv):
+        self.n = n
+        self.d = lax.axis_index("dp")
+        self.s = lax.axis_index("seq")
+        d, s = self.d, self.s
+        self.px = d + 1 - 2 * (d % 2)
+        self.s1 = s + 1 - 2 * (s % 2)
+        self.s2 = (s + 2) % 4
+        self.s3 = 3 - s
+        self.send, self.recv = send, recv
+        self.n_send = self.n_recv = 0
+
+    def sems(self, sends, recvs):
+        base = (self.n_send, self.n_recv)
+        self.n_send += sends
+        self.n_recv += recvs
+        return base
+
+    def block(self, i):
+        s = self.s
+        return (s % 2 + i % 2) % 2 + 2 * ((s // 2 + i // 2) % 2)
+
+    def copy(self, src, dst, si, ri, dev):
+        return pltpu.make_async_remote_copy(
+            src_ref=src, dst_ref=dst, send_sem=self.send.at[si], recv_sem=self.recv.at[ri],
+            device_id=dev, device_id_type=MESH,
+        )
+
+    def barrier(self):
+        b = pltpu.get_barrier_semaphore()
+        for k in range(1, self.n):
+            pl.semaphore_signal(b, inc=1, device_id=((self.d + k) % self.n, self.s), device_id_type=MESH)
+        for t in (self.s1, self.s2, self.s3):
+            pl.semaphore_signal(b, inc=1, device_id=(self.d, t), device_id_type=MESH)
+        pl.semaphore_wait(b, self.n + 2)
+
+
+class ToAll:
+    def __init__(self, links, src, buf):
+        self.l, self.src, self.buf = links, src, buf
+        self.si, self.ri = links.sems(links.n, links.n)
+
+    def _to(self, k):
+        l = self.l
+        peer = (l.d + k) % l.n
+        return l.copy(self.src(peer), self.buf.at[l.d], self.si + k, self.ri + l.d, (peer, l.s))
+
+    def start(self):
+        for k in range(1, self.l.n):
+            self._to(k).start()
+
+    def wait_recv(self):
+        l = self.l
+        for k in range(1, l.n):
+            peer = (l.d + k) % l.n
+            l.copy(self.buf.at[peer], self.buf.at[peer], self.si + k, self.ri + peer, (peer, l.s)).wait_recv()
+
+    def wait_send(self):
+        for k in range(1, self.l.n):
+            self._to(k).wait_send()
+
+
+class SeqAll:
+    def __init__(self, links, buf):
+        self.l, self.buf = links, buf
+        self.si, self.ri = links.sems(4, 4)
+
+    def _to(self, k):
+        l = self.l
+        t = l.block(k)
+        return l.copy(self.buf.at[l.s], self.buf.at[l.s], self.si + k, self.ri + l.s, (l.d, t))
+
+    def start(self):
+        for k in (2, 3, 1):
+            self._to(k).start()
+
+    def wait_recv(self):
+        l = self.l
+        for k in (1, 2, 3):
+            t = l.block(k)
+            l.copy(self.buf.at[t], self.buf.at[t], self.si + k, self.ri + t, (l.d, t)).wait_recv()
+
+    def wait_send(self):
+        for k in (1, 2, 3):
+            self._to(k).wait_send()
+
+
+class DpGather:
+    def __init__(self, links, buf):
+        self.l, self.buf = links, buf
+        self.si, self.ri = links.sems(links.n, links.n)
+        self.half = links.n // 2
+
+    def _z(self, k):
+        l = self.l
+        return l.copy(self.buf.at[l.d], self.buf.at[l.d], self.si + k, self.ri + l.d, ((l.d + 2 * k) % l.n, l.s))
+
+    def _x(self, k):
+        l = self.l
+        r = (l.d + 2 * k) % l.n
+        return l.copy(self.buf.at[r], self.buf.at[r], self.si + self.half + k, self.ri + r, (l.px, l.s))
+
+    def start(self):
+        for k in range(1, self.half):
+            self._z(k).start()
+        self._x(0).start()
+
+    def hand_on(self):
+        l = self.l
+        for k in range(1, self.half):
+            r = (l.d + 2 * k) % l.n
+            l.copy(self.buf.at[r], self.buf.at[r], self.si, self.ri + r, (r, l.s)).wait_recv()
+            self._x(k).start()
+
+    def wait_rest(self):
+        l = self.l
+        for k in range(self.half):
+            r = (l.px + 2 * k) % l.n
+            l.copy(self.buf.at[r], self.buf.at[r], self.si, self.ri + r, (l.px, l.s)).wait_recv()
+
+    def wait_send(self):
+        for k in range(1, self.half):
+            self._z(k).wait_send()
+        for k in range(self.half):
+            self._x(k).wait_send()
+
+
+class SeqGather:
+    def __init__(self, links, buf):
+        self.l, self.buf = links, buf
+        self.si, self.ri = links.sems(3, 4)
+
+    def _c(self, slot, k, t):
+        l = self.l
+        return l.copy(self.buf.at[slot], self.buf.at[slot], self.si + k, self.ri + slot, (l.d, t))
+
+    def start(self):
+        l = self.l
+        self._c(l.s, 0, l.s2).start()
+        self._c(l.s, 1, l.s1).start()
+
+    def hand_on(self):
+        l = self.l
+        self.wait(l.s2)
+        self._c(l.s2, 2, l.s1).start()
+
+    def wait(self, slot):
+        l = self.l
+        l.copy(self.buf.at[slot], self.buf.at[slot], self.si, self.ri + slot, (l.d, l.s1)).wait_recv()
+
+    def wait_send(self):
+        l = self.l
+        self._c(l.s, 0, l.s2).wait_send()
+        self._c(l.s, 1, l.s1).wait_send()
+        self._c(l.s2, 2, l.s1).wait_send()
+
+
+class SeqSwap:
+    def __init__(self, links, out, into):
+        self.l, self.out, self.into = links, out, into
+        self.si, self.ri = links.sems(4, 4)
+
+    def copy_to(self, i):
+        l = self.l
+        t = l.block(i)
+        return l.copy(self.out.at[t], self.into.at[l.s], self.si + i, self.ri + l.s, (l.d, t))
+
+    def wait_recv(self):
+        l = self.l
+        for i in (1, 2, 3):
+            t = l.block(i)
+            l.copy(self.into.at[t], self.into.at[t], self.si + i, self.ri + t, (l.d, t)).wait_recv()
+
+    def wait_send(self):
+        for i in (1, 2, 3):
+            self.copy_to(i).wait_send()
+
+
+class SeqSum:
+    def __init__(self, links, held):
+        self.l, self.held = links, held
+        self.si, self.ri = links.sems(3, 3)
+
+    def _c(self, k, t):
+        l = self.l
+        return l.copy(self.held.at[k], self.held.at[3 + k], self.si + k, self.ri + k, (l.d, t))
+
+    def far(self, term):
+        l, held = self.l, self.held
+        held[0] = term(l.s3).astype(bf16)
+        self._c(0, l.s1).start()
+        mine = term(l.s2)
+        self._c(0, l.s1).wait_recv()
+        held[1] = (mine + held[3].astype(f32)).astype(bf16)
+        self._c(1, l.s2).start()
+
+    def near(self, term):
+        l = self.l
+        self.held[2] = term(l.s1).astype(bf16)
+        self._c(2, l.s1).start()
+
+    def total(self, mine):
+        l, held = self.l, self.held
+        self._c(2, l.s1).wait_recv()
+        self._c(1, l.s2).wait_recv()
+        return mine + held[5].astype(f32) + held[4].astype(f32)
+
+    def wait_send(self):
+        l = self.l
+        self._c(0, l.s1).wait_send()
+        self._c(1, l.s2).wait_send()
+        self._c(2, l.s1).wait_send()
+
+
+def kernel_a(
+    n,
+    frames, cot, tcols, bm, bias, wu_own, cos, sin, idr, idc, wm_hbm, wq_hbm, wo_hbm, wd_hbm,
+    xa, q, k, v, kt, vt, lse, ao, gh, dffn, gelu, xf, dhid, wq, wd, dmid, xmid, dattn, mod, fsum, bd_full,
+    wm, wu, wo, tbuf, psend, pbuf, bbuf, n_in, attn_branch, n_mid, ao_out, do_out, held,
+    send, recv, local,
+):
+    l = Links(n, send, recv)
+    d, s = l.d, l.s
+    rows, width = frames.shape
+    quarter = width // 4
+    own_rows = tcols.shape[2]
+    mq = bm.shape[1]
+    units = wd.shape[1]
+    ff_q = wu.shape[2]
+    lane = lax.broadcasted_iota(jnp.int32, (rows, 128), 1)
+    take = [
+        pltpu.make_async_copy(wm_hbm.at[:, pl.ds(pl.multiple_of(s * mq, 128), mq)], wm, local.at[0]),
+        pltpu.make_async_copy(wd_hbm.at[pl.ds(pl.multiple_of(s * units, 8), units), :], wd.at[d], local.at[1]),
+        pltpu.make_async_copy(wo_hbm.at[:, pl.ds(pl.multiple_of(s * quarter, 128), quarter)], wo.at[s, d], local.at[2]),
+    ] + [
+        pltpu.make_async_copy(
+            wq_hbm.at[:, pl.ds(pl.multiple_of(j * width + s * quarter, 128), quarter)],
+            wq.at[d, :, pl.ds(j * quarter, quarter)], local.at[3 + j],
+        )
+        for j in range(3)
+    ]
+    for c in take:
+        c.start()
+    times = ToAll(l, lambda peer: tcols.at[peer], tbuf)
+    parts = ToAll(l, lambda peer: psend.at[peer], pbuf)
+    biases = ToAll(l, lambda peer: bias.at[0], bbuf)
+    mods = SeqAll(l, mod)
+    g_wq, g_wu, g_wd = DpGather(l, wq), DpGather(l, wu), DpGather(l, wd)
+    g_wo = DpGather(l, wo.at[s])
+    s_xa, s_df, s_xf, s_wo = SeqGather(l, xa), SeqGather(l, dffn), SeqGather(l, xf), SeqGather(l, wo)
+    w_ao, w_do = SeqSwap(l, ao_out, ao), SeqSwap(l, do_out, gh)
+    sums = SeqSum(l, held)
+    l.barrier()
+    times.start()
+    for c in take[3:]:
+        c.wait()
+    g_wq.start()
+    biases.start()
+    tbuf[d] = tcols[d]
+    wu[d] = wu_own[...]
+    for c in take[:3]:
+        c.wait()
+    n_in[...] = normed(frames[...])[0]
+    times.wait_recv()
+    lhs = jnp.concatenate([tbuf[i] for i in range(n)], axis=0).astype(bf16)
+    part = nn(lhs, wm[...]) + bm[...]
+    for i in range(n):
+        psend[i] = part[i : i + 1]
+    parts.start()
+    total = psend[d]
+    parts.wait_recv()
+    for j in range(1, n):
+        total = total + pbuf[(d + j) % n]
+    mod[s] = total
+    mods.start()
+    mods.wait_recv()
+    flat = jnp.concatenate([mod[i] for i in range(4)], axis=1)
+    shift_a, scale_a, gate_a, shift_f, scale_f, gate_f = (
+        flat[:, i * width : (i + 1) * width] for i in range(6)
+    )
+    xa[s] = (n_in[...] * (1.0 + scale_a) + shift_a).astype(bf16)
+    s_xa.start()
+    dffn[s] = (gate_f * cot[...]).astype(bf16)
+    g_wq.hand_on()
+    g_wd.start()
+    g_wu.start()
+    g_wo.start()
+    g_wq.wait_rest()
+    biases.wait_recv()
+    own_bias = bias[0]
+    for j in range(1, n):
+        own_bias = own_bias + bbuf[(d + j) % n]
+    qw = 3 * quarter
+    bq = own_bias[:, :qw]
+    bo = own_bias[:, qw : qw + width]
+    bu = own_bias[:, qw + width : qw + width + ff_q]
+    bd_full[...] = own_bias[:, qw + width + ff_q :]
+
+    def project(i, carry):
+        @pl.when(i == 1)
+        def _():
+            s_xa.wait(l.s1)
+
+        @pl.when(i == 2)
+        def _():
+            s_xa.hand_on()
+            s_df.start()
+
+        @pl.when(i == 3)
+        def _():
+            s_xa.wait(l.s3)
+
+        b = l.block(i)
+        at = pl.ds(pl.multiple_of(b * rows, rows), rows)
+        pr = nn(xa[b], merged(wq)) + bq
+        cb, sb = cos[at, :], sin[at, :]
+        for p in range(quarter // 128):
+            c0 = 128 * p
+            qp = pr[:, c0 : c0 + 128]
+            kp = pr[:, quarter + c0 : quarter + c0 + 128]
+            vp = pr[:, 2 * quarter + c0 : 2 * quarter + c0 + 128].astype(bf16)
+            qp = (qp * cb + swap_halves(qp, lane) * sb).astype(bf16)
+            kp = (kp * cb + swap_halves(kp, lane) * sb).astype(bf16)
+            q[at, c0 : c0 + 128] = qp * jnp.bfloat16(0.125)
+            k[at, c0 : c0 + 128] = kp
+            v[at, c0 : c0 + 128] = vp
+            kt[p, :, at] = jnp.transpose(kp.astype(f32)).astype(bf16)
+            vt[p, :, at] = jnp.transpose(vp.astype(f32)).astype(bf16)
+        return carry
+
+    lax.fori_loop(0, 4, project, 0)
+    g_wd.hand_on()
+    g_wu.hand_on()
+
+    def attend(j, carry):
+        i = (j + 2) % 4
+        b = l.block(i)
+        at = pl.ds(pl.multiple_of(b * rows, rows), rows)
+        same = idc[...] == idr[:, at]
+        for p in range(quarter // 128):
+            qp, kp = q[at, 128 * p : 128 * p + 128], k[:, 128 * p : 128 * p + 128]
+            outs = []
+            for h in range(2):
+                qm = jnp.where((lane < 64) == (h == 0), qp, jnp.zeros_like(qp))
+                sc = jnp.where(same, nt(kp, qm), -1e30)
+                top = jnp.max(sc, axis=0, keepdims=True)
+                ex = jnp.exp(sc - top)
+                su = jnp.sum(ex, axis=0, keepdims=True)
+                lse[2 * p + h, :, at] = top + jnp.log(su)
+                pt = (ex * (1.0 / su)).astype(bf16)
+                outs.append(nn(vt[p, 64 * h : 64 * h + 64, :], pt))
+            ao_out[b, :, 128 * p : 128 * p + 128] = jnp.transpose(jnp.concatenate(outs, axis=0)).astype(bf16)
+
+        @pl.when(j != 2)
+        def _():
+            w_ao.copy_to(i).start()
+
+        @pl.when(j == 2)
+        def _():
+            ao[s] = ao_out[s]
+
+        @pl.when(j == 0)
+        def _():
+            g_wo.hand_on()
+            s_df.hand_on()
+
+        @pl.when(j == 1)
+        def _():
+            g_wo.wait_rest()
+            s_wo.start()
+
+        @pl.when(j == 3)
+        def _():
+            s_wo.hand_on()
+
+        return carry
+
+    lax.fori_loop(0, 4, attend, 0)
+    s_wo.wait(l.s1)
+    s_wo.wait(l.s3)
+    w_ao.wait_recv()
+    left = jnp.concatenate([ao[i] for i in range(4)], axis=1)
+    for c in range(4):
+        cs = slice(c * quarter, (c + 1) * quarter)
+        attn_branch[:, cs] = nn(left, merged(wo.at[c])) + bo[:, cs]
+    xm = frames[...] + gate_a * attn_branch[...]
+    xmid[...] = xm
+    nm, rstd = normed(xm)
+    n_mid[...] = nm
+    xf[s] = (nm * (1.0 + scale_f) + shift_f).astype(bf16)
+    s_xf.start()
+    s_df.wait(l.s1)
+    s_df.wait(l.s3)
+    g_wd.wait_rest()
+    g_wu.wait_rest()
+
+    def term(b):
+        at = pl.ds(pl.multiple_of(b * rows, rows), rows)
+        return nt(dhid[at, :], merged(wu))
+
+    def feed(i, carry):
+        @pl.when(i == 1)
+        def _():
+            s_xf.wait(l.s1)
+
+        @pl.when(i == 2)
+        def _():
+            sums.near(term)
+            s_xf.hand_on()
+
+        @pl.when(i == 3)
+        def _():
+            s_xf.wait(l.s3)
+
+        b = l.block(i)
+        at = pl.ds(pl.multiple_of(b * rows, rows), rows)
+        act, slope = gelu_both(nn(xf[b], merged(wu)) + bu)
+        gelu[at, :] = act.astype(bf16)
+        dhid[at, :] = (nt(dffn[b], merged(wd)) * slope).astype(bf16)
+        return carry
+
+    lax.fori_loop(0, 4, feed, 0)
+    sums.far(term)
+    g = sums.total(term(s))
+    nm = n_mid[...]
+    fsum[0:1, :] = jnp.sum(g, axis=0, keepdims=True)
+    fsum[1:2, :] = jnp.sum(g * nm, axis=0, keepdims=True)
+    dm = cot[...] + norm_back(g * (1.0 + scale_f), nm, rstd)
+    dmid[...] = dm
+    da = (gate_a * dm).astype(bf16)
+    dattn[...] = da
+    fsum[2:3, :] = jnp.sum(dm * attn_branch[...], axis=0, keepdims=True)
+    fsum[3:4, :] = jnp.sum(da.astype(f32), axis=0, keepdims=True)
+    per = n // 4
+
+    def give(j, carry):
+        i = (j + 2) % 4
+        t = l.block(i)
+        out = None
+        for c in range(4):
+            wt = wo[c, pl.ds(t * per, per)].reshape(quarter, quarter)
+            o = nt(dattn[:, c * quarter : (c + 1) * quarter], wt)
+            out = o if out is None else out + o
+        do_out[t] = out.astype(bf16)
+
+        @pl.when(j != 2)
+        def _():
+            w_do.copy_to(i).start()
+
+        @pl.when(j == 2)
+        def _():
+            gh[s] = do_out[s]
+
+        return carry
+
+    lax.fori_loop(0, 4, give, 0)
+    w_do.wait_recv()
+    for c in (times, parts, biases, mods, g_wq, g_wu, g_wd, g_wo, s_xa, s_df, s_xf, s_wo, w_ao, w_do, sums):
+        c.wait_send()
+
+
+def run_a(n, frames, cot, tcols, bm, bias, wu_own, cos, sin, idr, idc, w_mod, w_qkv, w_out, w_down):
+    rows, width = frames.shape
+    item = 4 * rows
+    quarter = width // 4
+    ff = w_down.shape[0] * n
+    ff_q = ff // 4
+    own_rows = width // n
+    units = ff_q // n
+    heads = quarter // 64
+    pairs = quarter // 128
+    S = jax.ShapeDtypeStruct
+    outs = [
+        S((4, rows, width), bf16), S((item, quarter), bf16), S((item, quarter), bf16), S((item, quarter), bf16),
+        S((pairs, 128, item), bf16), S((pairs, 128, item), bf16), S((heads, 1, item), f32),
+        S((4, rows, quarter), bf16), S((4, rows, quarter), bf16), S((4, rows, width), bf16), S((item, ff_q), bf16),
+        S((4, rows, width), bf16), S((item, ff_q), bf16), S((n, own_rows, 3 * quarter), bf16), S((n, units, width), bf16),
+        S((rows, width), f32), S((rows, width), f32), S((rows, width), bf16), S((4, 1, 6 * quarter), f32),
+        S((8, width), f32), S((1, width), f32),
+    ]
+    V = pltpu.VMEM
+    scratch = [
+        V((own_rows, 6 * quarter), bf16), V((n, own_rows, ff_q), bf16), V((4, n, own_rows, quarter), bf16),
+        V((n, 1, own_rows), f32), V((n, 1, 6 * quarter), f32), V((n, 1, 6 * quarter), f32), V((n, 1, bias.shape[2]), f32),
+        V((rows, width), f32), V((rows, width), f32), V((rows, width), f32), V((4, rows, quarter), bf16),
+        V((4, rows, quarter), bf16), V((6, rows, width), bf16),
+        pltpu.SemaphoreType.DMA((7 * n + 40,)), pltpu.SemaphoreType.DMA((7 * n + 40,)), pltpu.SemaphoreType.DMA((6,)),
+    ]
+    vm = pl.BlockSpec(memory_space=pltpu.VMEM)
+    hb = pl.BlockSpec(memory_space=pl.ANY)
+    return pl.pallas_call(
+        functools.partial(kernel_a, n),
+        out_shape=outs,
+        in_specs=[vm] * 10 + [hb] * 4,
+        out_specs=[vm] * len(outs),
+        scratch_shapes=scratch,
+        compiler_params=pltpu.CompilerParams(collective_id=0, has_side_effects=True, vmem_limit_bytes=60 << 20),
+    )(frames, cot, tcols, bm, bias, wu_own, cos, sin, idr, idc, w_mod, w_qkv, w_out, w_down)
+
+
+def clip_layout(lengths, length):
+    clips = lengths.shape[0]
+    earlier = jnp.arange(clips)[None, :] <= jnp.arange(clips)[:, None]
+    clip_end = jnp.sum(jnp.where(earlier, lengths[None, :], 0), axis=1)
+    clip_start = clip_end - lengths
+    item_frames = jnp.arange(length, dtype=jnp.int32)
+    inside = (item_frames[:, None] >= clip_start[None, :]) & (
+        item_frames[:, None] < clip_end[None, :]
+    )
+    clip_ids = jnp.sum(
+        jnp.where(inside, jnp.arange(clips, dtype=jnp.int32)[None, :], 0), axis=1
+    )
+    positions = item_frames - jnp.sum(jnp.where(inside, clip_start[None, :], 0), axis=1)
+    return (clip_ids, positions)
+
+
+def tables(positions):
+    lanes = jnp.arange(128)
+    inv_rate = jnp.exp((lanes % 32).astype(f32) * (-2.0 * math.log(10000.0) / 64))
+    phases = positions.astype(f32)[:, None] * inv_rate[None, :]
+    sign = jnp.where(lanes % 64 < 32, -1.0, 1.0)
+    return jnp.cos(phases), jnp.sin(phases) * sign[None, :]
+
+
+def prepare(seq_rank, dp_rank, n, frames, time_embed, clip_len, b_qkv, b_out, w_up, b_up, b_down, b_mod):
+    rows, width = frames.shape
+    quarter = width // 4
+    own_rows, ff = w_up.shape
+    units = ff // 4 // n
+    clip_ids, positions = clip_layout(clip_len[0], 4 * rows)
+    cos, sin = tables(positions)
+    tcols = jax.nn.silu(time_embed).astype(bf16).astype(f32).reshape(n, 1, own_rows)
+
+    def placed(b):
+        return lax.dynamic_update_slice(
+            jnp.zeros((b.shape[0] * n,), f32), b.astype(f32), (dp_rank * b.shape[0],)
+        )
+
+    def own(value, axis):
+        return lax.dynamic_index_in_dim(value, seq_rank, axis, keepdims=False)
+
+    bm = own(placed(b_mod).reshape(4, 6 * quarter), 0)[None]
+    bias = jnp.concatenate(
+        [
+            own(placed(b_qkv).reshape(3, 4, quarter), 1).reshape(-1),
+            placed(b_out),
+            own(placed(b_up).reshape(n, 4, units), 1).reshape(-1),
+            placed(b_down),
+        ]
+    ).reshape(1, 1, -1)
+    wu_own = own(w_up.reshape(own_rows, n, 4, units), 2).reshape(own_rows, ff // 4)
+    return tcols, bm, bias, wu_own, cos, sin, clip_ids[None, :], clip_ids[:, None]
 
 
 def layer_norm(values):
@@ -35,15 +632,6 @@
     )
 
 
-def angles(positions, head_dim):
-    half_dim = head_dim // 2
-    inv_rate = jnp.exp(
-        jnp.arange(half_dim, dtype=jnp.float32) * (-2.0 * math.log(10000.0) / head_dim)
-    )
-    phases = positions.astype(jnp.float32)[:, None] * inv_rate[None, :]
-    return (jnp.cos(phases)[:, None, :], jnp.sin(phases)[:, None, :])
-
-
 def across_rows(left_side, right_side):
     return lax.dot_general(
         left_side, right_side, (((0,), (0,)), ((), ())), preferred_element_type=jnp.float32
@@ -80,22 +668,6 @@
 
 def dp_reduce(value):
     return lax.psum_scatter(value.astype(jnp.bfloat16), "dp", scatter_dimension=0, tiled=True)
-
-
-def clip_layout(lengths, length):
-    clips = lengths.shape[0]
-    earlier = jnp.arange(clips)[None, :] <= jnp.arange(clips)[:, None]
-    clip_end = jnp.sum(jnp.where(earlier, lengths[None, :], 0), axis=1)
-    clip_start = clip_end - lengths
-    item_frames = jnp.arange(length, dtype=jnp.int32)
-    inside = (item_frames[:, None] >= clip_start[None, :]) & (
-        item_frames[:, None] < clip_end[None, :]
-    )
-    clip_ids = jnp.sum(
-        jnp.where(inside, jnp.arange(clips, dtype=jnp.int32)[None, :], 0), axis=1
-    )
-    positions = item_frames - jnp.sum(jnp.where(inside, clip_start[None, :], 0), axis=1)
-    return (clip_ids, positions)
 
 
 def per_device(
@@ -132,55 +704,47 @@
     units_each = w_down.shape[0] // seq_count
     units_here = ff_width // seq_count
 
-    def own_part(value, axis):
-        return lax.dynamic_index_in_dim(value, seq_rank, axis, keepdims=False)
-
-    wq_part = own_part(w_qkv.reshape(own_rows, 3, seq_count, local_width), 2).reshape(
-        own_rows, 3 * local_width
-    )
-    wu_part = own_part(w_up.reshape(own_rows, dp_count, seq_count, units_each), 2).reshape(
-        own_rows, units_here
-    )
-    wd_part = own_part(w_down.reshape(seq_count, units_each, model_width), 0)
-    wq_here = dp_gather(wq_part)
-    wo_full = dp_gather(w_out)
-    wu_here = dp_gather(wu_part)
-    wd_here = dp_gather(wd_part)
+    pre = prepare(
+        seq_rank, dp_rank, dp_count, frames, time_embed, clip_len, b_qkv, b_out, w_up, b_up, b_down, b_mod
+    )
+    outs = run_a(dp_count, frames, cotangent, *pre, w_mod, w_qkv, w_out, w_down)
+    x_a, q8, k, v, _, _, lse, attn_out, grad_heads, d_ffn_item, gelu_act, x_f, d_hidden, wq, wd = outs[:15]
+    d_mid, x_mid, d_attn, mod, fsum, bd_full = outs[15:]
+    tcols, _, _, _, cos, sin, clip_ids = pre[:7]
+    clip_ids = clip_ids[0]
+    cosine_tab, sine_tab = cos[:, None, :32], -sin[:, None, :32]
     sizes = [b_qkv.shape[0], b_out.shape[0], b_up.shape[0], b_down.shape[0]]
-    biases = lax.all_gather(jnp.concatenate([b_qkv, b_out, b_up, b_down]), "dp", axis=0)
     cuts = [sizes[0], sizes[0] + sizes[1], sizes[0] + sizes[1] + sizes[2]]
-    bq_all, bo_all, bu_all, bd_all = (
-        b.astype(jnp.float32) for b in jnp.split(biases, cuts, axis=1)
-    )
-    bq_here = own_part(bq_all.reshape(3, seq_count, local_width), 1).reshape(3 * local_width)
-    bo_full = bo_all.reshape(model_width)
-    bu_here = own_part(bu_all.reshape(dp_count, seq_count, units_each), 1).reshape(units_here)
-    bd_full = bd_all.reshape(model_width)
-
-    clip_ids, positions = clip_layout(clip_len[0], length)
-    cosine_tab, sine_tab = angles(positions, head_dim)
-
-    time_act = jax.nn.silu(time_embed).astype(jnp.bfloat16)
-    time_all = dp_gather(time_act)
+    time_all = dp_gather(jax.nn.silu(time_embed).astype(jnp.bfloat16))
     time_cols = lax.dynamic_slice_in_dim(time_all, dp_rank * own_rows, own_rows, 1)
-    bias_cols = lax.dynamic_update_slice(
-        jnp.zeros((6 * model_width,), jnp.float32),
-        b_mod.astype(jnp.float32),
-        (dp_rank * b_mod.shape[0],),
-    )
-    modulation = lax.psum_scatter(
-        forward_dot(time_cols, w_mod) + bias_cols, "dp", scatter_dimension=0, tiled=True
-    )
-    shift_a, scale_a, gate_a, shift_f, scale_f, gate_f = jnp.split(modulation, 6, axis=1)
-
-    d_ffn = (gate_f * cotangent).astype(jnp.bfloat16)
-    d_ffn_item = seq_gather(d_ffn)
-    x_a = seq_gather(modulate(frames, shift_a, scale_a).astype(jnp.bfloat16))
-    projected = forward_dot(x_a, wq_here) + bq_here
-    pieces = projected.reshape(length, 3, heads_here, head_dim)
-    query_heads = rotate(pieces[:, 0], cosine_tab, sine_tab).astype(jnp.bfloat16)
-    keys_heads = rotate(pieces[:, 1], cosine_tab, sine_tab).astype(jnp.bfloat16)
-    values_heads = pieces[:, 2].astype(jnp.bfloat16)
+    x_a = x_a.reshape(length, model_width)
+    x_f = x_f.reshape(length, model_width)
+    d_ffn_item = d_ffn_item.reshape(length, model_width)
+    wq_here = wq.reshape(model_width, -1)
+    wd_here = wd.reshape(units_here, model_width)
+    query_heads = (q8 * jnp.bfloat16(8)).reshape(length, heads_here, head_dim)
+    keys_heads = k.reshape(length, heads_here, head_dim)
+    values_heads = v.reshape(length, heads_here, head_dim)
+    attn_out = attn_out.transpose(1, 0, 2).reshape(frame_rows, model_width)
+    grad_heads = grad_heads.reshape(length, heads_here, head_dim)
+    log_totals = (
+        lse.reshape(heads_here, block_count, block_rows).transpose(1, 0, 2)[:, :, :, None]
+    )
+    shift_a, scale_a, gate_a, shift_f, scale_f, gate_f = jnp.split(
+        mod.reshape(1, 6 * model_width), 6, axis=1
+    )
+    d_shift_f, d_scale_f, d_gate_a, g_bo = fsum[0:1], fsum[1:2], fsum[2:3], fsum[3]
+    ffn_branch = seq_reduce(forward_dot(gelu_act, wd_here)) + bd_full
+    block_out = x_mid + gate_f * ffn_branch
+    d_gate_f = jnp.sum(cotangent * ffn_branch, axis=0, keepdims=True)
+    g_wd = across_rows(gelu_act, d_ffn_item)
+    g_bd = column_sums(d_ffn_item)
+    g_wu = across_rows(x_f, d_hidden)
+    g_bu = column_sums(d_hidden)
+    g_wo_run = across_rows(attn_out, d_attn)
+    g_wo = lax.psum_scatter(
+        g_wo_run.astype(jnp.bfloat16), "seq", scatter_dimension=1, tiled=True
+    )
 
     def block_scores(block_index):
         first_row = block_index * block_rows
@@ -192,51 +756,6 @@
             * factor
         )
         return (query_blk, same_clip, jnp.where(same_clip, raw_scores, -1e30))
-
-    def attend(block_index):
-        query_blk, same_clip, masked = block_scores(block_index)
-        row_max = jnp.max(masked, axis=-1, keepdims=True)
-        exp_scores = jnp.exp(masked - row_max)
-        row_sum = jnp.sum(exp_scores, axis=-1, keepdims=True)
-        attn_prob = (exp_scores / row_sum).astype(jnp.bfloat16)
-        mixed_rows = jnp.einsum(
-            "hqk,khe->qhe", attn_prob, values_heads, preferred_element_type=jnp.float32
-        )
-        return (mixed_rows.astype(jnp.bfloat16), row_max + jnp.log(row_sum))
-
-    attn_blocks, log_totals = lax.map(attend, jnp.arange(block_count))
-    attn_heads = attn_blocks.reshape(length, local_width)
-    attn_out = lax.all_to_all(attn_heads, "seq", split_axis=0, concat_axis=1, tiled=True)
-    attn_branch = forward_dot(attn_out, wo_full) + bo_full
-    x_mid = frames + gate_a * attn_branch
-    x_f = seq_gather(modulate(x_mid, shift_f, scale_f).astype(jnp.bfloat16))
-    hidden = forward_dot(x_f, wu_here) + bu_here
-    gelu_act, gelu_pull = jax.vjp(lambda inner: jax.nn.gelu(inner, approximate=True), hidden)
-    gelu_act = gelu_act.astype(jnp.bfloat16)
-    ffn_branch = seq_reduce(forward_dot(gelu_act, wd_here)) + bd_full
-    block_out = x_mid + gate_f * ffn_branch
-    d_gate_f = jnp.sum(cotangent * ffn_branch, axis=0, keepdims=True)
-    d_gelu = against(d_ffn_item, wd_here)
-    d_hidden = gelu_pull(d_gelu)[0].astype(jnp.bfloat16)
-    d_xf = seq_reduce(against(d_hidden, wu_here))
-    g_wd = across_rows(gelu_act, d_ffn_item)
-    g_bd = column_sums(d_ffn_item)
-    g_wu = across_rows(x_f, d_hidden)
-    g_bu = column_sums(d_hidden)
-    mid_pull = jax.vjp(modulate, x_mid, shift_f, scale_f)[1]
-    d_mid_part, d_shift_f, d_scale_f = mid_pull(d_xf)
-    d_mid = cotangent + d_mid_part
-    d_attn = (gate_a * d_mid).astype(jnp.bfloat16)
-    d_gate_a = jnp.sum(d_mid * attn_branch, axis=0, keepdims=True)
-    g_wo_run = across_rows(attn_out, d_attn)
-    g_wo = lax.psum_scatter(
-        g_wo_run.astype(jnp.bfloat16), "seq", scatter_dimension=1, tiled=True
-    )
-    g_bo = column_sums(d_attn)
-    d_out = against(d_attn, wo_full).astype(jnp.bfloat16)
-    grad_heads = lax.all_to_all(d_out, "seq", split_axis=1, concat_axis=0, tiled=True).reshape(
-        length, heads_here, head_dim
-    )
 
     def attend_back(running, inputs):
         grad_keys, grad_values = running

time: 847 us -> 572 us (0.68)
  waiting for transfers between devices: 362 us -> 70.5 us
  Pallas kernels: 0 us -> 138 us
  matrix products: 170 us -> 128 us
  blocking collectives: 183 us -> 150 us
  local copies, waits for them, and re-layouts: 55.6 us -> 24.2 us
    all_gather x7 -> x0, waiting for transfers between devices: 162 us -> none  [the longest x4 92.9 us: dp_gather(): return lax.all_gather(value, 'dp', axis=0, tiled=True)]
    pallas_call x0 -> x1, Pallas kernels: none -> 138 us  [run_a(): pl.pallas_call(functools.partial(kernel_a, n), out_shape=outs, in_specs=[...]
    unnamed x17 -> x7, waiting for transfers between devices: 66.8 us -> 0.75 us
    reduce_scatter x3 -> x2, waiting for transfers between devices: 92.1 us -> 49 us  [seq_reduce(): lax.psum_scatter(value.astype(jnp.bfloat16), 'seq', scatter_dimension=0,...]
    all_gather x1 -> x0, blocking collectives: 30.6 us -> none  [per_device(): lax.all_gather(jnp.concatenate([b_qkv, b_out, b_up, b_down]), 'dp', axis=0)]
    reduce_scatter x1, waiting for transfers between devices: 14.6 us -> 0.02 us  [per_device(): lax.psum_scatter(g_wo_run.astype(jnp.bfloat16), 'seq', scatter_dimension=...]
    dot_general x5 -> x1, matrix products: 17.5 us -> 3.86 us  [forward_dot(): return jnp.dot(left_side, right_side, preferred_element_type=jnp.float32)]
    reduce_sum x6 -> x1, other arithmetic: 9.16 us -> 0.1 us  [clip_layout(): jnp.sum(jnp.where(inside, jnp.arange(clips, dtype=jnp.int32)[None, :], 0)...]
  transfers between devices with their start and end apart: 19 -> 8, of which waited for: 14 -> 3; matrix products, arithmetic and copies ran while one was open for 27% -> 28% of each run, Pallas kernels for 0% -> 0%
where the time goes in v2:
time: 572 us; the launch traced here: 562 us
  blocking collectives  150 us (26%)
  Pallas kernels  138 us (24%)
  matrix products  128 us (22%)
  waiting for transfers between devices  70.5 us (12%)
  other arithmetic  29.6 us (5%)
  local copies, waits for them, and re-layouts  24.2 us (4%)
  between operations  15.1 us (3%)
  starting transfers between devices  5.93 us (1%)
    pallas_call x1, Pallas kernels, run_a(): pl.pallas_call(functools.partial(kernel_a, n), out_shape=outs, in_specs=[...  138 us
    all_gather x2, blocking collectives, dp_gather(): return lax.all_gather(value, 'dp', axis=0, tiled=True)  61.4 us
    reduce_scatter x2, waiting for transfers between devices, seq_reduce(): lax.psum_scatter(value.astype(jnp.bfloat16), 'seq', scatter_dimension=0,...  49 us
    dot_general x2, matrix products, attend_back(): jnp.einsum('hqk,qhe->khe', d_scores, query_blk, preferred_element_type=jn...  46.5 us
    unnamed x1, blocking collectives  37.6 us
    dot_general x2, matrix products, attend_back(): jnp.einsum('hqk,khe->qhe', d_scores, keys_heads, preferred_element_type=j...  36.1 us
    all_gather x4, blocking collectives, spread(): return lax.all_gather(dp_reduce(value), 'seq', axis=0).astype(jnp.float32)  30.1 us
    reduce_scatter x4, waiting for transfers between devices, dp_reduce(): lax.psum_scatter(value.astype(jnp.bfloat16), 'dp', scatter_dimension=0, t...  20.8 us
  transfers between devices with their start and end apart: 8, of which 3 were waited for; matrix products, arithmetic and copies ran while one was open for 28% of the time, Pallas kernels for 0%

profile of v2, /device:TPU:0, one launch (start us, length us, event | category | flops | bytes accessed | tf_op | source)
XLA Modules:
  0.0 562.2 jit_solution(8934862728744838208)
XLA Ops:
  7.2 0.8 select_reduce_fusion.2
  8.8 0.8 convert_dynamic-update-slice_fusion.2
  10.5 1.3 bitcast_convert_fusion.tcols
  12.6 0.8 convert_dynamic-update-slice_fusion.3
  14.7 0.8 convert_dynamic-update-slice_fusion
  16.1 1.0 copy.100.idc
  17.1 1.3 copy.98
  18.5 0.8 copy.99.wu_own
  19.2 3.0 fusion.85
  22.3 137.9 %shard_map.237 = (bf16[4,256,1024]{2,1,0:T(8,128)(2,1)}, bf16[1024,256]{1,0:T(8,128)(2,1)}, bf16[1024,256]{1,0:T(8,128)(2,1)}, bf16[1024,256]{1,0:T(8,128)(2,1)}...) custom-call(f32[256,1024]{1,0:T(8,128)} %frames.1, ...), custom_call_target="tpu_custom_call" | custom-call | tf_op jit(solution)/shard_map/pallas_call | solution.py:547
  160.2 4.3 convolution_convert_fusion.5
  164.6 2.2 convolution_convert_fusion.4
  167.1 1.1 broadcast_multiply_fusion
  168.4 1.2 copy.102
  170.7 106.5 %while.15 = (s32[]{:T(128)}, f32[1024,4,64]{0,2,1:T(8,128)}, f32[1024,4,64]{0,2,1:T(8,128)}, bf16[2,512,4,64]{1,3,2,0:T(8,128)(2,1)}, s32[2]{0:T(128)S(1)}, /*in...) while((s32[]{:T(128)}, f32[1024,4,64]{0,2,1:T(8,128)}, ...), condition=%wide.region_6.7_spmd.clone, body=%wide.region_4.6_spmd.clone.sunk | while | flops 1398806528 | bytes 136120592 | solution.py:787
  172.4 1.3 fusion.142
  173.7 3.7 fusion.144
  177.4 4.5 fusion.141
  181.9 18.1 %fusion.145 = bf16[2,512,4,64]{1,3,2,0:T(8,128)(2,1)} fusion(bf16[2,512,4,64]{1,3,2,0:T(8,128)(2,1)} %get-tuple-element.346, s32[]{:T(128)S(6)} %copy.145, bf16[1024,4,64]{0,2,1:T(8,128)(2,1)S(1)} %get-tuple-element.365, f32[4,512,1024]{2,1,0:T(8,128)} %fusion.141, f32[4,512,1024]{2,1,0:T(8,128)} %copy-done, ...), kind=kOutput, calls=%fused_computation.28.clone.1 | convolution fusion | flops 291769344 | bytes 35405828 | tf_op jit(solution)/shard_map/while/body/eval_jaxpr/hqk,khe->qhe/dot_general | solution.py:773
  200.0 23.2 %fusion.143 = f32[1024,4,64]{0,2,1:T(8,128)} fusion(f32[4,512,1024]{2,1,0:T(8,128)} %fusion.141, f32[4,512,1024]{2,1,0:T(8,128)} %copy-done, f32[4,512]{1,0:T(4,128)S(1)} %dynamic-slice_bitcast_fusion.4, pred[512,1024]{1,0:T(8,128)(4,1)S(1)} %broadcast_compare_fusion.2, f32[1024,4,64]{0,2,1:T(8,128)} %get-tuple-element.344, pred[]{:T(512)S(6)} %compare.5, ...), kind=kOutput, calls=%fused_computation.23.clone.1 | convolution fusion | flops 292293632 | bytes 36978692 | tf_op jit(solution)/shard_map/while/body/eval_jaxpr/hqk,qhe->khe/dot_general | solution.py:778
  224.9 1.3 fusion.142
  226.2 5.0 fusion.144
  231.2 4.5 fusion.141
  235.7 18.0 %fusion.145 = bf16[2,512,4,64]{1,3,2,0:T(8,128)(2,1)} fusion(bf16[2,512,4,64]{1,3,2,0:T(8,128)(2,1)} %get-tuple-element.346, s32[]{:T(128)S(6)} %copy.145, bf16[1024,4,64]{0,2,1:T(8,128)(2,1)S(1)} %get-tuple-element.365, f32[4,512,1024]{2,1,0:T(8,128)} %fusion.141, f32[4,512,1024]{2,1,0:T(8,128)} %copy-done, ...), kind=kOutput, calls=%fused_computation.28.clone.1 | convolution fusion | flops 291769344 | bytes 35405828 | tf_op jit(solution)/shard_map/while/body/eval_jaxpr/hqk,khe->qhe/dot_general | solution.py:773
  253.7 23.3 %fusion.143 = f32[1024,4,64]{0,2,1:T(8,128)} fusion(f32[4,512,1024]{2,1,0:T(8,128)} %fusion.141, f32[4,512,1024]{2,1,0:T(8,128)} %copy-done, f32[4,512]{1,0:T(4,128)S(1)} %dynamic-slice_bitcast_fusion.4, pred[512,1024]{1,0:T(8,128)(4,1)S(1)} %broadcast_compare_fusion.2, f32[1024,4,64]{0,2,1:T(8,128)} %get-tuple-element.344, pred[]{:T(512)S(6)} %compare.5, ...), kind=kOutput, calls=%fused_computation.23.clone.1 | convolution fusion | flops 292293632 | bytes 36978692 | tf_op jit(solution)/shard_map/while/body/eval_jaxpr/hqk,qhe->khe/dot_general | solution.py:778
  277.2 1.2 copy.107
  278.6 1.3 convert_bitcast_fusion
  280.0 1.3 convert.38
  281.9 1.6 copy-done.21
  283.5 3.0 convolution_convert_fusion.3
  286.6 4.7 convolution_convert_fusion.2
  291.4 3.9 convolution_convert_fusion.1
  295.5 3.2 convolution_convert_fusion
  298.8 1.5 convert_reduce_fusion.2
  300.6 1.6 convert_reduce_fusion.1
  302.4 30.5 %all-gather.9 = bf16[8,1,1024]{2,1,0:T(2,128)(2,1)S(1)} all-gather(bf16[1,1,1024]{2,1,0:T(2,128)(2,1)S(1)} %get-tuple-element.241), channel_id=1, replica_groups=mesh['dp'=8,'seq'=4] {'dp'}, dimensions={0}, use_global_device_ids=true | all-gather | bytes 18432 | tf_op jit(solution)/shard_map/all_gather | solution.py:660
  333.6 5.1 all-gather.8
  339.0 5.2 all-gather.7
  344.8 7.4 %all-gather.4 = bf16[512,512]{1,0:T(8,128)(2,1)S(1)} all-gather(bf16[128,512]{1,0:T(8,128)(2,1)} %reduce-scatter.18.cloned.1.call-done), channel_id=6, replica_groups=mesh['dp'=8,'seq'=4] {'seq'}, dimensions={0}, use_global_device_ids=true | all-gather | bytes 655360 | tf_op jit(solution)/shard_map/all_gather | solution.py:822
  352.9 1.3 copy.120
  354.3 7.5 %all-gather.5 = bf16[256,1024]{1,0:T(8,128)(2,1)S(1)} all-gather(bf16[64,1024]{1,0:T(8,128)(2,1)} %reduce-scatter.20.cloned.1.call-done), channel_id=7, replica_groups=mesh['dp'=8,'seq'=4] {'seq'}, dimensions={0}, use_global_device_ids=true | all-gather | bytes 655360 | tf_op jit(solution)/shard_map/all_gather | solution.py:822
  361.8 1.1 reshape.331
  362.8 9.2 %all-gather = bf16[512,768]{1,0:T(8,128)(2,1)S(1)} all-gather(bf16[128,768]{1,0:T(8,128)(2,1)} %reduce-scatter.12.cloned.1.call-done), channel_id=2, replica_groups=mesh['dp'=8,'seq'=4] {'seq'}, dimensions={0}, use_global_device_ids=true | all-gather | bytes 983040 | tf_op jit(solution)/shard_map/all_gather | solution.py:822
  372.3 1.6 reshape.322
  374.0 1.6 copy.111
  375.5 1.6 copy.119
  377.1 17.8 %reduce-scatter.10.cloned.1.call-done = bf16[256,1024]{1,0:T(8,128)(2,1)} async-done(((bf16[1024,1024]{1,0:T(8,128)(2,1)}), bf16[256,1024]{1,0:T(8,128)(2,1)}) %reduce-scatter.10.cloned.1.call-update) | async-done | bytes 524304 | tf_op jit(solution)/shard_map/reduce_scatter | solution.py:664
  394.9 1.5 multiply_reduce_fusion.2
  396.5 1.6 fusion.84
  398.1 31.2 %reduce-scatter.8.cloned.1.call-done = bf16[256,1024]{1,0:T(8,128)(2,1)} async-done(((bf16[1024,1024]{1,0:T(8,128)(2,1)}), bf16[256,1024]{1,0:T(8,128)(2,1)}) %reduce-scatter.8.cloned.1.call-update) | async-done | bytes 524304 | tf_op jit(solution)/shard_map/reduce_scatter | solution.py:664
  429.3 3.1 multiply_reduce_fusion.1
  432.4 10.3 %psum.7 = f32[1,7168]{1,0:T(1,128)S(1)} all-reduce(f32[1,7168]{1,0:T(1,128)S(1)} %constant_dynamic-update-slice_fusion), channel_id=1, replica_groups=mesh['dp'=8,'seq'=4] {'seq'}, use_global_device_ids=true, to_apply=%region_15.16 | all-reduce | flops 7168 | bytes 57344 | tf_op jit(solution)/shard_map/psum | solution.py:810
  442.7 30.9 %all-gather.6 = bf16[8,1,6144]{2,1,0:T(2,128)(2,1)S(1)} all-gather(bf16[1,1,6144]{2,1,0:T(2,128)(2,1)S(1)} %fusion.93), channel_id=1, replica_groups=mesh['dp'=8,'seq'=4] {'dp'}, dimensions={0}, use_global_device_ids=true | all-gather | bytes 110592 | tf_op jit(solution)/shard_map/all_gather | solution.py:660
  473.7 1.1 fusion.88
  474.8 5.5 all-to-all-start
  481.0 37.6 %all-reduce = f32[8,896]{1,0:T(8,128)S(1)} all-reduce(f32[8,896]{1,0:T(8,128)S(1)} %pad_maximum_fusion.3), channel_id=11, replica_groups=mesh['dp'=8,'seq'=4] {'dp'}, use_global_device_ids=true, to_apply=%region_20.21.clone | all-reduce | flops 7168 | bytes 57344
  518.6 2.3 fusion.86
  520.8 1.3 add_add_fusion.1
  522.2 1.2 dynamic-slice_bitcast_fusion.1
  523.4 1.3 dynamic-slice.6
  524.7 1.2 dynamic-slice_reduce_fusion.2
  527.2 20.8 %reduce-scatter.16.cloned.1.call-done = bf16[128,256]{1,0:T(8,128)(2,1)} async-done(((bf16[1024,256]{1,0:T(8,128)(2,1)}), bf16[128,256]{1,0:T(8,128)(2,1)}) %reduce-scatter.16.cloned.1.call-update) | async-done | bytes 65552 | tf_op jit(solution)/shard_map/reduce_scatter | solution.py:670
  548.0 6.0 %all-gather.3 = bf16[512,256]{1,0:T(8,128)(2,1)S(1)} all-gather(bf16[128,256]{1,0:T(8,128)(2,1)} %reduce-scatter.16.cloned.1.call-done), channel_id=5, replica_groups=mesh['dp'=8,'seq'=4] {'seq'}, dimensions={0}, use_global_device_ids=true | all-gather | bytes 327680 | tf_op jit(solution)/shard_map/all_gather | solution.py:822
  554.0 0.9 copy.124
  (145 shorter events, 14.3 us)
Async XLA Ops:
  7.2 337.6 %reduce-scatter.18.cloned.1.call-start = ((), (), s32[]{:S(2)}) async-start(), calls=%async_computation.13 | async-start | bytes 1179648 | tf_op jit(solution)/shard_map/reduce_scatter | solution.py:670
  160.2 4.4 copy-start.2
  160.2 4.4 copy-start.12
  164.5 189.8 %reduce-scatter.20.cloned.1.call-start = ((), (), s32[]{:S(2)}) async-start(), calls=%async_computation.14 | async-start | bytes 1179648 | tf_op jit(solution)/shard_map/reduce_scatter | solution.py:670
  166.8 2.9 copy-start.16
  166.8 3.6 copy-start.15
  166.8 3.8 copy-start.18
  166.8 196.0 %reduce-scatter.12.cloned.1.call-start = ((), (), s32[]{:S(2)}) async-start(), calls=%async_computation.10 | async-start | bytes 1769472 | tf_op jit(solution)/shard_map/reduce_scatter | solution.py:670
  170.7 107.8 %copy-start.6 = (f32[1024,128]{1,0:T(8,128)S(1)}, f32[1024,128]{1,0:T(8,128)}, u32[]{:S(2)}) copy-start(f32[1024,128]{1,0:T(8,128)} %get-tuple-element.255.sin) | copy-start | bytes 1572868
  173.7 3.7 copy-start
  226.2 5.0 copy-start
  278.6 2.7 copy-start.11
  281.3 5.3 copy-start.7
  281.3 2.2 copy-start.21
  281.8 4.8 copy-start.8
  281.9 4.7 copy-start.9
  286.5 108.4 %reduce-scatter.10.cloned.1.call-start = ((), (), s32[]{:S(2)}) async-start(), calls=%async_computation.9 | async-start | bytes 2621440 | tf_op jit(solution)/shard_map/reduce_scatter | solution.py:664
  286.6 4.8 copy-start.13
  291.3 138.0 %reduce-scatter.8.cloned.1.call-start = ((), (), s32[]{:S(2)}) async-start(), calls=%async_computation.8 | async-start | bytes 2621440 | tf_op jit(solution)/shard_map/reduce_scatter | solution.py:664
  291.4 4.0 copy-start.14
  295.3 5.0 copy-start.3
  295.3 185.1 %reduce-scatter.14.cloned.1.call-start = ((), (), s32[]{:S(2)}) async-start(), calls=%async_computation.11 | async-start | bytes 2621440 | tf_op jit(solution)/shard_map/reduce_scatter | solution.py:745
  298.7 3.6 copy-start.1
  298.7 45.5 %copy-start.22 = (u32[32]{0:T(128)S(1)}, u32[32]{0:T(128)}, u32[]{:S(2)}) copy-start(u32[32]{0:T(128)} %constant.134) | copy-start | bytes 388
  373.9 24.1 %copy-start.19 = (f32[8,1024]{1,0:T(8,128)S(1)}, f32[8,1024]{1,0:T(8,128)}, u32[]{:S(2)}) copy-start(f32[8,1024]{1,0:T(8,128)} %get-tuple-element.106) | copy-start | bytes 98308
  373.9 55.4 %copy-start.20 = (f32[1,1024]{1,0:T(1,128)S(1)}, f32[1,1024]{1,0:T(1,128)}, u32[]{:S(2)}) copy-start(f32[1,1024]{1,0:T(1,128)} %get-tuple-element.95) | copy-start | bytes 12292
  377.1 96.5 %copy-start.4 = (bf16[128,6144]{1,0:T(8,128)(2,1)S(1)}, bf16[128,6144]{1,0:T(8,128)(2,1)}, u32[]{:S(2)}) copy-start(bf16[128,6144]{1,0:T(8,128)(2,1)} %wm_hbm.1) | copy-start | bytes 4718596
  429.3 91.5 %copy-start.5 = (bf16[256,1024]{1,0:T(8,128)(2,1)S(1)}, bf16[256,1024]{1,0:T(8,128)(2,1)}, u32[]{:S(2)}) copy-start(bf16[256,1024]{1,0:T(8,128)(2,1)} %reduce-scatter.10.cloned.1.call-done) | copy-start | bytes 1572868
  474.8 46.1 %copy-start.10 = (f32[256,1024]{1,0:T(8,128)S(1)}, f32[256,1024]{1,0:T(8,128)}, u32[]{:S(2)}) copy-start(f32[256,1024]{1,0:T(8,128)} %get-tuple-element.96) | copy-start | bytes 3145732
  474.8 51.8 %copy-start.17 = (f32[1,1024]{1,0:T(1,128)S(1)}, f32[1,1024]{1,0:T(1,128)}, u32[]{:S(2)}) copy-start(f32[1,1024]{1,0:T(1,128)} %param.17) | copy-start | bytes 12292
  474.8 51.8 %all-to-all-start = ((f32[8,1,128]{2,1,0:T(1,128)}), f32[8,1,128]{2,1,0:T(1,128)S(1)}, u32[]{:S(2)}, u32[]{:S(2)}) async-start(f32[8,1,128]{2,1,0:T(1,128)} %bitcast.27), calls=%async_computation.2 | async-start | bytes 8192 | tf_op jit(solution)/shard_map/all_to_all | solution.py:816
  480.2 67.8 %reduce-scatter.16.cloned.1.call-start = ((), (), s32[]{:S(2)}) async-start(), calls=%async_computation.12 | async-start | bytes 589824 | tf_op jit(solution)/shard_map/reduce_scatter | solution.py:670
Sparse Core Ops, SparseCore 0:
  164.6 62.4 reduce-scatter.17
  231.4 62.5 reduce-scatter.19
  298.0 63.8 reduce-scatter.11
  364.5 30.4 reduce-scatter.9
  397.9 31.4 reduce-scatter.7
  431.9 31.4 reduce-scatter.13
  484.4 63.5 reduce-scatter.15

commit v3 on v2

--- a/solution.py
+++ b/solution.py
@@ -271,8 +271,8 @@
 def kernel_a(
     n,
     frames, cot, tcols, bm, bias, wu_own, cos, sin, idr, idc, wm_hbm, wq_hbm, wo_hbm, wd_hbm,
-    xa, q, k, v, kt, vt, lse, ao, gh, dffn, gelu, xf, dhid, wq, wd, dmid, xmid, dattn, mod, fsum, bd_full,
-    wm, wu, wo, tbuf, psend, pbuf, bbuf, n_in, attn_branch, n_mid, ao_out, do_out, held,
+    xa, q, k, v, kt, vt, lse, ao, gh, dffn, gelu, xf, dhid, wq, wd, dmid, xmid, dattn, mod, fsum, bd_full, tbuf,
+    wm, wu, wo, psend, pbuf, bbuf, n_in, attn_branch, n_mid, ao_out, do_out, held,
     send, recv, local,
 ):
     l = Links(n, send, recv)
@@ -532,12 +532,12 @@
         S((4, rows, quarter), bf16), S((4, rows, quarter), bf16), S((4, rows, width), bf16), S((item, ff_q), bf16),
         S((4, rows, width), bf16), S((item, ff_q), bf16), S((n, own_rows, 3 * quarter), bf16), S((n, units, width), bf16),
         S((rows, width), f32), S((rows, width), f32), S((rows, width), bf16), S((4, 1, 6 * quarter), f32),
-        S((8, width), f32), S((1, width), f32),
+        S((8, width), f32), S((1, width), f32), S((n, 1, own_rows), f32),
     ]
     V = pltpu.VMEM
     scratch = [
         V((own_rows, 6 * quarter), bf16), V((n, own_rows, ff_q), bf16), V((4, n, own_rows, quarter), bf16),
-        V((n, 1, own_rows), f32), V((n, 1, 6 * quarter), f32), V((n, 1, 6 * quarter), f32), V((n, 1, bias.shape[2]), f32),
+        V((n, 1, 6 * quarter), f32), V((n, 1, 6 * quarter), f32), V((n, 1, bias.shape[2]), f32),
         V((rows, width), f32), V((rows, width), f32), V((rows, width), f32), V((4, rows, quarter), bf16),
         V((4, rows, quarter), bf16), V((6, rows, width), bf16),
         pltpu.SemaphoreType.DMA((7 * n + 40,)), pltpu.SemaphoreType.DMA((7 * n + 40,)), pltpu.SemaphoreType.DMA((6,)),
@@ -554,6 +554,315 @@
     )(frames, cot, tcols, bm, bias, wu_own, cos, sin, idr, idc, w_mod, w_qkv, w_out, w_down)
 
 
+def tn(left_side, right_side):
+    return lax.dot_general(left_side, right_side, (((0,), (0,)), ((), ())), preferred_element_type=f32)
+
+
+class DpSum:
+    def __init__(self, links, g, xin, zin):
+        self.l, self.g, self.xin, self.zin = links, g, xin, zin
+        self.half = links.n // 2
+        self.si, self.ri = links.sems(links.n, links.n)
+
+    def _x(self, t):
+        l = self.l
+        h = t // 2
+        return l.copy(self.g.at[t], self.xin.at[h], self.si + h, self.ri + h, (l.px, l.s))
+
+    def _z(self, k):
+        l = self.l
+        t = (l.d + 2 * k) % l.n
+        at = self.half + k
+        return l.copy(self.g.at[t], self.zin.at[k], self.si + at, self.ri + at, (t, l.s))
+
+    def send_x(self, first, count):
+        for i in range(count // 2):
+            self._x(first + 2 * i + self.l.px % 2).start()
+
+    def fold(self):
+        l = self.l
+
+        def one(k, carry):
+            t = (l.d + 2 * k) % l.n
+            h = t // 2
+            l.copy(self.xin.at[h], self.xin.at[h], self.si, self.ri + h, (l.px, l.s)).wait_recv()
+            self.g[t] = (self.g[t].astype(f32) + self.xin[h].astype(f32)).astype(bf16)
+            self._z(k).start()
+            return carry
+
+        lax.fori_loop(1, self.half, one, 0)
+
+    def total(self):
+        l = self.l
+        h = l.d // 2
+        l.copy(self.xin.at[h], self.xin.at[h], self.si, self.ri + h, (l.px, l.s)).wait_recv()
+        out = self.g[l.d].astype(f32) + self.xin[h].astype(f32)
+        for k in range(1, self.half):
+            self._z(k).wait_recv()
+            out = out + self.zin[k].astype(f32)
+        return out
+
+    def wait_send(self):
+        l = self.l
+        for k in range(self.half):
+            self._x((l.px + 2 * k) % l.n).wait_send()
+        for k in range(1, self.half):
+            self._z(k).wait_send()
+
+
+def kernel_b(
+    n,
+    frames, cot, time3, tbuf, cos, sin, idr, idc, xa, q, k, v, kt, lse, ao, gh, dffn, gelu, xf, dhid, wq, wd,
+    dmid, xmid, dattn, mod, fsum, bd_full, wm,
+    block_out, grad_input, grad_time, gwm, gbm, f_wq, f_wo, f_wu, f_wd, f_b,
+    g_wq, x_wq, z_wq, g_wo, x_wo, z_wo, g_wu, x_wu, z_wu, g_wd, x_wd, z_wd,
+    held_f, held_o, held_a, dk, dv, dproj, n_in, em, lm, ebuf, lbuf, eb, ebb, lb, lbb, dts, dtb,
+    send, recv,
+):
+    l = Links(n, send, recv)
+    d, s = l.d, l.s
+    rows, width = frames.shape
+    item = 4 * rows
+    quarter = width // 4
+    own_rows = wm.shape[0]
+    units = wd.shape[1]
+    ff_q = gelu.shape[1]
+    pairs = quarter // 128
+    lane = lax.broadcasted_iota(jnp.int32, (rows, 128), 1)
+    sum_f, sum_o, sum_a = SeqSum(l, held_f), SeqSum(l, held_o), SeqSum(l, held_a)
+    d_wq, d_wo, d_wu, d_wd = (
+        DpSum(l, g_wq, x_wq, z_wq), DpSum(l, g_wo, x_wo, z_wo), DpSum(l, g_wu, x_wu, z_wu), DpSum(l, g_wd, x_wd, z_wd),
+    )
+    o_wq, o_wo, o_wu, o_wd = SeqGather(l, f_wq), SeqGather(l, f_wo), SeqGather(l, f_wu), SeqGather(l, f_wd)
+    e_mod, l_mod, o_b = SeqAll(l, em), SeqAll(l, lm), SeqAll(l, f_b)
+    e_all, l_all = ToAll(l, lambda peer: ebuf.at[d], ebuf), ToAll(l, lambda peer: lbuf.at[d], lbuf)
+    eb_all, lb_all = ToAll(l, lambda peer: eb, ebb), ToAll(l, lambda peer: lb, lbb)
+    t_all = ToAll(l, lambda peer: dts.at[peer], dtb)
+    flat = jnp.concatenate([mod[i] for i in range(4)], axis=1)
+    scale_a = flat[:, width : 2 * width]
+    gate_f = flat[:, 5 * width :]
+    l.barrier()
+
+    def at_rows(b):
+        return pl.ds(pl.multiple_of(b * rows, rows), rows)
+
+    def ffn_term(b):
+        return nn(gelu[at_rows(b), :], merged(wd))
+
+    def out_term(t):
+        part = dattn[:, pl.ds(pl.multiple_of(t * quarter, 128), quarter)]
+        return jnp.concatenate([tn(ao[i], part) for i in range(4)], axis=0)
+
+    def xa_term(b):
+        return nt(dproj[at_rows(b), :], merged(wq))
+
+    sum_f.far(ffn_term)
+
+    def make(left_of, right, g, chain, each):
+        per = 256 // each
+
+        def one(m, carry):
+            val = tn(left_of(m), right()).astype(bf16)
+            g[pl.ds(m * per, per)] = val.reshape(per, each, val.shape[1])
+            chain.send_x(m * per, per)
+            return carry
+
+        lax.fori_loop(0, n // per, one, 0)
+
+    make(lambda m: gelu[:, pl.ds(pl.multiple_of(m * 256, 256), 256)], lambda: merged(dffn), g_wd, d_wd, units)
+
+    def cols_of(ref, m):
+        return ref[:, :, pl.ds(pl.multiple_of(m * 256, 256), 256)].reshape(item, 256)
+
+    make(lambda m: cols_of(xf, m), lambda: dhid[...], g_wu, d_wu, own_rows)
+    sum_f.near(ffn_term)
+    eb[:, :ff_q] = jnp.sum(dhid[...].astype(f32), axis=0, keepdims=True)
+    eb[:, ff_q : ff_q + width] = fsum[3:4, :]
+    eb[:, ff_q + width :] = jnp.sum(dffn[s].astype(f32), axis=0, keepdims=True)
+    eb_all.start()
+    n_val, rstd = normed(frames[...])
+    n_in[...] = n_val
+    dk[...] = jnp.zeros_like(dk)
+    dv[...] = jnp.zeros_like(dv)
+
+    def turned(values, at):
+        val = values.astype(bf16).astype(f32)
+        return (val * cos[at, :] - swap_halves(val, lane) * sin[at, :]).astype(bf16)
+
+    def attend_back(j, carry):
+        b = j
+        at = at_rows(b)
+        same = idc[...] == idr[:, at]
+        for p in range(pairs):
+            c0 = 128 * p
+            kp, vp = k[:, c0 : c0 + 128], v[:, c0 : c0 + 128]
+            qp, dop = q[at, c0 : c0 + 128], gh[b, :, c0 : c0 + 128]
+            dqs = []
+            for h in range(2):
+                mine = (lane < 64) == (h == 0)
+                qm = jnp.where(mine, qp, jnp.zeros_like(qp))
+                dom = jnp.where(mine, dop, jnp.zeros_like(dop))
+                pt = jnp.exp(jnp.where(same, nt(kp, qm), -1e30) - lse[2 * p + h, :, at])
+                dpt = nt(vp, dom)
+                mean = jnp.sum(dpt * pt, axis=0, keepdims=True)
+                dst = (pt * (dpt - mean)).astype(bf16)
+                dv[p] += nn(pt.astype(bf16), dom)
+                dk[p] += nn(dst, qm)
+                dqs.append(nn(kt[p, 64 * h : 64 * h + 64, :], dst))
+            dq = jnp.transpose(jnp.concatenate(dqs, axis=0)) * 0.125
+            dproj[at, c0 : c0 + 128] = turned(dq, at)
+
+        @pl.when(j == 0)
+        def _():
+            d_wd.fold()
+            sum_o.far(out_term)
+
+        @pl.when(j == 1)
+        def _():
+            sum_o.near(out_term)
+            ffn = sum_f.total(ffn_term(s)) + bd_full[...]
+            block_out[...] = xmid[...] + gate_f * ffn
+            em[s, :, 3 * width :] = jnp.sum(cot[...] * ffn, axis=0, keepdims=True)
+            em[s, :, :width] = fsum[2:3, :]
+            em[s, :, width : 2 * width] = fsum[0:1, :]
+            em[s, :, 2 * width : 3 * width] = fsum[1:2, :]
+            e_mod.start()
+
+        @pl.when(j == 2)
+        def _():
+            d_wu.fold()
+            g_wo[...] = sum_o.total(out_term(s)).astype(bf16).reshape(n, own_rows, quarter)
+            d_wo.send_x(0, n)
+
+        @pl.when(j == 3)
+        def _():
+            e_mod.wait_recv()
+            tot = em[0] + em[1] + em[2] + em[3]
+            ebuf[d] = tot.astype(bf16).astype(f32)
+            e_all.start()
+            f_wd[s] = d_wd.total().astype(bf16)
+            o_wd.start()
+
+        return carry
+
+    lax.fori_loop(0, 4, attend_back, 0)
+
+    def finish(b, carry):
+        at = at_rows(b)
+        for p in range(pairs):
+            c0 = 128 * p
+            dproj[at, quarter + c0 : quarter + c0 + 128] = turned(dk[p, at, :], at)
+            dproj[at, 2 * quarter + c0 : 2 * quarter + c0 + 128] = dv[p, at, :].astype(bf16)
+        return carry
+
+    lax.fori_loop(0, 4, finish, 0)
+    sum_a.far(xa_term)
+    make(lambda m: cols_of(xa, m), lambda: dproj[...], g_wq, d_wq, own_rows)
+    sum_a.near(xa_term)
+    d_wo.fold()
+    lb[...] = jnp.sum(dproj[...].astype(f32), axis=0, keepdims=True)
+    lb_all.start()
+    o_wd.hand_on()
+    f_wu[s] = d_wu.total().astype(bf16)
+    o_wu.start()
+    times = jnp.concatenate([tbuf[i] for i in range(n)], axis=0).astype(bf16)
+    e_all.wait_recv()
+    dm_e = jnp.concatenate([ebuf[i] for i in range(n)], axis=0)
+    gbm[:, 2 * width :] = jnp.sum(dm_e, axis=0, keepdims=True)
+    dm_e = dm_e.astype(bf16)
+    for c in range(2, 6):
+        gwm[:, c * width : (c + 1) * width] = tn(times, dm_e[:, (c - 2) * width : (c - 1) * width])
+    dt = nt(dm_e, wm[:, 2 * width :])
+    g = sum_a.total(xa_term(s))
+    n_val = n_in[...]
+    lm[s, :, :width] = jnp.sum(g, axis=0, keepdims=True)
+    lm[s, :, width:] = jnp.sum(g * n_val, axis=0, keepdims=True)
+    l_mod.start()
+    grad_input[...] = dmid[...] + norm_back(g * (1.0 + scale_a), n_val, rstd)
+    d_wq.fold()
+    l_mod.wait_recv()
+    lbuf[d] = (lm[0] + lm[1] + lm[2] + lm[3]).astype(bf16).astype(f32)
+    l_all.start()
+    o_wu.hand_on()
+    f_wo[s] = d_wo.total().astype(bf16)
+    o_wo.start()
+    eb_all.wait_recv()
+    lb_all.wait_recv()
+    esum, lsum = eb[...], lb[...]
+    for j in range(1, n):
+        esum = esum + ebb[(d + j) % n]
+        lsum = lsum + lbb[(d + j) % n]
+    f_b[s, :, : 3 * quarter] = lsum
+    f_b[s, :, 3 * quarter :] = esum
+    o_b.start()
+    l_all.wait_recv()
+    dm_l = jnp.concatenate([lbuf[i] for i in range(n)], axis=0)
+    gbm[:, : 2 * width] = jnp.sum(dm_l, axis=0, keepdims=True)
+    dm_l = dm_l.astype(bf16)
+    dt = dt + nt(dm_l, wm[:, : 2 * width])
+    for i in range(n):
+        dts[i] = dt[i : i + 1]
+    t_all.start()
+    for c in range(2):
+        gwm[:, c * width : (c + 1) * width] = tn(times, dm_l[:, c * width : (c + 1) * width])
+    f_wq[s] = d_wq.total().astype(bf16)
+    o_wq.start()
+    o_wo.hand_on()
+    t_all.wait_recv()
+    dtb[d] = dts[d]
+    tv = time3[...]
+    sig = 1.0 / (1.0 + jnp.exp(-tv))
+    grad_time[...] = dtb[...] * (sig + tv * sig * (1.0 - sig))
+    o_wq.hand_on()
+    for o in (o_wq, o_wo, o_wu, o_wd):
+        o.wait(l.s1)
+        o.wait(l.s3)
+    o_b.wait_recv()
+    for c in (
+        sum_f, sum_o, sum_a, d_wq, d_wo, d_wu, d_wd, o_wq, o_wo, o_wu, o_wd, e_mod, l_mod, o_b,
+        e_all, l_all, eb_all, lb_all, t_all,
+    ):
+        c.wait_send()
+
+
+def run_b(n, *ops):
+    frames, w_mod, wd, gelu = ops[0], ops[-1], ops[21], ops[17]
+    rows, width = frames.shape
+    item, quarter, own_rows, units, ff_q = 4 * rows, width // 4, w_mod.shape[0], wd.shape[1], gelu.shape[1]
+    S, V = jax.ShapeDtypeStruct, pltpu.VMEM
+    bw = 3 * quarter + ff_q + 2 * width
+    outs = [
+        S((rows, width), f32), S((rows, width), f32), S((n, 1, own_rows), f32), S((own_rows, 6 * width), f32),
+        S((1, 6 * width), f32), S((4, own_rows, 3 * quarter), bf16), S((4, own_rows, quarter), bf16),
+        S((4, own_rows, ff_q), bf16), S((4, units, width), bf16), S((4, 1, bw), f32),
+    ]
+
+    def chain(a, b):
+        return [V((n, a, b), bf16), V((n // 2, a, b), bf16), V((n // 2, a, b), bf16)]
+
+    scratch = (
+        chain(own_rows, 3 * quarter) + chain(own_rows, quarter) + chain(own_rows, ff_q) + chain(units, width)
+        + [V((6, rows, width), bf16), V((6, width, quarter), bf16), V((6, rows, width), bf16)]
+        + [V((quarter // 128, item, 128), f32)] * 2
+        + [
+            V((item, 3 * quarter), bf16), V((rows, width), f32), V((4, 1, 4 * width), f32), V((4, 1, 2 * width), f32),
+            V((n, 1, 4 * width), f32), V((n, 1, 2 * width), f32), V((1, ff_q + 2 * width), f32),
+            V((n, 1, ff_q + 2 * width), f32), V((1, 3 * quarter), f32), V((n, 1, 3 * quarter), f32),
+            V((n, 1, own_rows), f32), V((n, 1, own_rows), f32),
+        ]
+        + [pltpu.SemaphoreType.DMA((9 * n + 40,)), pltpu.SemaphoreType.DMA((9 * n + 40,))]
+    )
+    vm = pl.BlockSpec(memory_space=pltpu.VMEM)
+    return pl.pallas_call(
+        functools.partial(kernel_b, n),
+        out_shape=outs,
+        in_specs=[vm] * len(ops),
+        out_specs=[vm] * len(outs),
+        scratch_shapes=scratch,
+        compiler_params=pltpu.CompilerParams(collective_id=1, has_side_effects=True, vmem_limit_bytes=62 << 20),
+    )(*ops)
+
+
 def clip_layout(lengths, length):
     clips = lengths.shape[0]
     earlier = jnp.arange(clips)[None, :] <= jnp.arange(clips)[:, None]
@@ -608,260 +917,41 @@
     return tcols, bm, bias, wu_own, cos, sin, clip_ids[None, :], clip_ids[:, None]
 
 
-def layer_norm(values):
-    mean_val = jnp.mean(values, axis=-1, keepdims=True)
-    centred = values - mean_val
-    variance = jnp.mean(centred * centred, axis=-1, keepdims=True)
-    return centred * lax.rsqrt(variance + norm_eps)
-
-
-def modulate(values, shift_term, scale_term):
-    return layer_norm(values) * (1.0 + scale_term) + shift_term
-
-
-def rotate(values, cosine_tab, sine_tab):
-    half_dim = values.shape[-1] // 2
-    lower_half = values[..., :half_dim]
-    upper_half = values[..., half_dim:]
-    return jnp.concatenate(
-        [
-            lower_half * cosine_tab - upper_half * sine_tab,
-            upper_half * cosine_tab + lower_half * sine_tab,
-        ],
-        axis=-1,
+def per_device(
+    frames, time_embed, clip_len, w_qkv, b_qkv, w_out, b_out, w_up, b_up, w_down, b_down, w_mod, b_mod, cotangent
+):
+    n = lax.axis_size("dp")
+    seq_rank, dp_rank = lax.axis_index("seq"), lax.axis_index("dp")
+    rows, width = frames.shape
+    quarter = width // 4
+    own_rows, ff = w_up.shape
+    units = w_down.shape[0] // 4
+    pre = prepare(seq_rank, dp_rank, n, frames, time_embed, clip_len, b_qkv, b_out, w_up, b_up, b_down, b_mod)
+    cos, sin, idr, idc = pre[4:]
+    outs = run_a(n, frames, cotangent, *pre, w_mod, w_qkv, w_out, w_down)
+    xa, q, k, v, kt, _, lse, ao, gh, dffn, gelu, xf, dhid, wq, wd, dmid, xmid, dattn, mod, fsum, bd, tbuf = outs
+    time3 = time_embed.reshape(n, 1, own_rows)
+    block_out, grad_input, grad_time, gwm, gbm, f_wq, f_wo, f_wu, f_wd, f_b = run_b(
+        n, frames, cotangent, time3, tbuf, cos, sin, idr, idc, xa, q, k, v, kt, lse, ao, gh, dffn, gelu, xf, dhid,
+        wq, wd, dmid, xmid, dattn, mod, fsum, bd, w_mod,
     )
-
-
-def across_rows(left_side, right_side):
-    return lax.dot_general(
-        left_side, right_side, (((0,), (0,)), ((), ())), preferred_element_type=jnp.float32
-    )
-
-
-def against(left_side, right_side):
-    return lax.dot_general(
-        left_side, right_side, (((1,), (1,)), ((), ())), preferred_element_type=jnp.float32
-    )
-
-
-def forward_dot(left_side, right_side):
-    return jnp.dot(left_side, right_side, preferred_element_type=jnp.float32)
-
-
-def column_sums(values):
-    return jnp.sum(values.astype(jnp.float32), axis=0)
-
-
-def seq_gather(value):
-    return lax.all_gather(value, "seq", axis=0, tiled=True)
-
-
-def dp_gather(value):
-    return lax.all_gather(value, "dp", axis=0, tiled=True)
-
-
-def seq_reduce(value):
-    return lax.psum_scatter(
-        value.astype(jnp.bfloat16), "seq", scatter_dimension=0, tiled=True
-    ).astype(jnp.float32)
-
-
-def dp_reduce(value):
-    return lax.psum_scatter(value.astype(jnp.bfloat16), "dp", scatter_dimension=0, tiled=True)
-
-
-def per_device(
-    frames,
-    time_embed,
-    clip_len,
-    w_qkv,
-    b_qkv,
-    w_out,
-    b_out,
-    w_up,
-    b_up,
-    w_down,
-    b_down,
-    w_mod,
-    b_mod,
-    cotangent,
-):
-    seq_count = lax.axis_size("seq")
-    seq_rank = lax.axis_index("seq")
-    dp_count = lax.axis_size("dp")
-    dp_rank = lax.axis_index("dp")
-    frame_rows = frames.shape[0]
-    model_width = frames.shape[1]
-    length = frame_rows * seq_count
-    heads_here = HEADS // seq_count
-    head_dim = model_width // HEADS
-    local_width = heads_here * head_dim
-    factor = head_dim ** (-0.5)
-    block_rows = min(512, length)
-    block_count = length // block_rows
-    own_rows = w_qkv.shape[0]
-    ff_width = w_up.shape[1]
-    units_each = w_down.shape[0] // seq_count
-    units_here = ff_width // seq_count
-
-    pre = prepare(
-        seq_rank, dp_rank, dp_count, frames, time_embed, clip_len, b_qkv, b_out, w_up, b_up, b_down, b_mod
-    )
-    outs = run_a(dp_count, frames, cotangent, *pre, w_mod, w_qkv, w_out, w_down)
-    x_a, q8, k, v, _, _, lse, attn_out, grad_heads, d_ffn_item, gelu_act, x_f, d_hidden, wq, wd = outs[:15]
-    d_mid, x_mid, d_attn, mod, fsum, bd_full = outs[15:]
-    tcols, _, _, _, cos, sin, clip_ids = pre[:7]
-    clip_ids = clip_ids[0]
-    cosine_tab, sine_tab = cos[:, None, :32], -sin[:, None, :32]
-    sizes = [b_qkv.shape[0], b_out.shape[0], b_up.shape[0], b_down.shape[0]]
-    cuts = [sizes[0], sizes[0] + sizes[1], sizes[0] + sizes[1] + sizes[2]]
-    time_all = dp_gather(jax.nn.silu(time_embed).astype(jnp.bfloat16))
-    time_cols = lax.dynamic_slice_in_dim(time_all, dp_rank * own_rows, own_rows, 1)
-    x_a = x_a.reshape(length, model_width)
-    x_f = x_f.reshape(length, model_width)
-    d_ffn_item = d_ffn_item.reshape(length, model_width)
-    wq_here = wq.reshape(model_width, -1)
-    wd_here = wd.reshape(units_here, model_width)
-    query_heads = (q8 * jnp.bfloat16(8)).reshape(length, heads_here, head_dim)
-    keys_heads = k.reshape(length, heads_here, head_dim)
-    values_heads = v.reshape(length, heads_here, head_dim)
-    attn_out = attn_out.transpose(1, 0, 2).reshape(frame_rows, model_width)
-    grad_heads = grad_heads.reshape(length, heads_here, head_dim)
-    log_totals = (
-        lse.reshape(heads_here, block_count, block_rows).transpose(1, 0, 2)[:, :, :, None]
-    )
-    shift_a, scale_a, gate_a, shift_f, scale_f, gate_f = jnp.split(
-        mod.reshape(1, 6 * model_width), 6, axis=1
-    )
-    d_shift_f, d_scale_f, d_gate_a, g_bo = fsum[0:1], fsum[1:2], fsum[2:3], fsum[3]
-    ffn_branch = seq_reduce(forward_dot(gelu_act, wd_here)) + bd_full
-    block_out = x_mid + gate_f * ffn_branch
-    d_gate_f = jnp.sum(cotangent * ffn_branch, axis=0, keepdims=True)
-    g_wd = across_rows(gelu_act, d_ffn_item)
-    g_bd = column_sums(d_ffn_item)
-    g_wu = across_rows(x_f, d_hidden)
-    g_bu = column_sums(d_hidden)
-    g_wo_run = across_rows(attn_out, d_attn)
-    g_wo = lax.psum_scatter(
-        g_wo_run.astype(jnp.bfloat16), "seq", scatter_dimension=1, tiled=True
-    )
-
-    def block_scores(block_index):
-        first_row = block_index * block_rows
-        query_blk = lax.dynamic_slice_in_dim(query_heads, first_row, block_rows, 0)
-        clip_blk = lax.dynamic_slice_in_dim(clip_ids, first_row, block_rows, 0)
-        same_clip = (clip_blk[:, None] == clip_ids[None, :])[None]
-        raw_scores = (
-            jnp.einsum("qhe,khe->hqk", query_blk, keys_heads, preferred_element_type=jnp.float32)
-            * factor
-        )
-        return (query_blk, same_clip, jnp.where(same_clip, raw_scores, -1e30))
-
-    def attend_back(running, inputs):
-        grad_keys, grad_values = running
-        block_index, log_blk = inputs
-        query_blk, same_clip, masked = block_scores(block_index)
-        attn_prob = jnp.exp(masked - log_blk)
-        prob_low = attn_prob.astype(jnp.bfloat16)
-        grad_blk = lax.dynamic_slice_in_dim(grad_heads, block_index * block_rows, block_rows, 0)
-        d_prob = jnp.einsum(
-            "qhe,khe->hqk", grad_blk, values_heads, preferred_element_type=jnp.float32
-        )
-        d_scores = attn_prob * (d_prob - jnp.sum(d_prob * attn_prob, axis=-1, keepdims=True))
-        d_scores = jnp.where(same_clip, d_scores, 0.0).astype(jnp.bfloat16)
-        d_query = (
-            jnp.einsum("hqk,khe->qhe", d_scores, keys_heads, preferred_element_type=jnp.float32)
-            * factor
-        )
-        grad_keys = (
-            grad_keys
-            + jnp.einsum("hqk,qhe->khe", d_scores, query_blk, preferred_element_type=jnp.float32)
-            * factor
-        )
-        grad_values = grad_values + jnp.einsum(
-            "hqk,qhe->khe", prob_low, grad_blk, preferred_element_type=jnp.float32
-        )
-        return ((grad_keys, grad_values), d_query.astype(jnp.bfloat16))
-
-    zero_heads = jnp.zeros((length, heads_here, head_dim), jnp.float32)
-    (grad_keys, grad_values), query_grads = lax.scan(
-        attend_back, (zero_heads, zero_heads), (jnp.arange(block_count), log_totals)
-    )
-    def turned_back(value):
-        return rotate(value.astype(jnp.bfloat16).astype(jnp.float32), cosine_tab, -sine_tab)
-
-    d_projected = jnp.concatenate(
-        [
-            turned_back(query_grads.reshape(length, heads_here, head_dim)).reshape(length, -1),
-            turned_back(grad_keys).reshape(length, -1),
-            grad_values.reshape(length, -1),
-        ],
-        axis=1,
-    ).astype(jnp.bfloat16)
-    d_xa = seq_reduce(against(d_projected, wq_here))
-    g_wq = across_rows(x_a, d_projected)
-    g_bq = column_sums(d_projected)
-    input_pull = jax.vjp(modulate, frames, shift_a, scale_a)[1]
-    d_input_part, d_shift_a, d_scale_a = input_pull(d_xa)
-    grad_input = d_mid + d_input_part
-    mod_part = jnp.concatenate(
-        [d_shift_a, d_scale_a, d_gate_a, d_shift_f, d_scale_f, d_gate_f, g_bo[None]], axis=1
-    )
-    mod_sum = lax.psum(mod_part, "seq")
-    d_mod = dp_gather(mod_sum[:, : 6 * model_width].astype(jnp.bfloat16))
-    g_wm = across_rows(time_cols, d_mod)
-    g_bm = column_sums(
-        lax.dynamic_slice_in_dim(d_mod, dp_rank * b_mod.shape[0], b_mod.shape[0], 1)
-    )
-    d_time_act = lax.all_to_all(
-        against(d_mod, w_mod), "dp", split_axis=0, concat_axis=1, tiled=True
-    )
-    grad_time = jax.vjp(jax.nn.silu, time_embed)[1](d_time_act)[0]
-
-    def spread(value):
-        return lax.all_gather(dp_reduce(value), "seq", axis=0).astype(jnp.float32)
-
-    s_wq = (
-        spread(g_wq)
-        .reshape(seq_count, own_rows, 3, local_width)
-        .transpose(1, 2, 0, 3)
-        .reshape(own_rows, 3 * model_width)
-    )
-    s_wo = spread(g_wo).transpose(1, 0, 2).reshape(own_rows, model_width)
-    s_wu = (
-        spread(g_wu)
-        .reshape(seq_count, own_rows, dp_count, units_each)
-        .transpose(1, 2, 0, 3)
-        .reshape(own_rows, ff_width)
-    )
-    s_wd = spread(g_wd).reshape(seq_count * units_each, model_width)
-    bq_item = lax.all_gather(g_bq, "seq", axis=0).reshape(seq_count, 3, local_width)
-    bu_item = lax.all_gather(g_bu, "seq", axis=0).reshape(seq_count, dp_count, units_each)
-    bias_terms = jnp.concatenate(
-        [
-            bq_item.transpose(1, 0, 2).reshape(dp_count, sizes[0]),
-            mod_sum[:, 6 * model_width :].reshape(dp_count, sizes[1]),
-            bu_item.transpose(1, 0, 2).reshape(dp_count, sizes[2]),
-            g_bd.reshape(dp_count, sizes[3]),
-        ],
-        axis=1,
-    )
-    bias_sums = lax.psum_scatter(bias_terms, "dp", scatter_dimension=0, tiled=True)[0]
-    s_bq, s_bo, s_bu, s_bd = jnp.split(bias_sums, cuts)
+    s_wq = f_wq.astype(f32).reshape(4, own_rows, 3, quarter).transpose(1, 2, 0, 3).reshape(own_rows, 3 * width)
+    s_wo = f_wo.astype(f32).transpose(1, 0, 2).reshape(own_rows, width)
+    s_wu = f_wu.astype(f32).reshape(4, own_rows, n, units).transpose(1, 2, 0, 3).reshape(own_rows, ff)
+    s_wd = f_wd.astype(f32).reshape(4 * units, width)
+    qw, fq = 3 * quarter, ff // 4
+    bq = f_b[:, 0, :qw].reshape(4, 3, quarter).transpose(1, 0, 2).reshape(-1)
+    bu = f_b[:, 0, qw : qw + fq].reshape(4, n, units).transpose(1, 0, 2).reshape(-1)
+    bo = jnp.sum(f_b[:, 0, qw + fq : qw + fq + width], axis=0)
+    bd = jnp.sum(f_b[:, 0, qw + fq + width :], axis=0)
+
+    def own(value, like):
+        size = like.shape[0]
+        return lax.dynamic_slice_in_dim(value, dp_rank * size, size, 0)
+
     return (
-        block_out,
-        grad_input,
-        grad_time,
-        s_wq,
-        s_bq,
-        s_wo,
-        s_bo,
-        s_wu,
-        s_bu,
-        s_wd,
-        s_bd,
-        g_wm,
-        g_bm,
+        block_out, grad_input, grad_time.reshape(1, width), s_wq, own(bq, b_qkv), s_wo, own(bo, b_out), s_wu,
+        own(bu, b_up), s_wd, own(bd, b_down), gwm, own(gbm[0], b_mod),
     )
 
 

time: 572 us -> 268 us (0.47); the launches traced: 562 us -> 268 us
  blocking collectives: 150 us -> 0 us
  matrix products: 128 us -> 0 us
  Pallas kernels: 138 us -> 234 us
  waiting for transfers between devices: 70.5 us -> 0 us
  other arithmetic: 29.6 us -> 12.5 us
  between operations: 15.1 us -> 0.82 us
  starting transfers between devices: 5.93 us -> 0 us
    dot_general x18 -> x0, matrix products: 128 us -> none  [the longest x2 46.5 us: attend_back(): jnp.einsum('hqk,qhe->khe', d_scores, query_blk, preferred_element_type=jn...]
    all_gather x8 -> x0, blocking collectives: 102 us -> none  [the longest x2 61.4 us: dp_gather(): return lax.all_gather(value, 'dp', axis=0, tiled=True)]
    pallas_call x0 -> x1, Pallas kernels: none -> 96.2 us  [run_b(): pl.pallas_call(functools.partial(kernel_b, n), out_shape=outs, in_specs=[...]
    reduce_scatter x7 -> x0, waiting for transfers between devices: 69.8 us -> none  [the longest x2 49 us: seq_reduce(): lax.psum_scatter(value.astype(jnp.bfloat16), 'seq', scatter_dimension=0,...]
    unnamed x1 -> x0, blocking collectives: 37.6 us -> none
    psum x1 -> x0, blocking collectives: 10.3 us -> none  [per_device(): mod_sum = lax.psum(mod_part, 'seq')]
    reduce_sum x8 -> x1, other arithmetic: 10.5 us -> 0.77 us  [per_device(): bd = jnp.sum(f_b[:, 0, qw + fq + width:], axis=0)]
  transfers between devices with their start and end apart: 8 -> 0, of which waited for: 3 -> 0; matrix products, arithmetic and copies ran while one was open for 28% -> 0% of each run, Pallas kernels for 0% -> 0%
where the time goes in v3:
time: 268 us
  Pallas kernels  234 us (87%)
  local copies, waits for them, and re-layouts  20.5 us (8%)
  other arithmetic  12.5 us (5%)
    pallas_call x1, Pallas kernels, run_a(): pl.pallas_call(functools.partial(kernel_a, n), out_shape=outs, in_specs=[...  138 us
    pallas_call x1, Pallas kernels, run_b(): pl.pallas_call(functools.partial(kernel_b, n), out_shape=outs, in_specs=[...  96.2 us
    unnamed x23, local copies, waits for them, and re-layouts  11 us

profile of v3, /device:TPU:0, one launch (start us, length us, event | category | flops | bytes accessed | tf_op | source)
XLA Modules:
  0.0 267.9 jit_solution(11115958776284226199)
XLA Ops:
  0.6 0.8 select_reduce_fusion.2
  1.4 0.7 fusion.5
  2.1 1.3 bitcast_convert_fusion.1.tcols
  3.4 0.7 convert_dynamic-update-slice_fusion.3
  4.1 0.7 convert_dynamic-update-slice_fusion.4
  4.9 0.1 select_reduce_fusion
  5.0 0.0 copy-start.5
  5.0 0.8 convert_dynamic-update-slice_fusion.2
  5.8 0.1 reshape.141
  5.9 0.1 reshape.142
  6.0 0.8 convert_dynamic-update-slice_fusion.1
  6.8 0.6 reshape.143.bias
  7.4 0.8 convert_dynamic-update-slice_fusion
  8.2 0.6 constant_dynamic-slice_fusion.1.bm
  8.8 1.0 copy.58.idc
  9.8 1.3 copy.56
  11.2 0.8 copy.57.wu_own
  11.9 3.0 %fusion = (f32[1024,128]{1,0:T(8,128)}, f32[1024,128]{1,0:T(8,128)}) fusion(f32[128]{0:T(128)S(1)} %get-tuple-element.120, f32[128]{0:T(128)S(1)} %get-tuple-element.121, f32[1024]{0:T(1024)S(1)} %subtract_convert_fusion), kind=kLoop, calls=%fused_computation.2 | loop fusion | flops 262144 | bytes 1053696 | tf_op jit(solution)/shard_map/mul | solution.py:887
  15.0 0.0 copy-done.5
  15.0 137.8 %shard_map.237 = (bf16[4,256,1024]{2,1,0:T(8,128)(2,1)}, bf16[1024,256]{1,0:T(8,128)(2,1)}, bf16[1024,256]{1,0:T(8,128)(2,1)}, bf16[1024,256]{1,0:T(8,128)(2,1)}...) custom-call(f32[256,1024]{1,0:T(8,128)} %frames.3, ...), custom_call_target="tpu_custom_call" | custom-call | tf_op jit(solution)/shard_map/pallas_call | solution.py:547
  152.8 96.2 %shard_map.238 = (f32[256,1024]{1,0:T(8,128)}, f32[256,1024]{1,0:T(8,128)}, f32[8,1,128]{2,1,0:T(1,128)}, f32[128,6144]{1,0:T(8,128)}, f32[1,6144]{1,0:T(1,128)}...) custom-call(f32[256,1024]{1,0:T(8,128)} %frames.3, ...), custom_call_target="tpu_custom_call" | custom-call | tf_op jit(solution)/shard_map/pallas_call | solution.py:856
  249.0 0.0 copy-start.4
  249.0 1.3 dynamic-slice_reduce_fusion.1
  250.4 0.7 slice_reduce_fusion.2
  251.1 0.1 reshape_squeeze.7
  251.2 0.1 reshape.156
  251.3 0.6 dynamic_slice.39
  251.9 0.8 slice_reduce_fusion
  252.7 0.7 slice.12
  253.4 0.7 dynamic_slice.37
  254.1 0.6 dynamic_slice.40
  254.7 0.6 dynamic_slice.38
  255.2 1.0 convert_bitcast_fusion
  256.2 0.2 copy.63
  256.4 1.0 copy.68
  257.4 0.0 copy-done.4
  257.4 0.2 copy.64
  257.6 0.0 copy-start.3
  257.6 0.1 copy.65
  257.8 0.0 copy-start.2
  257.8 1.3 copy.69
  259.1 0.0 copy-done.3
  259.1 1.1 bitcast_convert_fusion
  260.2 0.0 copy-done.2
  260.2 0.3 copy.60
  260.5 0.1 copy.61
  260.6 0.0 copy-start.1
  260.6 1.6 copy.67
  262.2 0.0 copy-start.6
  262.2 0.0 copy-start
  262.2 2.5 copy.82
  264.7 0.0 copy-done.1
  264.7 1.0 copy.83
  265.6 0.0 copy-done.6
  265.6 0.6 copy.84
  266.2 0.0 copy-done
  266.2 1.7 copy.85
  (17 shorter events, 0.2 us)
Async XLA Ops:
  5.0 10.0 %copy-start.5 = (s32[1024]{0:T(1024)}, s32[1024]{0:T(1024)S(1)}, u32[]{:S(2)}) copy-start(s32[1024]{0:T(1024)S(1)} %get-tuple-element.116) | copy-start | bytes 12292
  249.0 8.4 %copy-start.4 = (bf16[4,128,512]{2,1,0:T(8,128)(2,1)S(1)}, bf16[4,128,512]{2,1,0:T(8,128)(2,1)}, u32[]{:S(2)}) copy-start(bf16[4,128,512]{2,1,0:T(8,128)(2,1)} %get-tuple-element.71) | copy-start | bytes 1572868
  257.6 1.4 copy-start.3
  257.8 2.4 copy-start.2
  260.6 4.1 %copy-start.1 = (f32[256,1024]{1,0:T(8,128)S(1)}, f32[256,1024]{1,0:T(8,128)}, u32[]{:S(2)}) copy-start(f32[256,1024]{1,0:T(8,128)} %get-tuple-element.136) | copy-start | bytes 3145732
  262.2 3.4 %copy-start.6 = (f32[8,1,128]{2,1,0:T(1,128)S(1)}, f32[8,1,128]{2,1,0:T(1,128)}, u32[]{:S(2)}) copy-start(f32[8,1,128]{2,1,0:T(1,128)} %get-tuple-element.67) | copy-start | bytes 12292
  262.2 4.0 %copy-start = (f32[128,6144]{1,0:T(8,128)S(1)}, f32[128,6144]{1,0:T(8,128)}, u32[]{:S(2)}) copy-start(f32[128,6144]{1,0:T(8,128)} %get-tuple-element.146) | copy-start | bytes 9437188

commit v4 on v2

v4 whole, which is shorter than its diff:
```python
import functools
import math

import jax
import jax.numpy as jnp
from jax import lax
from jax.experimental import pallas as pl
from jax.experimental.pallas import tpu as pltpu
from jax.sharding import PartitionSpec as P

HEADS = 16
MESH = pl.DeviceIdType.MESH
f32 = jnp.float32
bf16 = jnp.bfloat16
norm_eps = 1e-06


def nn(left_side, right_side):
    return lax.dot_general(left_side, right_side, (((1,), (0,)), ((), ())), preferred_element_type=f32)


def nt(left_side, right_side):
    return lax.dot_general(left_side, right_side, (((1,), (1,)), ((), ())), preferred_element_type=f32)


def merged(ref):
    shape = ref.shape
    return ref[...].reshape(shape[0] * shape[1], shape[2])


def swap_halves(values, lane):
    up = pltpu.roll(values, 96, 1)
    down = pltpu.roll(values, 32, 1)
    return jnp.where(lane % 64 < 32, up, down)


def gelu_both(h):
    c = math.sqrt(2.0 / math.pi)
    h2 = h * h
    t = jnp.tanh(c * h * (1.0 + 0.044715 * h2))
    half = 0.5 * (1.0 + t)
    return h * half, half + 0.5 * h * (1.0 - t * t) * (c * (1.0 + 3.0 * 0.044715 * h2))


def normed(values):
    mean_val = jnp.mean(values, axis=-1, keepdims=True)
    centred = values - mean_val
    rstd = lax.rsqrt(jnp.mean(centred * centred, axis=-1, keepdims=True) + norm_eps)
    return centred * rstd, rstd


def norm_back(e, n, rstd):
    return (e - jnp.mean(e, axis=-1, keepdims=True) - n * jnp.mean(e * n, axis=-1, keepdims=True)) * rstd


class Links:
    def __init__(self, n, send, recv):
        self.n = n
        self.d = lax.axis_index("dp")
        self.s = lax.axis_index("seq")
        d, s = self.d, self.s
        self.px = d + 1 - 2 * (d % 2)
        self.s1 = s + 1 - 2 * (s % 2)
        self.s2 = (s + 2) % 4
        self.s3 = 3 - s
        self.send, self.recv = send, recv
        self.n_send = self.n_recv = 0

    def sems(self, sends, recvs):
        base = (self.n_send, self.n_recv)
        self.n_send += sends
        self.n_recv += recvs
        return base

    def block(self, i):
        s = self.s
        return (s % 2 + i % 2) % 2 + 2 * ((s // 2 + i // 2) % 2)

    def copy(self, src, dst, si, ri, dev):
        return pltpu.make_async_remote_copy(
            src_ref=src, dst_ref=dst, send_sem=self.send.at[si], recv_sem=self.recv.at[ri],
            device_id=dev, device_id_type=MESH,
        )

    def barrier(self):
        b = pltpu.get_barrier_semaphore()
        for k in range(1, self.n):
            pl.semaphore_signal(b, inc=1, device_id=((self.d + k) % self.n, self.s), device_id_type=MESH)
        for t in (self.s1, self.s2, self.s3):
            pl.semaphore_signal(b, inc=1, device_id=(self.d, t), device_id_type=MESH)
        pl.semaphore_wait(b, self.n + 2)


class ToAll:
    def __init__(self, links, src, buf):
        self.l, self.src, self.buf = links, src, buf
        self.si, self.ri = links.sems(links.n, links.n)

    def _to(self, k):
        l = self.l
        peer = (l.d + k) % l.n
        return l.copy(self.src(peer), self.buf.at[l.d], self.si + k, self.ri + l.d, (peer, l.s))

    def start(self):
        for k in range(1, self.l.n):
            self._to(k).start()

    def wait_recv(self):
        l = self.l
        for k in range(1, l.n):
            peer = (l.d + k) % l.n
            l.copy(self.buf.at[peer], self.buf.at[peer], self.si + k, self.ri + peer, (peer, l.s)).wait_recv()

    def wait_send(self):
        for k in range(1, self.l.n):
            self._to(k).wait_send()


class SeqAll:
    def __init__(self, links, buf):
        self.l, self.buf = links, buf
        self.si, self.ri = links.sems(4, 4)

    def _to(self, k):
        l = self.l
        t = l.block(k)
        return l.copy(self.buf.at[l.s], self.buf.at[l.s], self.si + k, self.ri + l.s, (l.d, t))

    def start(self):
        for k in (2, 3, 1):
            self._to(k).start()

    def wait_recv(self):
        l = self.l
        for k in (1, 2, 3):
            t = l.block(k)
            l.copy(self.buf.at[t], self.buf.at[t], self.si + k, self.ri + t, (l.d, t)).wait_recv()

    def wait_send(self):
        for k in (1, 2, 3):
            self._to(k).wait_send()


class DpGather:
    def __init__(self, links, buf):
        self.l, self.buf = links, buf
        self.si, self.ri = links.sems(links.n, links.n)
        self.half = links.n // 2

    def _z(self, k):
        l = self.l
        return l.copy(self.buf.at[l.d], self.buf.at[l.d], self.si + k, self.ri + l.d, ((l.d + 2 * k) % l.n, l.s))

    def _x(self, k):
        l = self.l
        r = (l.d + 2 * k) % l.n
        return l.copy(self.buf.at[r], self.buf.at[r], self.si + self.half + k, self.ri + r, (l.px, l.s))

    def start(self):
        for k in range(1, self.half):
            self._z(k).start()
        self._x(0).start()

    def hand_on(self):
        l = self.l
        for k in range(1, self.half):
            r = (l.d + 2 * k) % l.n
            l.copy(self.buf.at[r], self.buf.at[r], self.si, self.ri + r, (r, l.s)).wait_recv()
            self._x(k).start()

    def wait_rest(self):
        l = self.l
        for k in range(self.half):
            r = (l.px + 2 * k) % l.n
            l.copy(self.buf.at[r], self.buf.at[r], self.si, self.ri + r, (l.px, l.s)).wait_recv()

    def wait_send(self):
        for k in range(1, self.half):
            self._z(k).wait_send()
        for k in range(self.half):
            self._x(k).wait_send()


class SeqGather:
    def __init__(self, links, buf):
        self.l, self.buf = links, buf
        self.si, self.ri = links.sems(3, 4)

    def _c(self, slot, k, t):
        l = self.l
        return l.copy(self.buf.at[slot], self.buf.at[slot], self.si + k, self.ri + slot, (l.d, t))

    def start(self):
        l = self.l
        self._c(l.s, 0, l.s2).start()
        self._c(l.s, 1, l.s1).start()

    def hand_on(self):
        l = self.l
        self.wait(l.s2)
        self._c(l.s2, 2, l.s1).start()

    def wait(self, slot):
        l = self.l
        l.copy(self.buf.at[slot], self.buf.at[slot], self.si, self.ri + slot, (l.d, l.s1)).wait_recv()

    def wait_send(self):
        l = self.l
        self._c(l.s, 0, l.s2).wait_send()
        self._c(l.s, 1, l.s1).wait_send()
        self._c(l.s2, 2, l.s1).wait_send()


class SeqSwap:
    def __init__(self, links, out, into):
        self.l, self.out, self.into = links, out, into
        self.si, self.ri = links.sems(4, 4)

    def copy_to(self, i):
        l = self.l
        t = l.block(i)
        return l.copy(self.out.at[t], self.into.at[l.s], self.si + i, self.ri + l.s, (l.d, t))

    def wait_one(self, i):
        l = self.l
        t = l.block(i)
        l.copy(self.into.at[t], self.into.at[t], self.si + i, self.ri + t, (l.d, t)).wait_recv()

    def wait_recv(self):
        l = self.l
        for i in (1, 2, 3):
            t = l.block(i)
            l.copy(self.into.at[t], self.into.at[t], self.si + i, self.ri + t, (l.d, t)).wait_recv()

    def wait_send(self):
        for i in (1, 2, 3):
            self.copy_to(i).wait_send()


class SeqSum:
    def __init__(self, links, held):
        self.l, self.held = links, held
        self.si, self.ri = links.sems(3, 3)

    def _c(self, k, t):
        l = self.l
        return l.copy(self.held.at[k], self.held.at[3 + k], self.si + k, self.ri + k, (l.d, t))

    def far(self, term):
        l, held = self.l, self.held
        held[0] = term(l.s3).astype(bf16)
        self._c(0, l.s1).start()
        mine = term(l.s2)
        self._c(0, l.s1).wait_recv()
        held[1] = (mine + held[3].astype(f32)).astype(bf16)
        self._c(1, l.s2).start()

    def near(self, term):
        l = self.l
        self.held[2] = term(l.s1).astype(bf16)
        self._c(2, l.s1).start()

    def total(self, mine):
        l, held = self.l, self.held
        self._c(2, l.s1).wait_recv()
        self._c(1, l.s2).wait_recv()
        return mine + held[5].astype(f32) + held[4].astype(f32)

    def wait_send(self):
        l = self.l
        self._c(0, l.s1).wait_send()
        self._c(1, l.s2).wait_send()
        self._c(2, l.s1).wait_send()


def tn(left_side, right_side):
    return lax.dot_general(left_side, right_side, (((0,), (0,)), ((), ())), preferred_element_type=f32)


class SlotGather:
    def __init__(self, links, buf):
        self.l, self.buf = links, buf
        self.half = links.n // 2
        self.si, self.ri = links.sems(3 * links.n, 3 * links.n)

    def _c(self, block, r, kind, t):
        l = self.l
        at = kind * l.n + r
        return l.copy(self.buf.at[block, r], self.buf.at[block, r], self.si + at, self.ri + at, (l.d, t))

    def _each(self, base, body):
        def one(k, carry):
            body((base + 2 * k) % self.l.n)
            return carry

        lax.fori_loop(0, self.half, one, 0)

    def send(self, base):
        l = self.l

        def body(r):
            self._c(l.s, r, 0, l.s2).start()
            self._c(l.s, r, 1, l.s1).start()

        self._each(base, body)

    def hand_on(self, base):
        l = self.l

        def body(r):
            self._c(l.s2, r, 0, l.s2).wait_recv()
            self._c(l.s2, r, 2, l.s1).start()

        self._each(base, body)

    def wait_rest(self):
        l = self.l

        def one(r, carry):
            self._c(l.s1, r, 1, l.s1).wait_recv()
            self._c(l.s3, r, 2, l.s1).wait_recv()
            return carry

        lax.fori_loop(0, l.n, one, 0)

    def wait_send(self):
        l = self.l

        def one(r, carry):
            self._c(l.s, r, 0, l.s2).wait_send()
            self._c(l.s, r, 1, l.s1).wait_send()
            self._c(l.s2, r, 2, l.s1).wait_send()
            return carry

        lax.fori_loop(0, l.n, one, 0)


class DpSum:
    def __init__(self, links, g, xin, zin):
        self.l, self.g, self.xin, self.zin = links, g, xin, zin
        self.half = links.n // 2
        self.si, self.ri = links.sems(links.n, links.n)

    def _x(self, t):
        l = self.l
        h = t // 2
        return l.copy(self.g.at[t], self.xin.at[h], self.si + h, self.ri + h, (l.px, l.s))

    def _z(self, k):
        l = self.l
        t = (l.d + 2 * k) % l.n
        at = self.half + k
        return l.copy(self.g.at[t], self.zin.at[k], self.si + at, self.ri + at, (t, l.s))

    def send_x(self, first, count):
        for i in range(count // 2):
            self._x(first + 2 * i + self.l.px % 2).start()

    def fold(self):
        l = self.l

        def one(k, carry):
            t = (l.d + 2 * k) % l.n
            h = t // 2
            l.copy(self.xin.at[h], self.xin.at[h], self.si, self.ri + h, (l.px, l.s)).wait_recv()
            self.g[t] = (self.g[t].astype(f32) + self.xin[h].astype(f32)).astype(bf16)
            self._z(k).start()
            return carry

        lax.fori_loop(1, self.half, one, 0)

    def total(self):
        l = self.l
        h = l.d // 2
        l.copy(self.xin.at[h], self.xin.at[h], self.si, self.ri + h, (l.px, l.s)).wait_recv()
        out = self.g[l.d].astype(f32) + self.xin[h].astype(f32)
        for k in range(1, self.half):
            self._z(k).wait_recv()
            out = out + self.zin[k].astype(f32)
        return out

    def wait_send(self):
        l = self.l
        for k in range(self.half):
            self._x((l.px + 2 * k) % l.n).wait_send()
        for k in range(1, self.half):
            self._z(k).wait_send()


def whole_kernel(
    n,
    lengths, frames, cot, time_row, bm, bias, wu_own, wm_hbm, wq_hbm, wo_hbm, wd_hbm,
    block_out, grad_input, grad_time, tbuf, ebuf, lbuf, f_q0, f_q1, f_wo, f_wu, f_wd, f_b,
    wm, wq, wu, wd, wo, tsrc, psend, pbuf, bbuf, mod, n_in, attn_branch, n_mid, cos, sin, idc, idr,
    xa, dffn, xf, q, k, v, kt, vt, lse, ao_out, ao, do_out, gh, gelu, dhid, dattn, fsum, dk, dv, dproj,
    held, held_f, held_o, g_q0, x_q0, z_q0, g_q1, x_q1, z_q1, g_wo, x_wo, z_wo, g_wu, x_wu, z_wu, g_wd, x_wd, z_wd,
    em, lm, eb, ebb, lb, lbb, dts, dtb,
    send, recv, local,
):
    l = Links(n, send, recv)
    d, s = l.d, l.s
    rows, width = frames.shape
    item = 4 * rows
    quarter = width // 4
    own_rows = wm.shape[0]
    mq = bm.shape[1]
    units = wd.shape[1]
    ff_q = wu.shape[2]
    pairs = quarter // 128
    qw = 3 * quarter
    pw = qw // pairs
    lane = lax.broadcasted_iota(jnp.int32, (rows, 128), 1)
    take = [
        pltpu.make_async_copy(wm_hbm, wm, local.at[0]),
        pltpu.make_async_copy(wd_hbm.at[pl.ds(pl.multiple_of(s * units, 8), units), :], wd.at[d], local.at[1]),
        pltpu.make_async_copy(wo_hbm.at[:, pl.ds(pl.multiple_of(s * quarter, 128), quarter)], wo.at[s, d], local.at[2]),
    ] + [
        pltpu.make_async_copy(
            wq_hbm.at[:, pl.ds(pl.multiple_of(j * width + s * quarter + 128 * p, 128), 128)],
            wq.at[d, :, pl.ds(p * pw + 128 * j, 128)], local.at[3 + 3 * p + j],
        )
        for p in range(pairs) for j in range(3)
    ]
    for c in take:
        c.start()
    times = ToAll(l, lambda peer: tsrc.at[peer], tbuf)
    parts = ToAll(l, lambda peer: psend.at[peer], pbuf)
    biases = ToAll(l, lambda peer: bias.at[0], bbuf)
    mods = SeqAll(l, mod)
    a_wq, a_wu, a_wd, a_wo = DpGather(l, wq), DpGather(l, wu), DpGather(l, wd), DpGather(l, wo.at[s])
    s_xa, s_df, s_xf, s_wo = SeqGather(l, xa), SeqGather(l, dffn), SeqGather(l, xf), SlotGather(l, wo)
    w_ao, w_do = SeqSwap(l, ao_out, ao), SeqSwap(l, do_out, gh)
    sum_x, sum_f, sum_o, sum_a = SeqSum(l, held), SeqSum(l, held_f), SeqSum(l, held_o), SeqSum(l, held)
    d_q0, d_q1, d_wo, d_wu, d_wd = (
        DpSum(l, g_q0, x_q0, z_q0), DpSum(l, g_q1, x_q1, z_q1), DpSum(l, g_wo, x_wo, z_wo),
        DpSum(l, g_wu, x_wu, z_wu), DpSum(l, g_wd, x_wd, z_wd),
    )
    o_q0, o_q1, o_wo, o_wu, o_wd = (
        SeqGather(l, f_q0), SeqGather(l, f_q1), SeqGather(l, f_wo), SeqGather(l, f_wu), SeqGather(l, f_wd)
    )
    e_mod, l_mod, o_b = SeqAll(l, em), SeqAll(l, lm), SeqAll(l, f_b)
    e_all, l_all = ToAll(l, lambda peer: ebuf.at[d], ebuf), ToAll(l, lambda peer: lbuf.at[d], lbuf)
    eb_all, lb_all = ToAll(l, lambda peer: eb, ebb), ToAll(l, lambda peer: lb, lbb)
    t_all = ToAll(l, lambda peer: dts.at[peer], dtb)

    def at_rows(b):
        return pl.ds(pl.multiple_of(b * rows, rows), rows)

    tv = time_row[...]
    act = (tv / (1.0 + jnp.exp(-tv))).astype(bf16).astype(f32)
    for i in range(n):
        tsrc[i] = act[:, i * own_rows : (i + 1) * own_rows]
    dffn[s] = cot[...].astype(bf16)
    for c in take[3:]:
        c.wait()
    l.barrier()
    times.start()
    a_wq.start()
    s_df.start()
    biases.start()
    tbuf[d] = tsrc[d]
    wu[d] = wu_own[...]
    for c in take[:3]:
        c.wait()
    n_in[...] = normed(frames[...])[0]
    times.wait_recv()
    lhs = jnp.concatenate([tbuf[i] for i in range(n)], axis=0).astype(bf16)
    part = nn(lhs, wm[:, pl.ds(pl.multiple_of(s * mq, 128), mq)]) + bm[...]
    for i in range(n):
        psend[i] = part[i : i + 1]
    parts.start()
    total = psend[d]
    parts.wait_recv()
    for j in range(1, n):
        total = total + pbuf[(d + j) % n]
    mod[s] = total
    mods.start()
    mods.wait_recv()
    flat = jnp.concatenate([mod[i] for i in range(4)], axis=1)
    shift_a, scale_a, gate_a, shift_f, scale_f, gate_f = (
        flat[:, i * width : (i + 1) * width] for i in range(6)
    )
    xa[s] = (n_in[...] * (1.0 + scale_a) + shift_a).astype(bf16)
    s_xa.start()

    def places(shape, dim):
        at = lax.broadcasted_iota(jnp.int32, shape, dim)
        number, first, end = jnp.zeros(shape, jnp.int32), jnp.zeros(shape, jnp.int32), 0
        for c in range(lengths.shape[1] - 1):
            end = end + lengths[0, c]
            past = at >= end
            number = number + jnp.where(past, 1, 0)
            first = jnp.where(past, end, first)
        return number, at - first

    idr[...] = places((1, item), 1)[0]
    number, position = places((item, 1), 0)
    idc[...] = number
    lanes = lax.broadcasted_iota(jnp.int32, (1, 128), 1)
    rate = jnp.exp((lanes % 32).astype(f32) * (-2.0 * math.log(10000.0) / 64))
    phase = position.astype(f32) * rate
    cos[...] = jnp.cos(phase)
    sin[...] = jnp.where(lanes % 64 < 32, -1.0, 1.0) * jnp.sin(phase)

    a_wq.hand_on()
    a_wo.start()
    s_df.hand_on()
    a_wq.wait_rest()
    biases.wait_recv()
    own_bias = bias[0]
    for j in range(1, n):
        own_bias = own_bias + bbuf[(d + j) % n]
    bq = own_bias[:, :qw]
    bo = own_bias[:, qw : qw + width]
    bu = own_bias[:, qw + width : qw + width + ff_q]
    bd = own_bias[:, qw + width + ff_q :]

    def project(i, carry):
        @pl.when(i == 1)
        def _():
            s_xa.wait(l.s1)
            a_wu.start()

        @pl.when(i == 2)
        def _():
            s_xa.hand_on()
            a_wd.start()

        @pl.when(i == 3)
        def _():
            s_xa.wait(l.s3)

        b = l.block(i)
        at = at_rows(b)
        pr = nn(xa[b], merged(wq)) + bq
        cb, sb = cos[at, :], sin[at, :]
        for p in range(pairs):
            c0 = 128 * p
            qp, kp, vp = (pr[:, p * pw + 128 * j : p * pw + 128 * j + 128] for j in range(3))
            vp = vp.astype(bf16)
            qp = (qp * cb + swap_halves(qp, lane) * sb).astype(bf16)
            kp = (kp * cb + swap_halves(kp, lane) * sb).astype(bf16)
            q[at, c0 : c0 + 128] = qp * jnp.bfloat16(0.125)
            k[at, c0 : c0 + 128] = kp
            v[at, c0 : c0 + 128] = vp
            kt[p, :, at] = jnp.transpose(kp.astype(f32)).astype(bf16)
            vt[p, :, at] = jnp.transpose(vp.astype(f32)).astype(bf16)
        return carry

    lax.fori_loop(0, 4, project, 0)
    a_wo.hand_on()
    s_wo.send(d)

    def attend(j, carry):
        i = (j + 2) % 4
        b = l.block(i)
        at = at_rows(b)
        same = idc[...] == idr[:, at]
        for p in range(pairs):
            qp, kp = q[at, 128 * p : 128 * p + 128], k[:, 128 * p : 128 * p + 128]
            outs = []
            for h in range(2):
                qm = jnp.where((lane < 64) == (h == 0), qp, jnp.zeros_like(qp))
                sc = jnp.where(same, nt(kp, qm), -1e30)
                top = jnp.max(sc, axis=0, keepdims=True)
                ex = jnp.exp(sc - top)
                su = jnp.sum(ex, axis=0, keepdims=True)
                lse[2 * p + h, :, at] = top + jnp.log(su)
                pt = (ex * (1.0 / su)).astype(bf16)
                outs.append(nn(vt[p, 64 * h : 64 * h + 64, :], pt))
            ao_out[b, :, 128 * p : 128 * p + 128] = jnp.transpose(jnp.concatenate(outs, axis=0)).astype(bf16)

        @pl.when(j != 2)
        def _():
            w_ao.copy_to(i).start()

        @pl.when(j == 0)
        def _():
            a_wo.wait_rest()
            s_wo.send(l.px)

        @pl.when(j == 1)
        def _():
            s_wo.hand_on(d)

        @pl.when(j == 2)
        def _():
            ao[s] = ao_out[s]
            a_wu.hand_on()

        @pl.when(j == 3)
        def _():
            s_wo.hand_on(l.px)

        return carry

    lax.fori_loop(0, 4, attend, 0)
    s_wo.wait_rest()
    w_ao.wait_recv()
    left = jnp.concatenate([ao[i] for i in range(4)], axis=1)
    for c in range(4):
        cs = slice(c * quarter, (c + 1) * quarter)
        attn_branch[:, cs] = nn(left, merged(wo.at[c])) + bo[:, cs]
    xm = frames[...] + gate_a * attn_branch[...]
    block_out[...] = xm
    nm, rstd = normed(xm)
    n_mid[...] = nm
    xf[s] = (nm * (1.0 + scale_f) + shift_f).astype(bf16)
    s_xf.start()
    a_wd.hand_on()
    s_df.wait(l.s1)
    s_df.wait(l.s3)
    s_df.wait_send()
    for b in range(4):
        dffn[b] = (gate_f * dffn[b].astype(f32)).astype(bf16)
    a_wu.wait_rest()
    a_wd.wait_rest()

    def hidden_term(b):
        return nt(dhid[at_rows(b), :], merged(wu))

    def ffn_term(b):
        return nn(gelu[at_rows(b), :], merged(wd))

    def out_term(t):
        part = dattn[:, pl.ds(pl.multiple_of(t * quarter, 128), quarter)]
        return jnp.concatenate([tn(ao[i], part) for i in range(4)], axis=0)

    def xa_term(b):
        return nt(dproj[at_rows(b), :], merged(wq))

    def feed(i, carry):
        @pl.when(i == 1)
        def _():
            s_xf.wait(l.s1)

        @pl.when(i == 2)
        def _():
            sum_x.near(hidden_term)
            s_xf.hand_on()

        @pl.when(i == 3)
        def _():
            s_xf.wait(l.s3)

        b = l.block(i)
        at = at_rows(b)
        act, slope = gelu_both(nn(xf[b], merged(wu)) + bu)
        gelu[at, :] = act.astype(bf16)
        dhid[at, :] = (nt(dffn[b], merged(wd)) * slope).astype(bf16)
        return carry

    lax.fori_loop(0, 4, feed, 0)
    sum_x.far(hidden_term)

    def make(left_of, right, g, chain, each):
        per = 256 // each

        def one(m, carry):
            val = tn(left_of(m), right()).astype(bf16)
            g[pl.ds(m * per, per)] = val.reshape(per, each, val.shape[1])
            chain.send_x(m * per, per)
            return carry

        lax.fori_loop(0, n // per, one, 0)

    def cols_of(ref, m):
        return ref[:, :, pl.ds(pl.multiple_of(m * 256, 256), 256)].reshape(item, 256)

    make(lambda m: gelu[:, pl.ds(pl.multiple_of(m * 256, 256), 256)], lambda: merged(dffn), g_wd, d_wd, units)
    make(lambda m: cols_of(xf, m), lambda: dhid[...], g_wu, d_wu, own_rows)
    eb[:, :ff_q] = jnp.sum(dhid[...].astype(f32), axis=0, keepdims=True)
    eb[:, ff_q + width :] = jnp.sum(dffn[s].astype(f32), axis=0, keepdims=True)
    dk[...] = jnp.zeros_like(dk)
    dv[...] = jnp.zeros_like(dv)
    g = sum_x.total(hidden_term(s))
    nm = n_mid[...]
    fsum[0:1, :] = jnp.sum(g, axis=0, keepdims=True)
    fsum[1:2, :] = jnp.sum(g * nm, axis=0, keepdims=True)
    dm = cot[...] + norm_back(g * (1.0 + scale_f), nm, normed(block_out[...])[1])
    grad_input[...] = dm
    dattn[...] = (gate_a * dm).astype(bf16)
    per4 = n // 4

    def give(j, carry):
        i = (j + 2) % 4
        t = l.block(i)
        out = None
        for c in range(4):
            wt = wo[c, pl.ds(t * per4, per4)].reshape(quarter, quarter)
            o = nt(dattn[:, c * quarter : (c + 1) * quarter], wt)
            out = o if out is None else out + o
        do_out[t] = out.astype(bf16)

        @pl.when(j != 2)
        def _():
            w_do.copy_to(i).start()

        @pl.when(j == 2)
        def _():
            gh[s] = do_out[s]

        return carry

    lax.fori_loop(0, 4, give, 0)
    fsum[2:3, :] = jnp.sum(dm * attn_branch[...], axis=0, keepdims=True)
    eb[:, ff_q : ff_q + width] = jnp.sum(dattn[...].astype(f32), axis=0, keepdims=True)
    eb_all.start()

    def turned(values, at):
        val = values.astype(bf16).astype(f32)
        return (val * cos[at, :] - swap_halves(val, lane) * sin[at, :]).astype(bf16)

    def back_pair(p, before, after):
        c0, base = 128 * p, p * pw

        def one(i, carry):
            before(i)
            b = l.block(i)
            at = at_rows(b)
            same = idc[...] == idr[:, at]
            kp, vp = k[:, c0 : c0 + 128], v[:, c0 : c0 + 128]
            qp, dop = q[at, c0 : c0 + 128], gh[b, :, c0 : c0 + 128]
            dqs = []
            for h in range(2):
                mine = (lane < 64) == (h == 0)
                qm = jnp.where(mine, qp, jnp.zeros_like(qp))
                dom = jnp.where(mine, dop, jnp.zeros_like(dop))
                pt = jnp.exp(jnp.where(same, nt(kp, qm), -1e30) - lse[2 * p + h, :, at])
                dpt = nt(vp, dom)
                mean = jnp.sum(dpt * pt, axis=0, keepdims=True)
                dst = (pt * (dpt - mean)).astype(bf16)
                dv[p] += nn(pt.astype(bf16), dom)
                dk[p] += nn(dst, qm)
                dqs.append(nn(kt[p, 64 * h : 64 * h + 64, :], dst))
            dq = jnp.transpose(jnp.concatenate(dqs, axis=0)) * 0.125
            dproj[at, base : base + 128] = turned(dq, at)
            after(i)
            return carry

        lax.fori_loop(0, 4, one, 0)

        def finish(b, carry):
            at = at_rows(b)
            dproj[at, base + 128 : base + 256] = turned(dk[p, at, :], at)
            dproj[at, base + 256 : base + 384] = dv[p, at, :].astype(bf16)
            return carry

        lax.fori_loop(0, 4, finish, 0)

    def before0(i):
        @pl.when(i == 1)
        def _():
            w_do.wait_one(1)

        @pl.when(i == 2)
        def _():
            w_do.wait_one(2)

        @pl.when(i == 3)
        def _():
            w_do.wait_one(3)

    def after0(i):
        @pl.when(i == 0)
        def _():
            d_wd.fold()

        @pl.when(i == 2)
        def _():
            sum_f.far(ffn_term)
            sum_f.near(ffn_term)

        @pl.when(i == 3)
        def _():
            d_wu.fold()

    def after1(i):
        @pl.when(i == 0)
        def _():
            sum_o.far(out_term)
            sum_o.near(out_term)

        @pl.when(i == 2)
        def _():
            ffn = sum_f.total(ffn_term(s)) + bd
            block_out[...] = block_out[...] + gate_f * ffn
            em[s, :, 3 * width :] = jnp.sum(cot[...] * ffn, axis=0, keepdims=True)
            em[s, :, :width] = fsum[2:3, :]
            em[s, :, width : 2 * width] = fsum[0:1, :]
            em[s, :, 2 * width : 3 * width] = fsum[1:2, :]
            e_mod.start()

        @pl.when(i == 3)
        def _():
            e_mod.wait_recv()
            ebuf[d] = (em[0] + em[1] + em[2] + em[3]).astype(bf16).astype(f32)
            e_all.start()

    back_pair(0, before0, after0)
    make(lambda m: cols_of(xa, m), lambda: dproj[:, :pw], g_q0, d_q0, own_rows)
    back_pair(1, lambda i: None, after1)
    sum_x.wait_send()
    sum_a.far(xa_term)
    make(lambda m: cols_of(xa, m), lambda: dproj[:, pw:], g_q1, d_q1, own_rows)
    sum_a.near(xa_term)
    d_q0.fold()
    g_wo[...] = sum_o.total(out_term(s)).astype(bf16).reshape(n, own_rows, quarter)
    d_wo.send_x(0, n)
    lb[...] = jnp.sum(dproj[...].astype(f32), axis=0, keepdims=True)
    lb_all.start()
    e_all.wait_recv()
    dm_e = jnp.concatenate([ebuf[i] for i in range(n)], axis=0).astype(bf16)
    dt = nt(dm_e, wm[:, 2 * width :])
    d_q1.fold()
    d_wo.fold()
    g = sum_a.total(xa_term(s))
    n_val = n_in[...]
    lm[s, :, :width] = jnp.sum(g, axis=0, keepdims=True)
    lm[s, :, width:] = jnp.sum(g * n_val, axis=0, keepdims=True)
    l_mod.start()
    f_wd[s] = d_wd.total().astype(bf16)
    o_wd.start()
    f_wu[s] = d_wu.total().astype(bf16)
    o_wu.start()
    grad_input[...] = grad_input[...] + norm_back(g * (1.0 + scale_a), n_val, normed(frames[...])[1])
    l_mod.wait_recv()
    lbuf[d] = (lm[0] + lm[1] + lm[2] + lm[3]).astype(bf16).astype(f32)
    l_all.start()
    eb_all.wait_recv()
    lb_all.wait_recv()
    esum, lsum = eb[...], lb[...]
    for j in range(1, n):
        esum = esum + ebb[(d + j) % n]
        lsum = lsum + lbb[(d + j) % n]
    f_b[s, :, :qw] = lsum
    f_b[s, :, qw:] = esum
    o_b.start()
    f_q0[s] = d_q0.total().astype(bf16)
    o_q0.start()
    l_all.wait_recv()
    dm_l = jnp.concatenate([lbuf[i] for i in range(n)], axis=0).astype(bf16)
    dt = dt + nt(dm_l, wm[:, : 2 * width])
    for i in range(n):
        dts[i] = dt[i : i + 1]
    t_all.start()
    f_wo[s] = d_wo.total().astype(bf16)
    o_wo.start()
    o_wd.hand_on()
    o_wu.hand_on()
    f_q1[s] = d_q1.total().astype(bf16)
    o_q1.start()
    o_q0.hand_on()
    o_wo.hand_on()
    t_all.wait_recv()
    dtb[d] = dts[d]
    sig = 1.0 / (1.0 + jnp.exp(-tv))
    slope = sig + tv * sig * (1.0 - sig)
    for i in range(n):
        at = slice(i * own_rows, (i + 1) * own_rows)
        grad_time[:, at] = dtb[i] * slope[:, at]
    o_q1.hand_on()
    for o in (o_q0, o_q1, o_wo, o_wu, o_wd):
        o.wait(l.s1)
        o.wait(l.s3)
    o_b.wait_recv()
    for c in (
        times, parts, biases, mods, a_wq, a_wu, a_wd, a_wo, s_xa, s_xf, s_wo, w_ao, w_do,
        sum_f, sum_o, sum_a, d_q0, d_q1, d_wo, d_wu, d_wd, o_q0, o_q1, o_wo, o_wu, o_wd, e_mod, l_mod, o_b,
        e_all, l_all, eb_all, lb_all, t_all,
    ):
        c.wait_send()


def run_whole(n, clip_len, frames, cot, time_embed, bm, bias, wu_own, w_mod, w_qkv, w_out, w_down):
    rows, width = frames.shape
    item, quarter, own_rows = 4 * rows, width // 4, width // n
    ff_q = w_down.shape[0] * n // 4
    units, heads, pairs = ff_q // n, quarter // 64, quarter // 128
    qw = 3 * quarter
    pw = qw // pairs
    S, V = jax.ShapeDtypeStruct, pltpu.VMEM
    bw = qw + ff_q + 2 * width
    outs = [
        S((rows, width), f32), S((rows, width), f32), S((1, width), f32), S((n, 1, own_rows), f32),
        S((n, 1, 4 * width), f32), S((n, 1, 2 * width), f32), S((4, own_rows, pw), bf16), S((4, own_rows, pw), bf16),
        S((4, own_rows, quarter), bf16), S((4, own_rows, ff_q), bf16), S((4, units, width), bf16), S((4, 1, bw), f32),
    ]

    def chain(a, b):
        return [V((n, a, b), bf16), V((n // 2, a, b), bf16), V((n // 2, a, b), bf16)]

    held = V((6, rows, width), bf16)
    scratch = (
        [
            V((own_rows, 6 * width), bf16), V((n, own_rows, qw), bf16), V((n, own_rows, ff_q), bf16), V((n, units, width), bf16),
            V((4, n, own_rows, quarter), bf16), V((n, 1, own_rows), f32), V((n, 1, 6 * quarter), f32),
            V((n, 1, 6 * quarter), f32), V((n, 1, bw), f32), V((4, 1, 6 * quarter), f32),
            V((rows, width), f32), V((rows, width), f32), V((rows, width), f32), V((item, 128), f32), V((item, 128), f32),
            V((item, 1), jnp.int32), V((1, item), jnp.int32),
            V((4, rows, width), bf16), V((4, rows, width), bf16), V((4, rows, width), bf16),
            V((item, quarter), bf16), V((item, quarter), bf16), V((item, quarter), bf16),
            V((pairs, 128, item), bf16), V((pairs, 128, item), bf16), V((heads, 1, item), f32),
        ]
        + [V((4, rows, quarter), bf16)] * 4
        + [
            V((item, ff_q), bf16), V((item, ff_q), bf16), V((rows, width), bf16), V((8, width), f32),
            V((pairs, item, 128), f32), V((pairs, item, 128), f32), V((item, qw), bf16),
            held, held, V((6, width, quarter), bf16),
        ]
        + chain(own_rows, pw) + chain(own_rows, pw) + chain(own_rows, quarter) + chain(own_rows, ff_q) + chain(units, width)
        + [
            V((4, 1, 4 * width), f32), V((4, 1, 2 * width), f32), V((1, ff_q + 2 * width), f32),
            V((n, 1, ff_q + 2 * width), f32), V((1, qw), f32), V((n, 1, qw), f32),
            V((n, 1, own_rows), f32), V((n, 1, own_rows), f32),
            pltpu.SemaphoreType.DMA((20 * n + 80,)), pltpu.SemaphoreType.DMA((20 * n + 90,)), pltpu.SemaphoreType.DMA((9,)),
        ]
    )
    vm = pl.BlockSpec(memory_space=pltpu.VMEM)
    hb = pl.BlockSpec(memory_space=pl.ANY)
    return pl.pallas_call(
        functools.partial(whole_kernel, n),
        out_shape=outs,
        in_specs=[pl.BlockSpec(memory_space=pltpu.SMEM)] + [vm] * 6 + [hb] * 4,
        out_specs=[vm] * len(outs),
        scratch_shapes=scratch,
        compiler_params=pltpu.CompilerParams(collective_id=0, has_side_effects=True, vmem_limit_bytes=63 << 20),
    )(clip_len, frames, cot, time_embed, bm, bias, wu_own, w_mod, w_qkv, w_out, w_down)


def per_device(
    frames, time_embed, clip_len, w_qkv, b_qkv, w_out, b_out, w_up, b_up, w_down, b_down, w_mod, b_mod, cotangent
):
    n = lax.axis_size("dp")
    seq_rank, dp_rank = lax.axis_index("seq"), lax.axis_index("dp")
    rows, width = frames.shape
    quarter = width // 4
    own_rows, ff = w_up.shape
    units = w_down.shape[0] // 4
    pairs = quarter // 128
    ff_q = ff // 4
    qw = 3 * quarter

    def placed(b):
        return lax.dynamic_update_slice(
            jnp.zeros((b.shape[0] * n,), f32), b.astype(f32), (dp_rank * b.shape[0],)
        )

    def mine(value, axis):
        return lax.dynamic_index_in_dim(value, seq_rank, axis, keepdims=False)

    bm = mine(placed(b_mod).reshape(4, 6 * quarter), 0)[None]
    bias = jnp.concatenate(
        [
            mine(placed(b_qkv).reshape(3, 4, pairs, 128), 1).transpose(1, 0, 2).reshape(-1),
            placed(b_out),
            mine(placed(b_up).reshape(n, 4, units), 1).reshape(-1),
            placed(b_down),
        ]
    ).reshape(1, 1, -1)
    wu_own = mine(w_up.reshape(own_rows, n, 4, units), 2).reshape(own_rows, ff_q)
    block_out, grad_input, grad_time, tbuf, ebuf, lbuf, f_q0, f_q1, f_wo, f_wu, f_wd, f_b = run_whole(
        n, clip_len, frames, cotangent, time_embed, bm, bias, wu_own, w_mod, w_qkv, w_out, w_down
    )
    f_wq = jnp.stack([f_q0, f_q1], axis=2).astype(f32).reshape(4, own_rows, pairs, 3, 128)
    s_wq = f_wq.transpose(1, 3, 0, 2, 4).reshape(own_rows, 3 * width)
    s_wo = f_wo.astype(f32).transpose(1, 0, 2).reshape(own_rows, width)
    s_wu = f_wu.astype(f32).reshape(4, own_rows, n, units).transpose(1, 2, 0, 3).reshape(own_rows, ff)
    s_wd = f_wd.astype(f32).reshape(4 * units, width)
    d_mod = jnp.concatenate([lbuf[:, 0], ebuf[:, 0]], axis=1)
    gwm = tn(tbuf[:, 0].astype(bf16), d_mod.astype(bf16))
    gbm = jnp.sum(d_mod, axis=0)
    bq = f_b[:, 0, :qw].reshape(4, pairs, 3, 128).transpose(2, 0, 1, 3).reshape(-1)
    bu = f_b[:, 0, qw : qw + ff_q].reshape(4, n, units).transpose(1, 0, 2).reshape(-1)
    bo = jnp.sum(f_b[:, 0, qw + ff_q : qw + ff_q + width], axis=0)
    bd = jnp.sum(f_b[:, 0, qw + ff_q + width :], axis=0)

    def own(value, like):
        size = like.shape[0]
        return lax.dynamic_slice_in_dim(value, dp_rank * size, size, 0)

    return (
        block_out, grad_input, grad_time, s_wq, own(bq, b_qkv), s_wo, own(bo, b_out), s_wu,
        own(bu, b_up), s_wd, own(bd, b_down), gwm, own(gbm, b_mod),
    )


def solution(mesh):
    placed = (
        P(("dp", "seq"), None),
        P("dp", None),
        P("dp", None),
        P("dp", None),
        P("dp"),
        P("dp", None),
        P("dp"),
        P("dp", None),
        P("dp"),
        P("dp", None),
        P("dp"),
        P("dp", None),
        P("dp"),
        P(("dp", "seq"), None),
    )
    return jax.shard_map(
        per_device,
        mesh=mesh,
        in_specs=placed,
        out_specs=(
            P(("dp", "seq"), None),
            P(("dp", "seq"), None),
            P("dp", None),
            P("dp", None),
            P("dp"),
            P("dp", None),
            P("dp"),
            P("dp", None),
            P("dp"),
            P("dp", None),
            P("dp"),
            P("dp", None),
            P("dp"),
        ),
        check_vma=False,
    )
```

time: 572 us -> 221 us (0.39); the launches traced: 562 us -> 220 us
  blocking collectives: 150 us -> 0 us
  matrix products: 128 us -> 2.27 us
  waiting for transfers between devices: 70.5 us -> 0 us
  Pallas kernels: 138 us -> 191 us
  other arithmetic: 29.6 us -> 6.62 us
  between operations: 15.1 us -> 0.82 us
  starting transfers between devices: 5.93 us -> 0 us
    dot_general x18 -> x1, matrix products: 128 us -> 2.27 us  [tn(): lax.dot_general(left_side, right_side, (((0,), (0,)), ((), ())), preferre...]
    all_gather x8 -> x0, blocking collectives: 102 us -> none  [the longest x2 61.4 us: dp_gather(): return lax.all_gather(value, 'dp', axis=0, tiled=True)]
    reduce_scatter x7 -> x0, waiting for transfers between devices: 69.8 us -> none  [the longest x2 49 us: seq_reduce(): lax.psum_scatter(value.astype(jnp.bfloat16), 'seq', scatter_dimension=0,...]
    pallas_call x1, Pallas kernels: 138 us -> 191 us  [run_whole(): pl.pallas_call(functools.partial(whole_kernel, n), out_shape=outs, in_spe...]
    unnamed x1 -> x0, blocking collectives: 37.6 us -> none
    reduce_sum x10 -> x2, other arithmetic: 11.3 us -> 0.82 us  [the longest x1 0.77 us: per_device(): bd = jnp.sum(f_b[:, 0, qw + ff_q + width:], axis=0)]
    psum x1 -> x0, blocking collectives: 10.3 us -> none  [per_device(): mod_sum = lax.psum(mod_part, 'seq')]
  transfers between devices with their start and end apart: 8 -> 0, of which waited for: 3 -> 0; matrix products, arithmetic and copies ran while one was open for 28% -> 0% of each run, Pallas kernels for 0% -> 0%
where the time goes in v4:
time: 221 us; the launch traced here: 220 us
  Pallas kernels  191 us (86%)
  local copies, waits for them, and re-layouts  19.3 us (9%)
  other arithmetic  6.62 us (3%)
  matrix products  2.27 us (1%)
    pallas_call x1, Pallas kernels, run_whole(): pl.pallas_call(functools.partial(whole_kernel, n), out_shape=outs, in_spe...  191 us
    unnamed x23, local copies, waits for them, and re-layouts  10.3 us

profile of v4, /device:TPU:0, one launch (start us, length us, event | category | flops | bytes accessed | tf_op | source)
XLA Modules:
  0.0 220.1 jit_solution(13128184622936347426)
XLA Ops:
  0.7 0.8 convert_dynamic-update-slice_fusion.3
  1.4 0.7 convert_dynamic-update-slice_fusion.4
  2.2 0.7 convert_dynamic-update-slice_fusion.2
  2.9 0.1 reshape.95
  3.0 0.1 reshape.96
  3.1 0.8 convert_dynamic-update-slice_fusion.1
  3.9 0.6 reshape.97.bias
  4.5 0.8 convert_dynamic-update-slice_fusion
  5.3 0.6 constant_dynamic-slice_fusion.1.bm
  5.9 1.3 copy.57
  7.2 0.8 copy.58.wu_own
  8.0 191.1 %shard_map.237 = (f32[256,1024]{1,0:T(8,128)}, f32[256,1024]{1,0:T(8,128)}, f32[1,1024]{1,0:T(1,128)}, f32[8,1,128]{2,1,0:T(1,128)}, f32[8,1,4096]{2,1,0:T(1,128...) custom-call(s32[1,6]{1,0:T(1,128)} %lengths.1, ...), custom_call_target="tpu_custom_call" | custom-call | tf_op jit(solution)/shard_map/pallas_call | solution.py:921
  199.1 0.0 copy-start.4
  199.1 0.0 copy-start.5
  199.1 0.7 convert_element_type.34
  199.9 0.7 slice_reduce_fusion.2
  200.6 0.1 reshape_squeeze.7
  200.7 0.1 reshape.108
  200.8 0.6 dynamic_slice.37
  201.4 0.8 slice_reduce_fusion
  202.2 0.7 slice.12
  202.9 0.7 dynamic_slice.35
  203.6 0.6 dynamic_slice.38
  204.2 0.6 dynamic_slice.36
  204.7 0.9 copy.82
  205.6 1.0 copy.81
  206.6 0.1 fusion
  206.6 0.7 dynamic_slice.39
  207.3 1.2 copy.59
  208.5 0.0 copy-done.4
  208.6 0.2 copy.60
  208.8 0.0 copy-done.5
  208.8 0.2 copy.64
  209.0 1.0 copy.69
  210.0 0.1 convert_bitcast_fusion
  210.1 0.1 copy.61
  210.3 0.0 copy-start.3
  210.3 1.6 copy.68
  211.9 0.0 copy-done.3
  211.9 0.2 copy.65
  212.1 0.1 copy.66
  212.2 0.0 copy-start.2
  212.3 1.3 copy.70
  213.6 0.0 copy-done.2
  213.6 1.1 bitcast_convert_fusion
  214.7 0.0 copy-start.1
  214.7 2.3 %fusion.2 = f32[128,6144]{1,0:T(8,128)} fusion(f32[8,4096]{1,0:T(8,128)S(1)} %bitcast.45, f32[8,2048]{1,0:T(8,128)S(1)} %bitcast.48, bf16[8,1,128]{2,1,0:T(2,128)(2,1)S(1)} %convert_element_type.34), kind=kOutput, calls=%fused_computation.7 | convolution fusion | flops 12779520 | bytes 3344384 | tf_op jit(solution)/shard_map/dot_general | solution.py:277
  217.0 0.0 copy-done.1
  217.0 0.0 copy-start
  217.0 1.0 copy.92
  217.9 0.6 copy-done
  218.6 0.0 copy-start.6
  218.6 1.0 copy.93
  219.5 0.0 copy-done.6
  219.5 0.6 copy.94
  (16 shorter events, 0.2 us)
Async XLA Ops:
  199.1 9.4 %copy-start.4 = (bf16[4,128,384]{2,1,0:T(8,128)(2,1)S(1)}, bf16[4,128,384]{2,1,0:T(8,128)(2,1)}, u32[]{:S(2)}) copy-start(bf16[4,128,384]{2,1,0:T(8,128)(2,1)} %get-tuple-element.29) | copy-start | bytes 1179652
  199.1 9.7 %copy-start.5 = (bf16[4,128,256]{2,1,0:T(8,128)(2,1)S(1)}, bf16[4,128,256]{2,1,0:T(8,128)(2,1)}, u32[]{:S(2)}) copy-start(bf16[4,128,256]{2,1,0:T(8,128)(2,1)} %get-tuple-element.31) | copy-start | bytes 786436
  210.3 1.6 copy-start.3
  212.2 1.3 copy-start.2
  214.7 2.3 %copy-start.1 = (f32[256,1024]{1,0:T(8,128)S(1)}, f32[256,1024]{1,0:T(8,128)}, u32[]{:S(2)}) copy-start(f32[256,1024]{1,0:T(8,128)} %get-tuple-element.91) | copy-start | bytes 3145732
  217.0 1.6 copy-start
  218.6 1.0 copy-start.6

commit v5 on v4

--- a/solution.py
+++ b/solution.py
@@ -92,14 +92,18 @@
 
 
 class ToAll:
-    def __init__(self, links, src, buf):
-        self.l, self.src, self.buf = links, src, buf
+    def __init__(self, links, src, buf, cols=None):
+        self.l, self.src, self.buf, self.cols = links, src, buf, cols
         self.si, self.ri = links.sems(links.n, links.n)
 
+    def _at(self, slot):
+        return self.buf.at[slot] if self.cols is None else self.buf.at[slot, :, self.cols]
+
     def _to(self, k):
         l = self.l
         peer = (l.d + k) % l.n
-        return l.copy(self.src(peer), self.buf.at[l.d], self.si + k, self.ri + l.d, (peer, l.s))
+        src = self._at(l.d) if self.src is None else self.src(peer)
+        return l.copy(src, self._at(l.d), self.si + k, self.ri + l.d, (peer, l.s))
 
     def start(self):
         for k in range(1, self.l.n):
@@ -109,7 +113,7 @@
         l = self.l
         for k in range(1, l.n):
             peer = (l.d + k) % l.n
-            l.copy(self.buf.at[peer], self.buf.at[peer], self.si + k, self.ri + peer, (peer, l.s)).wait_recv()
+            l.copy(self._at(peer), self._at(peer), self.si + k, self.ri + peer, (peer, l.s)).wait_recv()
 
     def wait_send(self):
         for k in range(1, self.l.n):
@@ -182,13 +186,16 @@
 
 
 class SeqGather:
-    def __init__(self, links, buf):
-        self.l, self.buf = links, buf
+    def __init__(self, links, buf, rows=None):
+        self.l, self.buf, self.rows = links, buf, rows
         self.si, self.ri = links.sems(3, 4)
 
+    def _at(self, slot):
+        return self.buf.at[slot] if self.rows is None else self.buf.at[slot, self.rows]
+
     def _c(self, slot, k, t):
         l = self.l
-        return l.copy(self.buf.at[slot], self.buf.at[slot], self.si + k, self.ri + slot, (l.d, t))
+        return l.copy(self._at(slot), self._at(slot), self.si + k, self.ri + slot, (l.d, t))
 
     def start(self):
         l = self.l
@@ -201,8 +208,7 @@
         self._c(l.s2, 2, l.s1).start()
 
     def wait(self, slot):
-        l = self.l
-        l.copy(self.buf.at[slot], self.buf.at[slot], self.si, self.ri + slot, (l.d, l.s1)).wait_recv()
+        self._c(slot, 0, self.l.s1).wait_recv()
 
     def wait_send(self):
         l = self.l
@@ -240,37 +246,63 @@
 class SeqSum:
     def __init__(self, links, held):
         self.l, self.held = links, held
-        self.si, self.ri = links.sems(3, 3)
-
-    def _c(self, k, t):
-        l = self.l
-        return l.copy(self.held.at[k], self.held.at[3 + k], self.si + k, self.ri + k, (l.d, t))
-
-    def far(self, term):
+        self.rows = held.shape[1]
+        self.si, self.ri = links.sems(5, 5)
+
+    def _c(self, k, h, t):
+        l = self.l
+        half = self.rows // 2
+        at = slice(None) if k == 2 else slice(h * half, (h + 1) * half)
+        sem = 4 if k == 2 else 2 * k + h
+        return l.copy(self.held.at[k, at], self.held.at[3 + k, at], self.si + sem, self.ri + sem, (l.d, t))
+
+    def _part(self, b, h):
+        half = self.rows // 2
+        return pl.ds(pl.multiple_of(b * self.rows + h * half, half), half)
+
+    def far(self, term, cross=True):
+        l, held, half = self.l, self.held, self.rows // 2
+        for h in range(2):
+            held[0, h * half : (h + 1) * half] = term(self._part(l.s3, h)).astype(bf16)
+            self._c(0, h, l.s1).start()
+        for h in range(2):
+            at = slice(h * half, (h + 1) * half)
+            mine = term(self._part(l.s2, h))
+            self._c(0, h, l.s1).wait_recv()
+            held[1, at] = (mine + held[3, at].astype(f32)).astype(bf16)
+            if cross:
+                self._c(1, h, l.s2).start()
+
+    def cross(self):
+        for h in range(2):
+            self._c(1, h, self.l.s2).start()
+
+    def near(self, term):
+        l = self.l
+        self.held[2] = term(pl.ds(pl.multiple_of(l.s1 * self.rows, self.rows), self.rows)).astype(bf16)
+        self._c(2, 0, l.s1).start()
+
+    def total(self, term):
         l, held = self.l, self.held
-        held[0] = term(l.s3).astype(bf16)
-        self._c(0, l.s1).start()
-        mine = term(l.s2)
-        self._c(0, l.s1).wait_recv()
-        held[1] = (mine + held[3].astype(f32)).astype(bf16)
-        self._c(1, l.s2).start()
-
-    def near(self, term):
-        l = self.l
-        self.held[2] = term(l.s1).astype(bf16)
-        self._c(2, l.s1).start()
-
-    def total(self, mine):
-        l, held = self.l, self.held
-        self._c(2, l.s1).wait_recv()
-        self._c(1, l.s2).wait_recv()
+        mine = term(pl.ds(pl.multiple_of(l.s * self.rows, self.rows), self.rows))
+        self._c(2, 0, l.s1).wait_recv()
+        for h in range(2):
+            self._c(1, h, l.s2).wait_recv()
         return mine + held[5].astype(f32) + held[4].astype(f32)
 
     def wait_send(self):
         l = self.l
-        self._c(0, l.s1).wait_send()
-        self._c(1, l.s2).wait_send()
-        self._c(2, l.s1).wait_send()
+        for h in range(2):
+            self._c(0, h, l.s1).wait_send()
+            self._c(1, h, l.s2).wait_send()
+        self._c(2, 0, l.s1).wait_send()
+
+
+def half_of_each(one, two, odd):
+    lane = lax.broadcasted_iota(jnp.int32, one.shape, 1)
+    low = jnp.where(odd, pltpu.roll(one, 64, 1), one)
+    high = jnp.where(odd, two, pltpu.roll(two, 64, 1))
+    return jnp.where(lane < 64, low, high)
 
 
 def tn(left_side, right_side):
@@ -335,6 +367,24 @@
         lax.fori_loop(0, l.n, one, 0)
 
 
+class One:
+    def __init__(self, links, src, dst, to):
+        self.l, self.src, self.dst, self.to = links, src, dst, to
+        self.si, self.ri = links.sems(1, 1)
+
+    def _c(self):
+        return self.l.copy(self.src, self.dst, self.si, self.ri, (self.l.d, self.to))
+
+    def start(self):
+        self._c().start()
+
+    def wait_recv(self):
+        self._c().wait_recv()
+
+    def wait_send(self):
+        self._c().wait_send()
+
+
 class DpSum:
     def __init__(self, links, g, xin, zin):
         self.l, self.g, self.xin, self.zin = links, g, xin, zin
@@ -350,7 +400,7 @@
         l = self.l
         t = (l.d + 2 * k) % l.n
         at = self.half + k
-        return l.copy(self.g.at[t], self.zin.at[k], self.si + at, self.ri + at, (t, l.s))
+        return l.copy(self.g.at[t], self.zin.at[k - 1], self.si + at, self.ri + at, (t, l.s))
 
     def send_x(self, first, count):
         for i in range(count // 2):
@@ -376,7 +426,7 @@
         out = self.g[l.d].astype(f32) + self.xin[h].astype(f32)
         for k in range(1, self.half):
             self._z(k).wait_recv()
-            out = out + self.zin[k].astype(f32)
+            out = out + self.zin[k - 1].astype(f32)
         return out
 
     def wait_send(self):
@@ -388,14 +438,14 @@
 
 
 def whole_kernel(
-    n,
-    lengths, frames, cot, time_row, bm, bias, wu_own, wm_hbm, wq_hbm, wo_hbm, wd_hbm,
-    block_out, grad_input, grad_time, tbuf, ebuf, lbuf, f_q0, f_q1, f_wo, f_wu, f_wd, f_b,
-    wm, wq, wu, wd, wo, tsrc, psend, pbuf, bbuf, mod, n_in, attn_branch, n_mid, cos, sin, idc, idr,
-    xa, dffn, xf, q, k, v, kt, vt, lse, ao_out, ao, do_out, gh, gelu, dhid, dattn, fsum, dk, dv, dproj,
-    held, held_f, held_o, g_q0, x_q0, z_q0, g_q1, x_q1, z_q1, g_wo, x_wo, z_wo, g_wu, x_wu, z_wu, g_wd, x_wd, z_wd,
+    n, plain,
+    lengths, time_row, bias, b1, b2, b3, b4, b5, wu_own, frames_hbm, cot_hbm, wm_hbm, wq_hbm, wo_hbm, wd_hbm,
+    grad_time, tmat, dmat, f_wu, bias_out, o_bq, o_bo, o_bd, o_bu, o_bm, out_hbm, grad_hbm, gwq_hbm, gwo_hbm, gwu_hbm, gwd_hbm,
+    tbuf, dmb, frames, cot, block_out, grad_input, bmv, wu_raw, f_b, wm, wq0, wq1, wu, wd, wo, tsrc, psend, pbuf, psend2, pbuf2, bbuf, mod, n_in, attn_branch, n_mid, cos, sin, idc, idr,
+    xa, dffn, xf, q, k, v, kt, vt, lse, ao_out, ao, gh, gelu, dhid, dattn, fsum, dk, dv, dproj,
+    f_q0, f_q1, f_wo, f_wd, held, held_f, ho, fo, g_q0, x_q0, z_q0, g_q1, x_q1, z_q1, g_wo, x_wo, z_wo, g_wu, x_wu, z_wu, g_wd, x_wd, z_wd,
     em, lm, eb, ebb, lb, lbb, dts, dtb,
-    send, recv, local,
+    send, recv, local, gone,
 ):
     l = Links(n, send, recv)
     d, s = l.d, l.s
@@ -403,7 +453,6 @@
     item = 4 * rows
     quarter = width // 4
     own_rows = wm.shape[0]
-    mq = bm.shape[1]
     units = wd.shape[1]
     ff_q = wu.shape[2]
     pairs = quarter // 128
@@ -417,71 +466,108 @@
     ] + [
         pltpu.make_async_copy(
             wq_hbm.at[:, pl.ds(pl.multiple_of(j * width + s * quarter + 128 * p, 128), 128)],
-            wq.at[d, :, pl.ds(p * pw + 128 * j, 128)], local.at[3 + 3 * p + j],
+            (wq0, wq1)[p].at[d, :, pl.ds(128 * j, 128)], local.at[3 + 3 * p + j],
         )
         for p in range(pairs) for j in range(3)
     ]
-    for c in take:
+    first = [
+        pltpu.make_async_copy(frames_hbm, frames, local.at[9]),
+        pltpu.make_async_copy(cot_hbm, cot, local.at[10]),
+    ]
+    if not plain:
+        wide = pl.multiple_of(s // 2 * 128, 128)
+        take_wu = [
+            pltpu.make_async_copy(wu_own.at[:, pl.ds(i * 4 * units + wide, 128)], wu_raw.at[i], local.at[11 + i])
+            for i in range(n)
+        ]
+    for c in first + take:
         c.start()
     times = ToAll(l, lambda peer: tsrc.at[peer], tbuf)
-    parts = ToAll(l, lambda peer: psend.at[peer], pbuf)
-    biases = ToAll(l, lambda peer: bias.at[0], bbuf)
+    parts, parts2 = ToAll(l, lambda peer: psend.at[peer], pbuf), ToAll(l, lambda peer: psend2.at[peer], pbuf2)
+    wide_b = bbuf.shape[2]
+    biases = ToAll(l, None, bbuf)
     mods = SeqAll(l, mod)
-    a_wq, a_wu, a_wd, a_wo = DpGather(l, wq), DpGather(l, wu), DpGather(l, wd), DpGather(l, wo.at[s])
-    s_xa, s_df, s_xf, s_wo = SeqGather(l, xa), SeqGather(l, dffn), SeqGather(l, xf), SlotGather(l, wo)
-    w_ao, w_do = SeqSwap(l, ao_out, ao), SeqSwap(l, do_out, gh)
-    sum_x, sum_f, sum_o, sum_a = SeqSum(l, held), SeqSum(l, held_f), SeqSum(l, held_o), SeqSum(l, held)
+    a_q0, a_q1, a_wu, a_wd, a_wo = DpGather(l, wq0), DpGather(l, wq1), DpGather(l, wu), DpGather(l, wd), DpGather(l, wo.at[s])
+    s_wo = SlotGather(l, wo)
+    s_a0, s_a1 = (SeqGather(l, xa, pl.ds(h * (rows // 2), rows // 2)) for h in range(2))
+    s_x0, s_x1 = (SeqGather(l, xf, pl.ds(h * (rows // 2), rows // 2)) for h in range(2))
+    s_d0, s_d1 = (SeqGather(l, dffn, pl.ds(h * (rows // 2), rows // 2)) for h in range(2))
+    w_ao, w_do = SeqSwap(l, ao_out, ao), SeqSwap(l, ao_out, gh)
+    sum_x, sum_f, sum_a = SeqSum(l, held), SeqSum(l, held_f), SeqSum(l, held)
     d_q0, d_q1, d_wo, d_wu, d_wd = (
         DpSum(l, g_q0, x_q0, z_q0), DpSum(l, g_q1, x_q1, z_q1), DpSum(l, g_wo, x_wo, z_wo),
         DpSum(l, g_wu, x_wu, z_wu), DpSum(l, g_wd, x_wd, z_wd),
     )
-    o_q0, o_q1, o_wo, o_wu, o_wd = (
-        SeqGather(l, f_q0), SeqGather(l, f_q1), SeqGather(l, f_wo), SeqGather(l, f_wu), SeqGather(l, f_wd)
+    o_q0, o_q1, o_wu, o_wd = (
+        SeqGather(l, f_q0), SeqGather(l, f_q1), SeqGather(l, f_wu), SeqGather(l, f_wd)
     )
+    core = s % 2
+    c_wo, y_wo = One(l, ho.at[0], ho.at[1], l.s1), One(l, fo.at[0], fo.at[1], l.s2)
+    o_wo = One(l, f_wo.at[core], f_wo.at[core], l.s1)
     e_mod, l_mod, o_b = SeqAll(l, em), SeqAll(l, lm), SeqAll(l, f_b)
-    e_all, l_all = ToAll(l, lambda peer: ebuf.at[d], ebuf), ToAll(l, lambda peer: lbuf.at[d], lbuf)
+    e_all, l_all = ToAll(l, None, dmb, slice(2 * width, 6 * width)), ToAll(l, None, dmb, slice(0, 2 * width))
     eb_all, lb_all = ToAll(l, lambda peer: eb, ebb), ToAll(l, lambda peer: lb, lbb)
     t_all = ToAll(l, lambda peer: dts.at[peer], dtb)
 
     def at_rows(b):
         return pl.ds(pl.multiple_of(b * rows, rows), rows)
 
+    if plain:
+        bbuf[d] = bias[0, :, :wide_b]
+        own_mod = bias[0, :, wide_b:]
+    else:
+        bbuf[d] = jnp.concatenate([b[...].astype(f32) for b in (b1, b2, b3, b4)], axis=1)
+        own_mod = b5[...].astype(f32)
+    if plain:
+        bmv[...] = own_mod
+    else:
+        bmv[...] = jnp.concatenate([jnp.where(d == i, own_mod, jnp.zeros_like(own_mod)) for i in range(n)], axis=1)
     tv = time_row[...]
     act = (tv / (1.0 + jnp.exp(-tv))).astype(bf16).astype(f32)
     for i in range(n):
         tsrc[i] = act[:, i * own_rows : (i + 1) * own_rows]
+    for c in first:
+        c.wait()
+    n_in[...] = normed(frames[...])[0]
     dffn[s] = cot[...].astype(bf16)
     for c in take[3:]:
         c.wait()
     l.barrier()
     times.start()
-    a_wq.start()
-    s_df.start()
+    a_q0.start()
+    s_d0.start()
     biases.start()
     tbuf[d] = tsrc[d]
-    wu[d] = wu_own[...]
+    if plain:
+        wu_copy = pltpu.make_async_copy(wu_own, wu.at[d], local.at[11])
+        wu_copy.start()
+        wu_copy.wait()
+    else:
+        for c in take_wu:
+            c.start()
     for c in take[:3]:
         c.wait()
-    n_in[...] = normed(frames[...])[0]
     times.wait_recv()
     lhs = jnp.concatenate([tbuf[i] for i in range(n)], axis=0).astype(bf16)
-    part = nn(lhs, wm[:, pl.ds(pl.multiple_of(s * mq, 128), mq)]) + bm[...]
+    tmat[...] = lhs
+    part = nn(lhs, wm[:, : 2 * width]) + bmv[:, : 2 * width]
     for i in range(n):
         psend[i] = part[i : i + 1]
     parts.start()
+    part = nn(lhs, wm[:, pl.ds(pl.multiple_of((2 + s) * width, 128), width)]) + bmv[:, pl.ds(pl.multiple_of((2 + s) * width, 128), width)]
+    for i in range(n):
+        psend2[i] = part[i : i + 1]
     total = psend[d]
     parts.wait_recv()
     for j in range(1, n):
         total = total + pbuf[(d + j) % n]
-    mod[s] = total
-    mods.start()
-    mods.wait_recv()
-    flat = jnp.concatenate([mod[i] for i in range(4)], axis=1)
-    shift_a, scale_a, gate_a, shift_f, scale_f, gate_f = (
-        flat[:, i * width : (i + 1) * width] for i in range(6)
-    )
+    shift_a, scale_a = total[:, :width], total[:, width:]
     xa[s] = (n_in[...] * (1.0 + scale_a) + shift_a).astype(bf16)
-    s_xa.start()
+    s_a0.start()
+    s_a1.start()
+    parts2.start()
+    a_q1.start()
+    a_wo.start()
 
     def places(shape, dim):
         at = lax.broadcasted_iota(jnp.int32, shape, dim)
@@ -502,41 +588,57 @@
     cos[...] = jnp.cos(phase)
     sin[...] = jnp.where(lanes % 64 < 32, -1.0, 1.0) * jnp.sin(phase)
 
-    a_wq.hand_on()
-    a_wo.start()
-    s_df.hand_on()
-    a_wq.wait_rest()
+    a_q0.hand_on()
+    total = psend2[d]
+    parts2.wait_recv()
+    for j in range(1, n):
+        total = total + pbuf2[(d + j) % n]
+    mod[s] = total
+    mods.start()
     biases.wait_recv()
-    own_bias = bias[0]
-    for j in range(1, n):
-        own_bias = own_bias + bbuf[(d + j) % n]
-    bq = own_bias[:, :qw]
-    bo = own_bias[:, qw : qw + width]
-    bu = own_bias[:, qw + width : qw + width + ff_q]
-    bd = own_bias[:, qw + width + ff_q :]
-
-    def project(i, carry):
-        @pl.when(i == 1)
-        def _():
-            s_xa.wait(l.s1)
-            a_wu.start()
-
-        @pl.when(i == 2)
-        def _():
-            s_xa.hand_on()
-            a_wd.start()
-
-        @pl.when(i == 3)
-        def _():
-            s_xa.wait(l.s3)
-
-        b = l.block(i)
-        at = at_rows(b)
-        pr = nn(xa[b], merged(wq)) + bq
-        cb, sb = cos[at, :], sin[at, :]
+    if plain:
+        own_bias = bbuf[0]
+        for j in range(1, n):
+            own_bias = own_bias + bbuf[j]
+        bq = own_bias[:, :qw]
+        bo = own_bias[:, qw : qw + width]
+        bu = own_bias[:, qw + width : qw + width + ff_q]
+        bd = own_bias[:, qw + width + ff_q :]
+    else:
+        each = 3 * own_rows // 128
+        bqs = []
         for p in range(pairs):
-            c0 = 128 * p
-            qp, kp, vp = (pr[:, p * pw + 128 * j : p * pw + 128 * j + 128] for j in range(3))
+            for j in range(3):
+                u = j * (width // 128) + s * pairs + p
+                bqs.append(bbuf[u // each, :, pl.ds(pl.multiple_of(u % each * 128, 128), 128)])
+        bq = jnp.concatenate(bqs, axis=1)
+        c0 = 3 * own_rows
+        bo = jnp.concatenate([bbuf[i, :, c0 : c0 + own_rows] for i in range(n)], axis=1)
+        c0 = c0 + own_rows
+        c1 = c0 + 4 * units
+        bd = jnp.concatenate([bbuf[i, :, c1 : c1 + own_rows] for i in range(n)], axis=1)
+        odd = s % 2 == 1
+        at = pl.ds(c0 + wide, 128)
+        bu = jnp.concatenate([half_of_each(bbuf[2 * i, :, at], bbuf[2 * i + 1, :, at], odd) for i in range(n // 2)], axis=1)
+        for c in take_wu:
+            c.wait()
+        for i in range(n // 2):
+            pair = half_of_each(wu_raw[2 * i].astype(f32), wu_raw[2 * i + 1].astype(f32), odd)
+            wu[d, :, 128 * i : 128 * i + 128] = pair.astype(bf16)
+    mods.wait_recv()
+    gate_a, shift_f, scale_f, gate_f = (mod[i] for i in range(4))
+    a_q0.wait_rest()
+
+    def project_pair(p, wq, before):
+        c0 = 128 * p
+
+        def one(i, carry):
+            before(i)
+            b = l.block(i)
+            at = at_rows(b)
+            pr = nn(xa[b], merged(wq)) + bq[:, p * pw : (p + 1) * pw]
+            cb, sb = cos[at, :], sin[at, :]
+            qp, kp, vp = (pr[:, 128 * j : 128 * j + 128] for j in range(3))
             vp = vp.astype(bf16)
             qp = (qp * cb + swap_halves(qp, lane) * sb).astype(bf16)
             kp = (kp * cb + swap_halves(kp, lane) * sb).astype(bf16)
@@ -545,18 +647,16 @@
             v[at, c0 : c0 + 128] = vp
             kt[p, :, at] = jnp.transpose(kp.astype(f32)).astype(bf16)
             vt[p, :, at] = jnp.transpose(vp.astype(f32)).astype(bf16)
-        return carry
-
-    lax.fori_loop(0, 4, project, 0)
-    a_wo.hand_on()
-    s_wo.send(d)
-
-    def attend(j, carry):
-        i = (j + 2) % 4
-        b = l.block(i)
-        at = at_rows(b)
-        same = idc[...] == idr[:, at]
-        for p in range(pairs):
+            return carry
+
+        lax.fori_loop(0, 4, one, 0)
+
+    def attend_pair(p, after):
+        def one(j, carry):
+            i = (j + 2) % 4
+            b = l.block(i)
+            at = at_rows(b)
+            same = idc[...] == idr[:, at]
             qp, kp = q[at, 128 * p : 128 * p + 128], k[:, 128 * p : 128 * p + 128]
             outs = []
             for h in range(2):
@@ -569,32 +669,73 @@
                 pt = (ex * (1.0 / su)).astype(bf16)
                 outs.append(nn(vt[p, 64 * h : 64 * h + 64, :], pt))
             ao_out[b, :, 128 * p : 128 * p + 128] = jnp.transpose(jnp.concatenate(outs, axis=0)).astype(bf16)
-
+            after(j, i)
+            return carry
+
+        lax.fori_loop(0, 4, one, 0)
+
+    def after_first(j, i):
+        @pl.when(j == 0)
+        def _():
+            a_wo.hand_on()
+            s_wo.send(d)
+
+        @pl.when(j == 1)
+        def _():
+            a_wd.start()
+
+        @pl.when(j == 2)
+        def _():
+            s_d1.hand_on()
+
+    def after_second(j, i):
         @pl.when(j != 2)
         def _():
             w_ao.copy_to(i).start()
 
         @pl.when(j == 0)
         def _():
-            a_wo.wait_rest()
-            s_wo.send(l.px)
+            s_wo.hand_on(d)
 
         @pl.when(j == 1)
         def _():
-            s_wo.hand_on(d)
+            a_wu.hand_on()
 
         @pl.when(j == 2)
         def _():
             ao[s] = ao_out[s]
-            a_wu.hand_on()
 
         @pl.when(j == 3)
         def _():
             s_wo.hand_on(l.px)
 
-        return carry
-
-    lax.fori_loop(0, 4, attend, 0)
+    def before_first(i):
+        @pl.when(i == 1)
+        def _():
+            s_a0.wait(l.s1)
+            s_a1.wait(l.s1)
+
+        @pl.when(i == 2)
+        def _():
+            s_a0.hand_on()
+            s_a1.hand_on()
+            s_d1.start()
+
+        @pl.when(i == 3)
+        def _():
+            s_a0.wait(l.s3)
+            s_a1.wait(l.s3)
+            s_d0.hand_on()
+            a_wu.start()
+
+    project_pair(0, wq0, before_first)
+    a_q1.hand_on()
+    attend_pair(0, after_first)
+    a_q1.wait_rest()
+    a_wo.wait_rest()
+    s_wo.send(l.px)
+    project_pair(1, wq1, lambda i: None)
+    attend_pair(1, after_second)
     s_wo.wait_rest()
     w_ao.wait_recv()
     left = jnp.concatenate([ao[i] for i in range(4)], axis=1)
@@ -606,51 +747,69 @@
     nm, rstd = normed(xm)
     n_mid[...] = nm
     xf[s] = (nm * (1.0 + scale_f) + shift_f).astype(bf16)
-    s_xf.start()
+    s_x0.start()
+    s_x1.start()
     a_wd.hand_on()
-    s_df.wait(l.s1)
-    s_df.wait(l.s3)
-    s_df.wait_send()
+    for g in (s_d0, s_d1):
+        g.wait(l.s1)
+        g.wait(l.s3)
+        g.wait_send()
     for b in range(4):
         dffn[b] = (gate_f * dffn[b].astype(f32)).astype(bf16)
     a_wu.wait_rest()
     a_wd.wait_rest()
 
-    def hidden_term(b):
-        return nt(dhid[at_rows(b), :], merged(wu))
-
-    def ffn_term(b):
-        return nn(gelu[at_rows(b), :], merged(wd))
-
-    def out_term(t):
-        part = dattn[:, pl.ds(pl.multiple_of(t * quarter, 128), quarter)]
+    def hidden_term(at):
+        return nt(dhid[at, :], merged(wu))
+
+    def ffn_term(at):
+        return nn(gelu[at, :], merged(wd))
+
+    def out_half(c):
+        part = dattn[:, pl.ds(pl.multiple_of(c * 2 * quarter, 128), 2 * quarter)]
         return jnp.concatenate([tn(ao[i], part) for i in range(4)], axis=0)
 
-    def xa_term(b):
-        return nt(dproj[at_rows(b), :], merged(wq))
-
-    def feed(i, carry):
-        @pl.when(i == 1)
-        def _():
-            s_xf.wait(l.s1)
-
-        @pl.when(i == 2)
+    def xa_term(at):
+        return nt(dproj[at, :pw], merged(wq0)) + nt(dproj[at, pw:], merged(wq1))
+
+    half = rows // 2
+
+    def feed(j, carry):
+        late = j // 4
+        i = late * (2 + j % 2) + (1 - late) * (j // 2)
+        h = late * (j // 2 % 2) + (1 - late) * (j % 2)
+
+        @pl.when(j == 2)
+        def _():
+            s_x0.wait(l.s1)
+            s_x1.wait(l.s1)
+
+        @pl.when(j == 4)
         def _():
             sum_x.near(hidden_term)
-            s_xf.hand_on()
-
-        @pl.when(i == 3)
-        def _():
-            s_xf.wait(l.s3)
+            s_x0.hand_on()
+
+        @pl.when(j == 5)
+        def _():
+            s_x0.wait(l.s3)
+
+        @pl.when(j == 6)
+        def _():
+            s_x1.hand_on()
+
+        @pl.when(j == 7)
+        def _():
+            s_x1.wait(l.s3)
 
         b = l.block(i)
-        at = at_rows(b)
-        act, slope = gelu_both(nn(xf[b], merged(wu)) + bu)
+        inner = pl.ds(pl.multiple_of(h * half, half), half)
+        at = pl.ds(pl.multiple_of(b * rows + h * half, half), half)
+        act, slope = gelu_both(nn(xf[b, inner], merged(wu)) + bu)
         gelu[at, :] = act.astype(bf16)
-        dhid[at, :] = (nt(dffn[b], merged(wd)) * slope).astype(bf16)
+        dhid[at, :] = (nt(dffn[b, inner], merged(wd)) * slope).astype(bf16)
         return carry
 
-    lax.fori_loop(0, 4, feed, 0)
+    lax.fori_loop(0, 8, feed, 0)
     sum_x.far(hidden_term)
 
     def make(left_of, right, g, chain, each):
@@ -673,7 +832,9 @@
     eb[:, ff_q + width :] = jnp.sum(dffn[s].astype(f32), axis=0, keepdims=True)
     dk[...] = jnp.zeros_like(dk)
     dv[...] = jnp.zeros_like(dv)
-    g = sum_x.total(hidden_term(s))
+    sum_f.far(ffn_term, False)
+    sum_f.near(ffn_term)
+    g = sum_x.total(hidden_term)
     nm = n_mid[...]
     fsum[0:1, :] = jnp.sum(g, axis=0, keepdims=True)
     fsum[1:2, :] = jnp.sum(g * nm, axis=0, keepdims=True)
@@ -681,6 +842,7 @@
     grad_input[...] = dm
     dattn[...] = (gate_a * dm).astype(bf16)
     per4 = n // 4
+    w_ao.wait_send()
 
     def give(j, carry):
         i = (j + 2) % 4
@@ -690,7 +852,7 @@
             wt = wo[c, pl.ds(t * per4, per4)].reshape(quarter, quarter)
             o = nt(dattn[:, c * quarter : (c + 1) * quarter], wt)
             out = o if out is None else out + o
-        do_out[t] = out.astype(bf16)
+        ao_out[t] = out.astype(bf16)
 
         @pl.when(j != 2)
         def _():
@@ -698,7 +860,7 @@
 
         @pl.when(j == 2)
         def _():
-            gh[s] = do_out[s]
+            gh[s] = ao_out[s]
 
         return carry
 
@@ -706,6 +868,9 @@
     fsum[2:3, :] = jnp.sum(dm * attn_branch[...], axis=0, keepdims=True)
     eb[:, ff_q : ff_q + width] = jnp.sum(dattn[...].astype(f32), axis=0, keepdims=True)
     eb_all.start()
+
+    def leave(src, dst, k):
+        return pltpu.make_async_copy(src, dst, gone.at[k])
 
     def turned(values, at):
         val = values.astype(bf16).astype(f32)
@@ -721,7 +886,7 @@
             same = idc[...] == idr[:, at]
             kp, vp = k[:, c0 : c0 + 128], v[:, c0 : c0 + 128]
             qp, dop = q[at, c0 : c0 + 128], gh[b, :, c0 : c0 + 128]
-            dqs = []
+            dqs, pts, dsts, qms, doms = [], [], [], [], []
             for h in range(2):
                 mine = (lane < 64) == (h == 0)
                 qm = jnp.where(mine, qp, jnp.zeros_like(qp))
@@ -730,9 +895,13 @@
                 dpt = nt(vp, dom)
                 mean = jnp.sum(dpt * pt, axis=0, keepdims=True)
                 dst = (pt * (dpt - mean)).astype(bf16)
-                dv[p] += nn(pt.astype(bf16), dom)
-                dk[p] += nn(dst, qm)
+                pts.append(pt.astype(bf16))
+                dsts.append(dst)
+                qms.append(qm)
+                doms.append(dom)
                 dqs.append(nn(kt[p, 64 * h : 64 * h + 64, :], dst))
+            dv[p] += nn(jnp.concatenate(pts, axis=1), jnp.concatenate(doms, axis=0))
+            dk[p] += nn(jnp.concatenate(dsts, axis=1), jnp.concatenate(qms, axis=0))
             dq = jnp.transpose(jnp.concatenate(dqs, axis=0)) * 0.125
             dproj[at, base : base + 128] = turned(dq, at)
             after(i)
@@ -764,27 +933,28 @@
     def after0(i):
         @pl.when(i == 0)
         def _():
-            d_wd.fold()
+            ho[0] = out_half(1 - core).astype(bf16)
+            c_wo.start()
+
+        @pl.when(i == 1)
+        def _():
+            mine = out_half(core)
+            c_wo.wait_recv()
+            g_wo[...] = (mine + ho[1].astype(f32)).astype(bf16).reshape(n, own_rows, 2 * quarter)
+            d_wo.send_x(0, n)
 
         @pl.when(i == 2)
         def _():
-            sum_f.far(ffn_term)
-            sum_f.near(ffn_term)
-
-        @pl.when(i == 3)
-        def _():
+            sum_f.cross()
             d_wu.fold()
 
     def after1(i):
-        @pl.when(i == 0)
-        def _():
-            sum_o.far(out_term)
-            sum_o.near(out_term)
-
         @pl.when(i == 2)
         def _():
-            ffn = sum_f.total(ffn_term(s)) + bd
+            ffn = sum_f.total(ffn_term) + bd
             block_out[...] = block_out[...] + gate_f * ffn
+            leave(block_out, out_hbm, 0).start()
+            d_wo.fold()
             em[s, :, 3 * width :] = jnp.sum(cot[...] * ffn, axis=0, keepdims=True)
             em[s, :, :width] = fsum[2:3, :]
             em[s, :, width : 2 * width] = fsum[0:1, :]
@@ -794,39 +964,43 @@
         @pl.when(i == 3)
         def _():
             e_mod.wait_recv()
-            ebuf[d] = (em[0] + em[1] + em[2] + em[3]).astype(bf16).astype(f32)
+            dmb[d, :, 2 * width :] = (em[0] + em[1] + em[2] + em[3]).astype(bf16).astype(f32)
             e_all.start()
 
+    d_wd.fold()
     back_pair(0, before0, after0)
     make(lambda m: cols_of(xa, m), lambda: dproj[:, :pw], g_q0, d_q0, own_rows)
     back_pair(1, lambda i: None, after1)
     sum_x.wait_send()
     sum_a.far(xa_term)
+    d_q0.fold()
     make(lambda m: cols_of(xa, m), lambda: dproj[:, pw:], g_q1, d_q1, own_rows)
     sum_a.near(xa_term)
-    d_q0.fold()
-    g_wo[...] = sum_o.total(out_term(s)).astype(bf16).reshape(n, own_rows, quarter)
-    d_wo.send_x(0, n)
     lb[...] = jnp.sum(dproj[...].astype(f32), axis=0, keepdims=True)
     lb_all.start()
+    f_wd[s] = d_wd.total().astype(bf16)
+    f_wu[s] = d_wu.total().astype(bf16)
     e_all.wait_recv()
-    dm_e = jnp.concatenate([ebuf[i] for i in range(n)], axis=0).astype(bf16)
+    dm_e = jnp.concatenate([dmb[i, :, 2 * width :] for i in range(n)], axis=0).astype(bf16)
+    dmat[:, 2 * width :] = dm_e
     dt = nt(dm_e, wm[:, 2 * width :])
     d_q1.fold()
-    d_wo.fold()
-    g = sum_a.total(xa_term(s))
+    g = sum_a.total(xa_term)
     n_val = n_in[...]
     lm[s, :, :width] = jnp.sum(g, axis=0, keepdims=True)
     lm[s, :, width:] = jnp.sum(g * n_val, axis=0, keepdims=True)
     l_mod.start()
-    f_wd[s] = d_wd.total().astype(bf16)
     o_wd.start()
-    f_wu[s] = d_wu.total().astype(bf16)
     o_wu.start()
     grad_input[...] = grad_input[...] + norm_back(g * (1.0 + scale_a), n_val, normed(frames[...])[1])
+    leave(grad_input, grad_hbm, 1).start()
     l_mod.wait_recv()
-    lbuf[d] = (lm[0] + lm[1] + lm[2] + lm[3]).astype(bf16).astype(f32)
+    dmb[d, :, : 2 * width] = (lm[0] + lm[1] + lm[2] + lm[3]).astype(bf16).astype(f32)
     l_all.start()
+    fo[0] = d_wo.total().astype(bf16)
+    y_wo.start()
+    f_q0[s] = d_q0.total().astype(bf16)
+    o_q0.start()
     eb_all.wait_recv()
     lb_all.wait_recv()
     esum, lsum = eb[...], lb[...]
@@ -836,22 +1010,21 @@
     f_b[s, :, :qw] = lsum
     f_b[s, :, qw:] = esum
     o_b.start()
-    f_q0[s] = d_q0.total().astype(bf16)
-    o_q0.start()
     l_all.wait_recv()
-    dm_l = jnp.concatenate([lbuf[i] for i in range(n)], axis=0).astype(bf16)
+    dm_l = jnp.concatenate([dmb[i, :, : 2 * width] for i in range(n)], axis=0).astype(bf16)
+    dmat[:, : 2 * width] = dm_l
     dt = dt + nt(dm_l, wm[:, : 2 * width])
     for i in range(n):
         dts[i] = dt[i : i + 1]
     t_all.start()
-    f_wo[s] = d_wo.total().astype(bf16)
-    o_wo.start()
+    f_q1[s] = d_q1.total().astype(bf16)
+    o_q1.start()
     o_wd.hand_on()
     o_wu.hand_on()
-    f_q1[s] = d_q1.total().astype(bf16)
-    o_q1.start()
+    y_wo.wait_recv()
+    f_wo[core] = (fo[0].astype(f32) + fo[1].astype(f32)).astype(bf16)
+    o_wo.start()
     o_q0.hand_on()
-    o_wo.hand_on()
     t_all.wait_recv()
     dtb[d] = dts[d]
     sig = 1.0 / (1.0 + jnp.exp(-tv))
@@ -859,20 +1032,86 @@
     for i in range(n):
         at = slice(i * own_rows, (i + 1) * own_rows)
         grad_time[:, at] = dtb[i] * slope[:, at]
-    o_q1.hand_on()
-    for o in (o_q0, o_q1, o_wo, o_wu, o_wd):
+    for o in (o_wu, o_wd, o_q0):
         o.wait(l.s1)
         o.wait(l.s3)
+    for t in range(4):
+        n_mid[t * units : (t + 1) * units, :] = f_wd[t].astype(f32)
+    ends = [leave(n_mid.at[: 4 * units], gwd_hbm, 2)]
+    ends[0].start()
+    if not plain:
+        for i in range(n):
+            for h in range(2):
+                c0 = i // 2 * 128
+                pair = half_of_each(
+                    f_wu[2 * h, :, c0 : c0 + 128].astype(f32), f_wu[2 * h + 1, :, c0 : c0 + 128].astype(f32), i % 2 == 1
+                )
+                col = i * 4 * units + 128 * h
+                r0 = col // width * own_rows
+                n_in[r0 : r0 + own_rows, col % width : col % width + 128] = pair
+        for c in range(2):
+            ends.append(leave(n_in.at[c * own_rows : (c + 1) * own_rows], gwu_hbm.at[:, c * width : (c + 1) * width], 3 + c))
+            ends[-1].start()
+    o_wo.wait_recv()
+    for c in range(2):
+        attn_branch[:own_rows, c * 2 * quarter : (c + 1) * 2 * quarter] = f_wo[c].astype(f32)
+    ends.append(leave(attn_branch.at[:own_rows], gwo_hbm, 5))
+    ends[-1].start()
+    thirds = (cot.at[:own_rows], cot.at[own_rows : 2 * own_rows], attn_branch.at[own_rows : 2 * own_rows])
+
+    def place(p, held_p):
+        for t in range(4):
+            for j in range(3):
+                at = t * quarter + 128 * p
+                thirds[j][:, at : at + 128] = held_p[t, :, 128 * j : 128 * j + 128].astype(f32)
+
+    place(0, f_q0)
     o_b.wait_recv()
+    if plain:
+        bias_out[...] = f_b[...]
+    else:
+        outs = []
+        for i in range(each):
+            u = d * each + i
+            j, v = u // (width // 128), u % (width // 128)
+            outs.append(f_b[v // pairs, :, pl.ds(pl.multiple_of(v % pairs * pw + j * 128, 128), 128)])
+        for base in (qw + ff_q, qw + ff_q + width):
+            at = pl.ds(pl.multiple_of(base + d * own_rows, 128), own_rows)
+            outs.append(f_b[0, :, at] + f_b[1, :, at] + f_b[2, :, at] + f_b[3, :, at])
+        at = pl.ds(pl.multiple_of(qw + d // 2 * 128, 128), 128)
+        for h in range(2):
+            outs.append(half_of_each(f_b[2 * h, :, at], f_b[2 * h + 1, :, at], d % 2 == 1))
+        mod_each = 6 * width // n
+        at = pl.ds(pl.multiple_of(d * mod_each, 128), mod_each)
+        row = dmb[0, :, at]
+        for i in range(1, n):
+            row = row + dmb[i, :, at]
+        outs.append(row)
+        o_bq[...] = jnp.concatenate(outs[:each], axis=1)
+        o_bo[...] = outs[each]
+        o_bd[...] = outs[each + 1]
+        o_bu[...] = jnp.concatenate(outs[each + 2 : each + 4], axis=1)
+        o_bm[...] = outs[each + 4]
+    o_q1.hand_on()
+    o_q1.wait(l.s1)
+    o_q1.wait(l.s3)
+    place(1, f_q1)
+    for j in range(3):
+        ends.append(leave(thirds[j], gwq_hbm.at[:, j * width : (j + 1) * width], 6 + j))
+        ends[-1].start()
+    leave(block_out, out_hbm, 0).wait()
+    leave(grad_input, grad_hbm, 1).wait()
+    for c in ends:
+        c.wait()
     for c in (
-        times, parts, biases, mods, a_wq, a_wu, a_wd, a_wo, s_xa, s_xf, s_wo, w_ao, w_do,
-        sum_f, sum_o, sum_a, d_q0, d_q1, d_wo, d_wu, d_wd, o_q0, o_q1, o_wo, o_wu, o_wd, e_mod, l_mod, o_b,
+        times, parts, parts2, biases, mods, s_a0, s_a1, a_q0, a_q1, a_wu, a_wd, a_wo, s_x0, s_x1, s_wo, w_do,
+        sum_f, sum_a, c_wo, y_wo, d_q0, d_q1, d_wo, d_wu, d_wd, o_q0, o_q1, o_wo, o_wu, o_wd, e_mod, l_mod, o_b,
         e_all, l_all, eb_all, lb_all, t_all,
     ):
         c.wait_send()
 
 
-def run_whole(n, clip_len, frames, cot, time_embed, bm, bias, wu_own, w_mod, w_qkv, w_out, w_down):
+def run_whole(n, plain, clip_len, time_embed, bias, raw, wu_own, frames, cot, w_mod, w_qkv, w_out, w_down):
     rows, width = frames.shape
     item, quarter, own_rows = 4 * rows, width // 4, width // n
     ff_q = w_down.shape[0] * n // 4
@@ -881,51 +1120,60 @@
     pw = qw // pairs
     S, V = jax.ShapeDtypeStruct, pltpu.VMEM
     bw = qw + ff_q + 2 * width
+    mod_own = 6 * width if plain else 6 * width // n
+    bias_wide = bw if plain else 7 * width // n
+    wide = V((rows, width), f32)
     outs = [
-        S((rows, width), f32), S((rows, width), f32), S((1, width), f32), S((n, 1, own_rows), f32),
-        S((n, 1, 4 * width), f32), S((n, 1, 2 * width), f32), S((4, own_rows, pw), bf16), S((4, own_rows, pw), bf16),
-        S((4, own_rows, quarter), bf16), S((4, own_rows, ff_q), bf16), S((4, units, width), bf16), S((4, 1, bw), f32),
+        S((1, width), f32), S((n, own_rows), bf16), S((n, 6 * width), bf16), S((4, own_rows, ff_q), bf16),
+        S((4, 1, bw) if plain else (1, 1, 128), f32), S((1, 3 * own_rows), f32), S((1, own_rows), f32), S((1, own_rows), f32),
+        S((1, 4 * units), f32), S((1, 6 * own_rows), f32), S((rows, width), f32), S((rows, width), f32),
+        S((own_rows, 3 * width), f32), S((own_rows, width), f32), S((own_rows, 4 * ff_q), f32), S((4 * units, width), f32),
     ]
 
     def chain(a, b):
-        return [V((n, a, b), bf16), V((n // 2, a, b), bf16), V((n // 2, a, b), bf16)]
+        return [V((n, a, b), bf16), V((n // 2, a, b), bf16), V((n // 2 - 1, a, b), bf16)]
 
     held = V((6, rows, width), bf16)
     scratch = (
-        [
-            V((own_rows, 6 * width), bf16), V((n, own_rows, qw), bf16), V((n, own_rows, ff_q), bf16), V((n, units, width), bf16),
-            V((4, n, own_rows, quarter), bf16), V((n, 1, own_rows), f32), V((n, 1, 6 * quarter), f32),
-            V((n, 1, 6 * quarter), f32), V((n, 1, bw), f32), V((4, 1, 6 * quarter), f32),
-            V((rows, width), f32), V((rows, width), f32), V((rows, width), f32), V((item, 128), f32), V((item, 128), f32),
-            V((item, 1), jnp.int32), V((1, item), jnp.int32),
+        [V((n, 1, own_rows), f32), V((n, 1, 6 * width), f32)]
+        + [wide] * 4
+        + [
+            V((1, 6 * width), f32), V((8, 128) if plain else (n, own_rows, 128), bf16), V((4, 1, bw), f32),
+            V((own_rows, 6 * width), bf16), V((n, own_rows, pw), bf16), V((n, own_rows, pw), bf16),
+            V((n, own_rows, ff_q), bf16), V((n, units, width), bf16), V((4, n, own_rows, quarter), bf16),
+            V((n, 1, own_rows), f32), V((n, 1, 2 * width), f32), V((n, 1, 2 * width), f32), V((n, 1, width), f32),
+            V((n, 1, width), f32), V((n, 1, bias_wide), f32), V((4, 1, width), f32), wide, wide, wide,
+            V((item, 128), f32), V((item, 128), f32), V((item, 1), jnp.int32), V((1, item), jnp.int32),
             V((4, rows, width), bf16), V((4, rows, width), bf16), V((4, rows, width), bf16),
             V((item, quarter), bf16), V((item, quarter), bf16), V((item, quarter), bf16),
             V((pairs, 128, item), bf16), V((pairs, 128, item), bf16), V((heads, 1, item), f32),
         ]
-        + [V((4, rows, quarter), bf16)] * 4
+        + [V((4, rows, quarter), bf16)] * 3
         + [
             V((item, ff_q), bf16), V((item, ff_q), bf16), V((rows, width), bf16), V((8, width), f32),
             V((pairs, item, 128), f32), V((pairs, item, 128), f32), V((item, qw), bf16),
-            held, held, V((6, width, quarter), bf16),
+            V((4, own_rows, pw), bf16), V((4, own_rows, pw), bf16), V((2, own_rows, 2 * quarter), bf16),
+            V((4, units, width), bf16), held, held, V((2, width, 2 * quarter), bf16), V((2, own_rows, 2 * quarter), bf16),
         ]
-        + chain(own_rows, pw) + chain(own_rows, pw) + chain(own_rows, quarter) + chain(own_rows, ff_q) + chain(units, width)
+        + chain(own_rows, pw) + chain(own_rows, pw) + chain(own_rows, 2 * quarter) + chain(own_rows, ff_q) + chain(units, width)
         + [
             V((4, 1, 4 * width), f32), V((4, 1, 2 * width), f32), V((1, ff_q + 2 * width), f32),
             V((n, 1, ff_q + 2 * width), f32), V((1, qw), f32), V((n, 1, qw), f32),
             V((n, 1, own_rows), f32), V((n, 1, own_rows), f32),
-            pltpu.SemaphoreType.DMA((20 * n + 80,)), pltpu.SemaphoreType.DMA((20 * n + 90,)), pltpu.SemaphoreType.DMA((9,)),
+            pltpu.SemaphoreType.DMA((22 * n + 90,)), pltpu.SemaphoreType.DMA((22 * n + 100,)),
+            pltpu.SemaphoreType.DMA((11 + n,)), pltpu.SemaphoreType.DMA((9,)),
         ]
     )
     vm = pl.BlockSpec(memory_space=pltpu.VMEM)
     hb = pl.BlockSpec(memory_space=pl.ANY)
     return pl.pallas_call(
-        functools.partial(whole_kernel, n),
+        functools.partial(whole_kernel, n, plain),
         out_shape=outs,
-        in_specs=[pl.BlockSpec(memory_space=pltpu.SMEM)] + [vm] * 6 + [hb] * 4,
-        out_specs=[vm] * len(outs),
+        in_specs=[pl.BlockSpec(memory_space=pltpu.SMEM)] + [vm] * 7 + [hb] * 7,
+        out_specs=[vm] * 10 + [hb] * 6,
         scratch_shapes=scratch,
         compiler_params=pltpu.CompilerParams(collective_id=0, has_side_effects=True, vmem_limit_bytes=63 << 20),
-    )(clip_len, frames, cot, time_embed, bm, bias, wu_own, w_mod, w_qkv, w_out, w_down)
+    )(clip_len, time_embed, bias, *raw, wu_own, frames, cot, w_mod, w_qkv, w_out, w_down)
 
 
 def per_device(
@@ -941,48 +1189,50 @@
     ff_q = ff // 4
     qw = 3 * quarter
 
-    def placed(b):
-        return lax.dynamic_update_slice(
-            jnp.zeros((b.shape[0] * n,), f32), b.astype(f32), (dp_rank * b.shape[0],)
-        )
-
-    def mine(value, axis):
-        return lax.dynamic_index_in_dim(value, seq_rank, axis, keepdims=False)
-
-    bm = mine(placed(b_mod).reshape(4, 6 * quarter), 0)[None]
-    bias = jnp.concatenate(
-        [
+    plain = own_rows % 128 != 0 or units != 64
+    raw = [b.reshape(1, -1) for b in (b_qkv, b_out, b_up, b_down, b_mod)]
+    bias = jnp.zeros((1, 1, 128), f32)
+    if plain:
+
+        def placed(b):
+            return lax.dynamic_update_slice(
+                jnp.zeros((b.shape[0] * n,), f32), b.astype(f32), (dp_rank * b.shape[0],)
+            )
+
+        def mine(value, axis):
+            return lax.dynamic_index_in_dim(value, seq_rank, axis, keepdims=False)
+
+        laid = [
             mine(placed(b_qkv).reshape(3, 4, pairs, 128), 1).transpose(1, 0, 2).reshape(-1),
             placed(b_out),
             mine(placed(b_up).reshape(n, 4, units), 1).reshape(-1),
             placed(b_down),
+            placed(b_mod),
         ]
-    ).reshape(1, 1, -1)
-    wu_own = mine(w_up.reshape(own_rows, n, 4, units), 2).reshape(own_rows, ff_q)
-    block_out, grad_input, grad_time, tbuf, ebuf, lbuf, f_q0, f_q1, f_wo, f_wu, f_wd, f_b = run_whole(
-        n, clip_len, frames, cotangent, time_embed, bm, bias, wu_own, w_mod, w_qkv, w_out, w_down
+        bias = jnp.concatenate(laid).reshape(1, 1, -1)
+        wu_own = mine(w_up.reshape(own_rows, n, 4, units), 2).reshape(own_rows, ff_q)
+    else:
+        wu_own = w_up
+    grad_time, tmat, d_mod, f_wu, f_b, *small, block_out, grad_input, s_wq, s_wo, s_wu, s_wd = run_whole(
+        n, plain, clip_len, time_embed, bias, raw, wu_own, frames, cotangent, w_mod, w_qkv, w_out, w_down
     )
-    f_wq = jnp.stack([f_q0, f_q1], axis=2).astype(f32).reshape(4, own_rows, pairs, 3, 128)
-    s_wq = f_wq.transpose(1, 3, 0, 2, 4).reshape(own_rows, 3 * width)
-    s_wo = f_wo.astype(f32).transpose(1, 0, 2).reshape(own_rows, width)
-    s_wu = f_wu.astype(f32).reshape(4, own_rows, n, units).transpose(1, 2, 0, 3).reshape(own_rows, ff)
-    s_wd = f_wd.astype(f32).reshape(4 * units, width)
-    d_mod = jnp.concatenate([lbuf[:, 0], ebuf[:, 0]], axis=1)
-    gwm = tn(tbuf[:, 0].astype(bf16), d_mod.astype(bf16))
-    gbm = jnp.sum(d_mod, axis=0)
-    bq = f_b[:, 0, :qw].reshape(4, pairs, 3, 128).transpose(2, 0, 1, 3).reshape(-1)
-    bu = f_b[:, 0, qw : qw + ff_q].reshape(4, n, units).transpose(1, 0, 2).reshape(-1)
-    bo = jnp.sum(f_b[:, 0, qw + ff_q : qw + ff_q + width], axis=0)
-    bd = jnp.sum(f_b[:, 0, qw + ff_q + width :], axis=0)
-
-    def own(value, like):
-        size = like.shape[0]
-        return lax.dynamic_slice_in_dim(value, dp_rank * size, size, 0)
-
-    return (
-        block_out, grad_input, grad_time, s_wq, own(bq, b_qkv), s_wo, own(bo, b_out), s_wu,
-        own(bu, b_up), s_wd, own(bd, b_down), gwm, own(gbm, b_mod),
-    )
+    gwm = tn(tmat, d_mod)
+    if plain:
+        s_wu = f_wu.astype(f32).reshape(4, own_rows, n, units).transpose(1, 2, 0, 3).reshape(own_rows, ff)
+
+        def own(value, like):
+            size = like.shape[0]
+            return lax.dynamic_slice_in_dim(value, dp_rank * size, size, 0)
+
+        bq = f_b[:, 0, :qw].reshape(4, pairs, 3, 128).transpose(2, 0, 1, 3).reshape(-1)
+        bu = f_b[:, 0, qw : qw + ff_q].reshape(4, n, units).transpose(1, 0, 2).reshape(-1)
+        bo = jnp.sum(f_b[:, 0, qw + ff_q : qw + ff_q + width], axis=0)
+        bd = jnp.sum(f_b[:, 0, qw + ff_q + width :], axis=0)
+        bq, bo, bu = own(bq, b_qkv), own(bo, b_out), own(bu, b_up)
+        bd, bm = own(bd, b_down), own(jnp.sum(d_mod.astype(f32), axis=0), b_mod)
+    else:
+        bq, bo, bd, bu, bm = (b.reshape(-1) for b in small)
+    return (block_out, grad_input, grad_time, s_wq, bq, s_wo, bo, s_wu, bu, s_wd, bd, gwm, bm)
 
 
 def solution(mesh):

time: 221 us -> 195 us (0.88)
  Pallas kernels: 191 us -> 175 us
  local copies, waits for them, and re-layouts: 19.3 us -> 12.7 us
  other arithmetic: 6.62 us -> 1.89 us
    pallas_call x1, Pallas kernels: 191 us -> 175 us  [run_whole(): pl.pallas_call(functools.partial(whole_kernel, n, plain), out_shape=outs,...]
    dynamic_update_slice x5 -> x0, other arithmetic: 3.78 us -> none  [placed(): lax.dynamic_update_slice(jnp.zeros((b.shape[0] * n,), f32), b.astype(f32)...]
    dynamic_slice x8 -> x0, local copies, waits for them, and re-layouts: 3.77 us -> none  [the longest x5 3.13 us: own(): return lax.dynamic_slice_in_dim(value, dp_rank * size, size, 0)]
    unnamed x23 -> x32, local copies, waits for them, and re-layouts: 10.3 us -> 8.47 us
where the time goes in v5:
time: 195 us; the launch traced here: 194 us
  Pallas kernels  175 us (90%)
  local copies, waits for them, and re-layouts  12.7 us (7%)
  matrix products  3.25 us (2%)
    pallas_call x1, Pallas kernels, run_whole(): pl.pallas_call(functools.partial(whole_kernel, n, plain), out_shape=outs,...  175 us
    unnamed x32, local copies, waits for them, and re-layouts  8.47 us

profile of v5, /device:TPU:0, one launch (start us, length us, event | category | flops | bytes accessed | tf_op | source)
XLA Modules:
  0.0 193.8 jit_solution(4957833994820214757)
XLA Ops:
  0.6 1.2 reshape.56.b1
  1.9 1.2 reshape.58.b3
  3.1 1.3 reshape.60.b5
  4.4 0.5 broadcast_in_dim.3.bias
  4.9 175.3 %shard_map.237 = (f32[1,1024]{1,0:T(1,128)}, bf16[8,128]{1,0:T(8,128)(2,1)}, bf16[8,6144]{1,0:T(8,128)(2,1)}, bf16[4,128,512]{2,1,0:T(8,128)(2,1)}, f32[1,1,128]...) custom-call(s32[1,6]{1,0:T(1,128)} %lengths.1, ...), custom_call_target="tpu_custom_call" | custom-call | tf_op jit(solution)/shard_map/pallas_call | solution.py:1169
  180.2 1.3 reduce
  181.4 0.0 copy-start.7
  181.4 0.0 copy-start.4
  181.4 3.3 %fusion = f32[128,6144]{1,0:T(8,128)} fusion(bf16[8,128]{1,0:T(8,128)(2,1)} %get-tuple-element.38, bf16[8,6144]{1,0:T(8,128)(2,1)} %get-tuple-element.39), kind=kOutput, calls=%fused_computation | convolution fusion | flops 12582912 | bytes 3246080 | tf_op jit(solution)/shard_map/dot_general | solution.py:309
  184.7 0.0 copy-start.3
  184.7 0.0 copy-done.7
  184.7 0.6 reduce.1
  185.3 0.0 copy-done.4
  185.3 0.0 copy-start.6
  185.3 1.0 copy.37
  186.3 0.0 copy-done.3
  186.3 0.0 copy-start
  186.3 1.0 copy.38
  187.3 0.0 copy-done.6
  187.3 0.6 copy.39
  187.9 0.2 copy-done
  188.1 0.0 copy-start.5
  188.1 0.0 copy-start.10
  188.1 0.0 copy-start.2
  188.1 1.1 copy.40
  189.2 0.2 copy-done.5
  189.5 0.0 copy-start.8
  189.5 0.0 copy-start.1
  189.5 0.8 copy.41
  190.2 0.0 copy-done.10
  190.3 0.5 copy.42
  190.8 0.0 copy-done.2
  190.8 1.0 copy.43
  191.7 0.0 copy-done.8
  191.7 0.0 copy-start.9
  191.7 0.6 copy.44
  192.3 0.0 copy-done.1
  192.3 1.0 copy.45
  193.3 0.0 copy-done.9
  193.3 0.5 copy.46
Async XLA Ops:
  181.4 3.3 %copy-start.7 = (f32[1,768]{1,0:T(1,128)S(1)}, f32[1,768]{1,0:T(1,128)}, u32[]{:S(2)}) copy-start(f32[1,768]{1,0:T(1,128)} %get-tuple-element.40) | copy-start | bytes 9220
  181.4 3.9 %copy-start.4 = (f32[256,1024]{1,0:T(8,128)S(1)}, f32[256,1024]{1,0:T(8,128)}, u32[]{:S(2)}) copy-start(f32[256,1024]{1,0:T(8,128)} %get-tuple-element.54) | copy-start | bytes 3145732
  184.7 1.6 copy-start.3
  185.3 1.9 %copy-start.6 = (f32[1,1024]{1,0:T(1,128)S(1)}, f32[1,1024]{1,0:T(1,128)}, u32[]{:S(2)}) copy-start(f32[1,1024]{1,0:T(1,128)} %get-tuple-element.56) | copy-start | bytes 12292
  186.3 1.8 copy-start
  188.1 1.4 copy-start.5
  188.1 2.2 %copy-start.10 = (f32[1,128]{1,0:T(1,128)S(1)}, f32[1,128]{1,0:T(1,128)}, u32[]{:S(2)}) copy-start(f32[1,128]{1,0:T(1,128)} %get-tuple-element.33) | copy-start | bytes 1540
  188.1 2.7 %copy-start.2 = (f32[128,2048]{1,0:T(8,128)S(1)}, f32[128,2048]{1,0:T(8,128)}, u32[]{:S(2)}) copy-start(f32[128,2048]{1,0:T(8,128)} %get-tuple-element.61) | copy-start | bytes 3145732
  189.5 2.3 %copy-start.8 = (f32[1,256]{1,0:T(1,128)S(1)}, f32[1,256]{1,0:T(1,128)}, u32[]{:S(2)}) copy-start(f32[1,256]{1,0:T(1,128)} %get-tuple-element.35) | copy-start | bytes 3076
  189.5 2.9 %copy-start.1 = (f32[256,1024]{1,0:T(8,128)S(1)}, f32[256,1024]{1,0:T(8,128)}, u32[]{:S(2)}) copy-start(f32[256,1024]{1,0:T(8,128)} %get-tuple-element.63) | copy-start | bytes 3145732
  191.7 1.5 copy-start.9

commit v6 on v5

--- a/solution.py
+++ b/solution.py
@@ -82,13 +82,15 @@
             device_id=dev, device_id_type=MESH,
         )
 
-    def barrier(self):
+    def greet(self):
         b = pltpu.get_barrier_semaphore()
         for k in range(1, self.n):
             pl.semaphore_signal(b, inc=1, device_id=((self.d + k) % self.n, self.s), device_id_type=MESH)
         for t in (self.s1, self.s2, self.s3):
             pl.semaphore_signal(b, inc=1, device_id=(self.d, t), device_id_type=MESH)
-        pl.semaphore_wait(b, self.n + 2)
+
+    def meet(self):
+        pl.semaphore_wait(pltpu.get_barrier_semaphore(), self.n + 2)
 
 
 class ToAll:
@@ -256,18 +258,14 @@
         sem = 4 if k == 2 else 2 * k + h
         return l.copy(self.held.at[k, at], self.held.at[3 + k, at], self.si + sem, self.ri + sem, (l.d, t))
 
-    def _part(self, b, h):
-        half = self.rows // 2
-        return pl.ds(pl.multiple_of(b * self.rows + h * half, half), half)
-
     def far(self, term, cross=True):
         l, held, half = self.l, self.held, self.rows // 2
         for h in range(2):
-            held[0, h * half : (h + 1) * half] = term(self._part(l.s3, h)).astype(bf16)
+            held[0, h * half : (h + 1) * half] = term(l.s3, h).astype(bf16)
             self._c(0, h, l.s1).start()
         for h in range(2):
             at = slice(h * half, (h + 1) * half)
-            mine = term(self._part(l.s2, h))
+            mine = term(l.s2, h)
             self._c(0, h, l.s1).wait_recv()
             held[1, at] = (mine + held[3, at].astype(f32)).astype(bf16)
             if cross:
@@ -279,12 +277,12 @@
 
     def near(self, term):
         l = self.l
-        self.held[2] = term(pl.ds(pl.multiple_of(l.s1 * self.rows, self.rows), self.rows)).astype(bf16)
+        self.held[2] = term(l.s1, None).astype(bf16)
         self._c(2, 0, l.s1).start()
 
     def total(self, term):
         l, held = self.l, self.held
-        mine = term(pl.ds(pl.multiple_of(l.s * self.rows, self.rows), self.rows))
+        mine = term(l.s, None)
         self._c(2, 0, l.s1).wait_recv()
         for h in range(2):
             self._c(1, h, l.s2).wait_recv()
@@ -365,24 +363,6 @@
             return carry
 
         lax.fori_loop(0, l.n, one, 0)
-
-
-class One:
-    def __init__(self, links, src, dst, to):
-        self.l, self.src, self.dst, self.to = links, src, dst, to
-        self.si, self.ri = links.sems(1, 1)
-
-    def _c(self):
-        return self.l.copy(self.src, self.dst, self.si, self.ri, (self.l.d, self.to))
-
-    def start(self):
-        self._c().start()
-
-    def wait_recv(self):
-        self._c().wait_recv()
-
-    def wait_send(self):
-        self._c().wait_send()
 
 
 class DpSum:
@@ -443,11 +423,12 @@
     grad_time, tmat, dmat, f_wu, bias_out, o_bq, o_bo, o_bd, o_bu, o_bm, out_hbm, grad_hbm, gwq_hbm, gwo_hbm, gwu_hbm, gwd_hbm,
     tbuf, dmb, frames, cot, block_out, grad_input, bmv, wu_raw, f_b, wm, wq0, wq1, wu, wd, wo, tsrc, psend, pbuf, psend2, pbuf2, bbuf, mod, n_in, attn_branch, n_mid, cos, sin, idc, idr,
     xa, dffn, xf, q, k, v, kt, vt, lse, ao_out, ao, gh, gelu, dhid, dattn, fsum, dk, dv, dproj,
-    f_q0, f_q1, f_wo, f_wd, held, held_f, ho, fo, g_q0, x_q0, z_q0, g_q1, x_q1, z_q1, g_wo, x_wo, z_wo, g_wu, x_wu, z_wu, g_wd, x_wd, z_wd,
+    f_q0, f_q1, f_wo, f_wd, held, held_f, held_o, g_q0, x_q0, z_q0, g_q1, x_q1, z_q1, g_wo, x_wo, z_wo, g_wu, x_wu, z_wu, g_wd, x_wd, z_wd,
     em, lm, eb, ebb, lb, lbb, dts, dtb,
     send, recv, local, gone,
 ):
     l = Links(n, send, recv)
+    l.greet()
     d, s = l.d, l.s
     rows, width = frames.shape
     item = 4 * rows
@@ -501,9 +482,7 @@
     o_q0, o_q1, o_wu, o_wd = (
         SeqGather(l, f_q0), SeqGather(l, f_q1), SeqGather(l, f_wu), SeqGather(l, f_wd)
     )
-    core = s % 2
-    c_wo, y_wo = One(l, ho.at[0], ho.at[1], l.s1), One(l, fo.at[0], fo.at[1], l.s2)
-    o_wo = One(l, f_wo.at[core], f_wo.at[core], l.s1)
+    sum_o, o_wo = SeqSum(l, held_o), SeqGather(l, f_wo)
     e_mod, l_mod, o_b = SeqAll(l, em), SeqAll(l, lm), SeqAll(l, f_b)
     e_all, l_all = ToAll(l, None, dmb, slice(2 * width, 6 * width)), ToAll(l, None, dmb, slice(0, 2 * width))
     eb_all, lb_all = ToAll(l, lambda peer: eb, ebb), ToAll(l, lambda peer: lb, lbb)
@@ -516,8 +495,8 @@
         bbuf[d] = bias[0, :, :wide_b]
         own_mod = bias[0, :, wide_b:]
     else:
-        bbuf[d] = jnp.concatenate([b[...].astype(f32) for b in (b1, b2, b3, b4)], axis=1)
-        own_mod = b5[...].astype(f32)
+        bbuf[d] = jnp.concatenate([b[...].astype(f32).reshape(1, -1) for b in (b1, b2, b3, b4)], axis=1)
+        own_mod = b5[...].astype(f32).reshape(1, -1)
     if plain:
         bmv[...] = own_mod
     else:
@@ -532,7 +511,7 @@
     dffn[s] = cot[...].astype(bf16)
     for c in take[3:]:
         c.wait()
-    l.barrier()
+    l.meet()
     times.start()
     a_q0.start()
     s_d0.start()
@@ -645,8 +624,8 @@
             q[at, c0 : c0 + 128] = qp * jnp.bfloat16(0.125)
             k[at, c0 : c0 + 128] = kp
             v[at, c0 : c0 + 128] = vp
-            kt[p, :, at] = jnp.transpose(kp.astype(f32)).astype(bf16)
-            vt[p, :, at] = jnp.transpose(vp.astype(f32)).astype(bf16)
+            kt[p, :, at] = jnp.transpose(kp)
+            vt[p, :, at] = jnp.transpose(vp)
             return carry
 
         lax.fori_loop(0, 4, one, 0)
@@ -759,17 +738,24 @@
     a_wu.wait_rest()
     a_wd.wait_rest()
 
-    def hidden_term(at):
-        return nt(dhid[at, :], merged(wu))
-
-    def ffn_term(at):
-        return nn(gelu[at, :], merged(wd))
-
-    def out_half(c):
-        part = dattn[:, pl.ds(pl.multiple_of(c * 2 * quarter, 128), 2 * quarter)]
-        return jnp.concatenate([tn(ao[i], part) for i in range(4)], axis=0)
-
-    def xa_term(at):
+    def run_of(b, h):
+        if h is None:
+            return at_rows(b)
+        return pl.ds(pl.multiple_of(b * rows + h * half, half), half)
+
+    def hidden_term(b, h):
+        return nt(dhid[run_of(b, h), :], merged(wu))
+
+    def ffn_term(b, h):
+        return nn(gelu[run_of(b, h), :], merged(wd))
+
+    def out_term(t, h):
+        part = dattn[:, pl.ds(pl.multiple_of(t * quarter, 128), quarter)]
+        blocks = range(4) if h is None else (2 * h, 2 * h + 1)
+        return jnp.concatenate([tn(ao[i], part) for i in blocks], axis=0)
+
+    def xa_term(b, h):
+        at = run_of(b, h)
         return nt(dproj[at, :pw], merged(wq0)) + nt(dproj[at, pw:], merged(wq1))
 
     half = rows // 2
@@ -933,39 +919,25 @@
     def after0(i):
         @pl.when(i == 0)
         def _():
-            ho[0] = out_half(1 - core).astype(bf16)
-            c_wo.start()
+            sum_o.far(out_term)
 
         @pl.when(i == 1)
         def _():
-            mine = out_half(core)
-            c_wo.wait_recv()
-            g_wo[...] = (mine + ho[1].astype(f32)).astype(bf16).reshape(n, own_rows, 2 * quarter)
+            sum_o.near(out_term)
+
+        @pl.when(i == 2)
+        def _():
+            d_wu.fold()
+
+        @pl.when(i == 3)
+        def _():
+            sum_f.cross()
+
+    def after1(i):
+        @pl.when(i == 1)
+        def _():
+            g_wo[...] = sum_o.total(out_term).astype(bf16).reshape(n, own_rows, quarter)
             d_wo.send_x(0, n)
-
-        @pl.when(i == 2)
-        def _():
-            sum_f.cross()
-            d_wu.fold()
-
-    def after1(i):
-        @pl.when(i == 2)
-        def _():
-            ffn = sum_f.total(ffn_term) + bd
-            block_out[...] = block_out[...] + gate_f * ffn
-            leave(block_out, out_hbm, 0).start()
-            d_wo.fold()
-            em[s, :, 3 * width :] = jnp.sum(cot[...] * ffn, axis=0, keepdims=True)
-            em[s, :, :width] = fsum[2:3, :]
-            em[s, :, width : 2 * width] = fsum[0:1, :]
-            em[s, :, 2 * width : 3 * width] = fsum[1:2, :]
-            e_mod.start()
-
-        @pl.when(i == 3)
-        def _():
-            e_mod.wait_recv()
-            dmb[d, :, 2 * width :] = (em[0] + em[1] + em[2] + em[3]).astype(bf16).astype(f32)
-            e_all.start()
 
     d_wd.fold()
     back_pair(0, before0, after0)
@@ -976,6 +948,18 @@
     d_q0.fold()
     make(lambda m: cols_of(xa, m), lambda: dproj[:, pw:], g_q1, d_q1, own_rows)
     sum_a.near(xa_term)
+    ffn = sum_f.total(ffn_term) + bd
+    em[s, :, 3 * width :] = jnp.sum(cot[...] * ffn, axis=0, keepdims=True)
+    em[s, :, :width] = fsum[2:3, :]
+    em[s, :, width : 2 * width] = fsum[0:1, :]
+    em[s, :, 2 * width : 3 * width] = fsum[1:2, :]
+    e_mod.start()
+    block_out[...] = block_out[...] + gate_f * ffn
+    leave(block_out, out_hbm, 0).start()
+    d_wo.fold()
+    e_mod.wait_recv()
+    dmb[d, :, 2 * width :] = (em[0] + em[1] + em[2] + em[3]).astype(bf16).astype(f32)
+    e_all.start()
     lb[...] = jnp.sum(dproj[...].astype(f32), axis=0, keepdims=True)
     lb_all.start()
     f_wd[s] = d_wd.total().astype(bf16)
@@ -997,8 +981,8 @@
     l_mod.wait_recv()
     dmb[d, :, : 2 * width] = (lm[0] + lm[1] + lm[2] + lm[3]).astype(bf16).astype(f32)
     l_all.start()
-    fo[0] = d_wo.total().astype(bf16)
-    y_wo.start()
+    f_wo[s] = d_wo.total().astype(bf16)
+    o_wo.start()
     f_q0[s] = d_q0.total().astype(bf16)
     o_q0.start()
     eb_all.wait_recv()
@@ -1021,10 +1005,8 @@
     o_q1.start()
     o_wd.hand_on()
     o_wu.hand_on()
-    y_wo.wait_recv()
-    f_wo[core] = (fo[0].astype(f32) + fo[1].astype(f32)).astype(bf16)
-    o_wo.start()
     o_q0.hand_on()
+    o_wo.hand_on()
     t_all.wait_recv()
     dtb[d] = dts[d]
     sig = 1.0 / (1.0 + jnp.exp(-tv))
@@ -1032,13 +1014,14 @@
     for i in range(n):
         at = slice(i * own_rows, (i + 1) * own_rows)
         grad_time[:, at] = dtb[i] * slope[:, at]
-    for o in (o_wu, o_wd, o_q0):
+    for o in (o_wu, o_wd, o_q0, o_wo):
         o.wait(l.s1)
         o.wait(l.s3)
     for t in range(4):
         n_mid[t * units : (t + 1) * units, :] = f_wd[t].astype(f32)
     ends = [leave(n_mid.at[: 4 * units], gwd_hbm, 2)]
     ends[0].start()
+    o_q1.hand_on()
     if not plain:
         for i in range(n):
             for h in range(2):
@@ -1052,9 +1035,8 @@
         for c in range(2):
             ends.append(leave(n_in.at[c * own_rows : (c + 1) * own_rows], gwu_hbm.at[:, c * width : (c + 1) * width], 3 + c))
             ends[-1].start()
-    o_wo.wait_recv()
-    for c in range(2):
-        attn_branch[:own_rows, c * 2 * quarter : (c + 1) * 2 * quarter] = f_wo[c].astype(f32)
+    for t in range(4):
+        attn_branch[:own_rows, t * quarter : (t + 1) * quarter] = f_wo[t].astype(f32)
     ends.append(leave(attn_branch.at[:own_rows], gwo_hbm, 5))
     ends[-1].start()
     thirds = (cot.at[:own_rows], cot.at[own_rows : 2 * own_rows], attn_branch.at[own_rows : 2 * own_rows])
@@ -1087,12 +1069,11 @@
         for i in range(1, n):
             row = row + dmb[i, :, at]
         outs.append(row)
-        o_bq[...] = jnp.concatenate(outs[:each], axis=1)
-        o_bo[...] = outs[each]
-        o_bd[...] = outs[each + 1]
-        o_bu[...] = jnp.concatenate(outs[each + 2 : each + 4], axis=1)
-        o_bm[...] = outs[each + 4]
-    o_q1.hand_on()
+        o_bq[...] = jnp.concatenate(outs[:each], axis=1).reshape(-1)
+        o_bo[...] = outs[each].reshape(-1)
+        o_bd[...] = outs[each + 1].reshape(-1)
+        o_bu[...] = jnp.concatenate(outs[each + 2 : each + 4], axis=1).reshape(-1)
+        o_bm[...] = outs[each + 4].reshape(-1)
     o_q1.wait(l.s1)
     o_q1.wait(l.s3)
     place(1, f_q1)
@@ -1105,7 +1086,7 @@
         c.wait()
     for c in (
         times, parts, parts2, biases, mods, s_a0, s_a1, a_q0, a_q1, a_wu, a_wd, a_wo, s_x0, s_x1, s_wo, w_do,
-        sum_f, sum_a, c_wo, y_wo, d_q0, d_q1, d_wo, d_wu, d_wd, o_q0, o_q1, o_wo, o_wu, o_wd, e_mod, l_mod, o_b,
+        sum_f, sum_o, sum_a, d_q0, d_q1, d_wo, d_wu, d_wd, o_q0, o_q1, o_wo, o_wu, o_wd, e_mod, l_mod, o_b,
         e_all, l_all, eb_all, lb_all, t_all,
     ):
         c.wait_send()
@@ -1125,8 +1106,8 @@
     wide = V((rows, width), f32)
     outs = [
         S((1, width), f32), S((n, own_rows), bf16), S((n, 6 * width), bf16), S((4, own_rows, ff_q), bf16),
-        S((4, 1, bw) if plain else (1, 1, 128), f32), S((1, 3 * own_rows), f32), S((1, own_rows), f32), S((1, own_rows), f32),
-        S((1, 4 * units), f32), S((1, 6 * own_rows), f32), S((rows, width), f32), S((rows, width), f32),
+        S((4, 1, bw) if plain else (1, 1, 128), f32), S((3 * own_rows,), f32), S((own_rows,), f32), S((own_rows,), f32),
+        S((4 * units,), f32), S((6 * own_rows,), f32), S((rows, width), f32), S((rows, width), f32),
         S((own_rows, 3 * width), f32), S((own_rows, width), f32), S((own_rows, 4 * ff_q), f32), S((4 * units, width), f32),
     ]
 
@@ -1152,10 +1133,10 @@
         + [
             V((item, ff_q), bf16), V((item, ff_q), bf16), V((rows, width), bf16), V((8, width), f32),
             V((pairs, item, 128), f32), V((pairs, item, 128), f32), V((item, qw), bf16),
-            V((4, own_rows, pw), bf16), V((4, own_rows, pw), bf16), V((2, own_rows, 2 * quarter), bf16),
-            V((4, units, width), bf16), held, held, V((2, width, 2 * quarter), bf16), V((2, own_rows, 2 * quarter), bf16),
+            V((4, own_rows, pw), bf16), V((4, own_rows, pw), bf16), V((4, own_rows, quarter), bf16),
+            V((4, units, width), bf16), held, held, V((6, width, quarter), bf16),
         ]
-        + chain(own_rows, pw) + chain(own_rows, pw) + chain(own_rows, 2 * quarter) + chain(own_rows, ff_q) + chain(units, width)
+        + chain(own_rows, pw) + chain(own_rows, pw) + chain(own_rows, quarter) + chain(own_rows, ff_q) + chain(units, width)
         + [
             V((4, 1, 4 * width), f32), V((4, 1, 2 * width), f32), V((1, ff_q + 2 * width), f32),
             V((n, 1, ff_q + 2 * width), f32), V((1, qw), f32), V((n, 1, qw), f32),
@@ -1190,8 +1171,8 @@
     qw = 3 * quarter
 
     plain = own_rows % 128 != 0 or units != 64
-    raw = [b.reshape(1, -1) for b in (b_qkv, b_out, b_up, b_down, b_mod)]
-    bias = jnp.zeros((1, 1, 128), f32)
+    raw = [b_qkv, b_out, b_up, b_down, b_mod]
+    bias = time_embed[None]
     if plain:
 
         def placed(b):
@@ -1231,7 +1212,7 @@
         bq, bo, bu = own(bq, b_qkv), own(bo, b_out), own(bu, b_up)
         bd, bm = own(bd, b_down), own(jnp.sum(d_mod.astype(f32), axis=0), b_mod)
     else:
-        bq, bo, bd, bu, bm = (b.reshape(-1) for b in small)
+        bq, bo, bd, bu, bm = small
     return (block_out, grad_input, grad_time, s_wq, bq, s_wo, bo, s_wu, bu, s_wd, bd, gwm, bm)
 
 

time: 195 us -> 187 us (0.959)
  local copies, waits for them, and re-layouts: 12.7 us -> 10.1 us
  Pallas kernels: 175 us -> 173 us
    reshape x3 -> x0, local copies, waits for them, and re-layouts: 3.72 us -> none  [per_device(): raw = [b.reshape(1, -1) for b in (b_qkv, b_out, b_up, b_down, b_mod)]]
    pallas_call x1, Pallas kernels: 175 us -> 173 us  [run_whole(): pl.pallas_call(functools.partial(whole_kernel, n, plain), out_shape=outs,...]
    unnamed x32 -> x36, local copies, waits for them, and re-layouts: 8.47 us -> 10.1 us
where the time goes in v6:
time: 187 us
  Pallas kernels  173 us (93%)
  local copies, waits for them, and re-layouts  10.1 us (5%)
  matrix products  3.26 us (2%)
    pallas_call x1, Pallas kernels, run_whole(): pl.pallas_call(functools.partial(whole_kernel, n, plain), out_shape=outs,...  173 us
    unnamed x36, local copies, waits for them, and re-layouts  10.1 us

profile of v6, /device:TPU:0, one launch (start us, length us, event | category | flops | bytes accessed | tf_op | source)
XLA Modules:
  0.0 186.7 jit_solution(14345899888761525393)
XLA Ops:
  0.7 172.7 %shard_map.237 = (f32[1,1024]{1,0:T(1,128)}, bf16[8,128]{1,0:T(8,128)(2,1)}, bf16[8,6144]{1,0:T(8,128)(2,1)}, bf16[4,128,512]{2,1,0:T(8,128)(2,1)}, f32[1,1,128]...) custom-call(s32[1,6]{1,0:T(1,128)} %lengths.1, ...), custom_call_target="tpu_custom_call" | custom-call | tf_op jit(solution)/shard_map/pallas_call | solution.py:1150
  173.3 0.0 copy-start.4
  173.3 3.3 %fusion = f32[128,6144]{1,0:T(8,128)} fusion(bf16[8,128]{1,0:T(8,128)(2,1)} %get-tuple-element.38, bf16[8,6144]{1,0:T(8,128)(2,1)} %get-tuple-element.39), kind=kOutput, calls=%fused_computation | convolution fusion | flops 12582912 | bytes 3246080 | tf_op jit(solution)/shard_map/dot_general | solution.py:307
  176.6 0.0 copy-done.4
  176.6 0.0 copy-start.3
  176.6 0.0 copy-start.7
  176.6 1.0 copy.39
  177.6 0.6 copy-done.3
  178.2 0.0 copy-start
  178.2 1.0 copy.40
  179.2 0.0 copy-done.7
  179.2 0.6 copy.41
  179.8 0.2 copy-done
  180.0 0.0 copy-start.8
  180.0 0.0 copy-start.5
  180.0 0.0 copy-start.11
  180.0 0.0 copy-start.2
  180.0 1.1 copy.42
  181.1 0.0 copy-done.8
  181.1 0.6 copy.43
  181.7 0.0 copy-done.5
  181.7 0.0 copy-start.9
  181.7 0.0 copy-start.1
  181.7 0.8 copy.44
  182.5 0.0 copy-done.11
  182.5 0.5 copy.45
  183.0 0.0 copy-done.2
  183.0 1.0 copy.46
  184.0 0.0 copy-done.9
  184.0 0.0 copy-start.10
  184.0 0.0 copy-start.6
  184.0 0.6 copy.47
  184.6 0.0 copy-done.1
  184.6 1.0 copy.48
  185.6 0.0 copy-done.10
  185.6 0.5 copy.49
  186.1 0.0 copy-done.6
  186.1 0.6 copy.50
Async XLA Ops:
  173.3 3.3 %copy-start.4 = (f32[256,1024]{1,0:T(8,128)S(1)}, f32[256,1024]{1,0:T(8,128)}, u32[]{:S(2)}) copy-start(f32[256,1024]{1,0:T(8,128)} %get-tuple-element.54) | copy-start | bytes 3145732
  176.6 1.6 copy-start.3
  176.6 2.6 %copy-start.7 = (f32[1,1024]{1,0:T(1,128)S(1)}, f32[1,1024]{1,0:T(1,128)}, u32[]{:S(2)}) copy-start(f32[1,1024]{1,0:T(1,128)} %get-tuple-element.56) | copy-start | bytes 12292
  178.2 1.8 copy-start
  180.0 1.2 copy-start.8
  180.0 1.7 copy-start.5
  180.0 2.5 %copy-start.11 = (f32[128]{0:T(128)S(1)}, f32[128]{0:T(128)}, u32[]{:S(2)}) copy-start(f32[128]{0:T(128)} %get-tuple-element.60) | copy-start | bytes 1540
  180.0 3.0 %copy-start.2 = (f32[128,2048]{1,0:T(8,128)S(1)}, f32[128,2048]{1,0:T(8,128)}, u32[]{:S(2)}) copy-start(f32[128,2048]{1,0:T(8,128)} %get-tuple-element.61) | copy-start | bytes 3145732
  181.7 2.3 %copy-start.9 = (f32[256]{0:T(256)S(1)}, f32[256]{0:T(256)}, u32[]{:S(2)}) copy-start(f32[256]{0:T(256)} %get-tuple-element.62) | copy-start | bytes 3076
  181.7 2.9 %copy-start.1 = (f32[256,1024]{1,0:T(8,128)S(1)}, f32[256,1024]{1,0:T(8,128)}, u32[]{:S(2)}) copy-start(f32[256,1024]{1,0:T(8,128)} %get-tuple-element.63) | copy-start | bytes 3145732
  184.0 1.5 copy-start.10
  184.0 2.1 %copy-start.6 = (f32[768]{0:T(1024)S(1)}, f32[768]{0:T(1024)}, u32[]{:S(2)}) copy-start(f32[768]{0:T(1024)} %get-tuple-element.66) | copy-start | bytes 9220
